TPU v7x, 256 devices: a whole 4x4x8 slice. The times are simulated.
256 devices in a mesh: dp: 16 (over y, x_hi, core), ctx: 16 (over x_lo, z).
Axes of the slice: x: 4 (x_hi: 2, x_lo: 2; x = x_hi * 2 + x_lo), y: 4, z: 8, core: 2. Of those that a mesh axis runs over, the one named last changes fastest.
Arguments:
- queries: bfloat16 [16, 2048, 3584], P('dp', 'ctx'), may hold values from -8 to 8
- keys: bfloat16 [16, 2048, 512], P('dp', 'ctx'), may hold values from -8 to 8
- values: bfloat16 [16, 2048, 512], P('dp', 'ctx'), may hold values from -6 to 6
- out_grad: bfloat16 [16, 2048, 3584], P('dp', 'ctx'), may hold values from -6 to 6
- routes: int32 [16, 2048], P('dp', 'ctx'), may hold values from -1 to 16383, as said below
- per_head_scale: float32 [28], replicated, may hold values from 0.5 to 2
Outputs:
- query_grad: bfloat16 [16, 2048, 3584], P('dp', 'ctx')
- key_grad: bfloat16 [16, 2048, 512], P('dp', 'ctx')
- value_grad: bfloat16 [16, 2048, 512], P('dp', 'ctx')
- scale_grad: float32 [28], replicated
Inputs may be any that keep to these rules, and one draw needn't show every extreme that they name: `routes`: each device's 128 slots hold its own 8 * 128 tokens of the sequence: the live slots come first, at least 16 of them, with positions rising along the sequence; -1 marks an empty slot; in every sequence the slots of some device are all live.
All inputs are finite; a program needn't handle non-finite values.
Results may differ from a plain program's by a relative error of at most 0.03.
Values may be sent and summed in bfloat16 or wider, within the bound.
No kernel may reach another device: no remote copies, remote signals or barrier semaphores. Data moves between devices by JAX's collectives and lax.ppermute only.
A program may use at most 64 MiB of HBM per device.

v0:
```python
import math

import jax
import jax.numpy as jnp
from jax import lax
from jax.sharding import PartitionSpec as P

HEAD_SIZE = 128


def local(queries, keys, values, out_grad, routes, per_head_scale):
    query_rows = queries[0]
    key_rows = keys[0]
    value_rows = values[0]
    grad_rows = out_grad[0]
    own_pos = routes[0]
    rows = query_rows.shape[0]
    half = rows // 2
    width = query_rows.shape[1]
    kv_width = key_rows.shape[1]
    kv_heads = kv_width // HEAD_SIZE
    heads = per_head_scale.shape[0]
    group = heads // kv_heads
    cycle = lax.axis_size("ctx")
    fourfold_scale = per_head_scale.reshape(kv_heads, group, 1, 1)
    shrink = 1.0 / math.sqrt(HEAD_SIZE)
    all_pos = lax.all_gather(own_pos, "ctx", axis=0, tiled=True)
    blocks = (
        (query_rows[:half], grad_rows[:half], own_pos[:half]),
        (query_rows[half:], grad_rows[half:], own_pos[half:]),
    )

    def products(block, key_tile, value_tile):
        query_head_rows = block[0].reshape(half, kv_heads, group, HEAD_SIZE)
        gradient_heads = block[1].reshape(half, kv_heads, group, HEAD_SIZE)
        key_head_rows = key_tile.reshape(-1, kv_heads, HEAD_SIZE)
        value_head_rows = value_tile.reshape(-1, kv_heads, HEAD_SIZE)
        raw = (
            jnp.einsum(
                "qgha,kga->ghqk", query_head_rows, key_head_rows, preferred_element_type=jnp.float32
            )
            * shrink
        )
        dots = jnp.einsum(
            "qgha,kga->ghqk", gradient_heads, value_head_rows, preferred_element_type=jnp.float32
        )
        return (query_head_rows, gradient_heads, key_head_rows, raw, dots)

    def seen(query_pos, key_pos):
        return (
            (query_pos[:, None] >= 0)
            & (key_pos[None, :] >= 0)
            & (key_pos[None, :] <= query_pos[:, None])
        )

    def reaches(query_pos, key_pos):
        return jnp.max(query_pos) >= jnp.min(jnp.where(key_pos >= 0, key_pos, 2**30))

    def keep(prior):
        return prior

    def stats_tile(stats, key_tile, value_tile, key_pos):
        updated = []
        for number in range(2):
            block = blocks[number]

            def stats_work(prior, block=block):
                top, total, weighted = prior
                query_head_rows, gradient_heads, key_head_rows, raw, dots = products(
                    block, key_tile, value_tile
                )
                scores = raw * fourfold_scale
                mask = seen(block[2], key_pos)
                new_top = jnp.maximum(top, jnp.max(jnp.where(mask, scores, -1e30), axis=-1))
                weights = jnp.where(mask, jnp.exp(scores - new_top[..., None]), 0.0)
                factor = jnp.exp(top - new_top)
                return (
                    new_top,
                    total * factor + jnp.sum(weights, axis=-1),
                    weighted * factor + jnp.sum(weights * dots, axis=-1),
                )

            updated.append(lax.cond(reaches(block[2], key_pos), stats_work, keep, stats[number]))
        return tuple(updated)

    def grads_tile(state, key_tile, value_tile, key_pos):
        query_grads, scale_part, key_part, value_part = state
        new_grads = []
        for number in range(2):
            block = blocks[number]
            log_total, mean_dot = finals[number]

            def grads_work(prior, block=block, log_total=log_total, mean_dot=mean_dot):
                query_grad, scale_sum, key_gradient_sum, value_gradient_sum = prior
                query_head_rows, gradient_heads, key_head_rows, raw, dots = products(
                    block, key_tile, value_tile
                )
                scores = raw * fourfold_scale
                mask = seen(block[2], key_pos)
                prob = jnp.where(mask, jnp.exp(scores - log_total[..., None]), 0.0)
                score_grad = prob * (dots - mean_dot[..., None])
                probability_lowered = prob.astype(jnp.bfloat16)
                score_lowered = (score_grad * fourfold_scale * shrink).astype(jnp.bfloat16)
                query_grad = query_grad + jnp.einsum(
                    "ghqk,kga->qgha",
                    score_lowered,
                    key_head_rows,
                    preferred_element_type=jnp.float32,
                ).reshape(half, width)
                key_gradient_sum = key_gradient_sum + jnp.einsum(
                    "pnmc,mpnl->cpl",
                    score_lowered,
                    query_head_rows,
                    preferred_element_type=jnp.float32,
                ).reshape(-1, kv_width)
                value_gradient_sum = value_gradient_sum + jnp.einsum(
                    "pnmc,mpnl->cpl",
                    probability_lowered,
                    gradient_heads,
                    preferred_element_type=jnp.float32,
                ).reshape(-1, kv_width)
                scale_sum = scale_sum + jnp.sum(score_grad * raw, axis=(2, 3))
                return (query_grad, scale_sum, key_gradient_sum, value_gradient_sum)

            query_grad, scale_part, key_part, value_part = lax.cond(
                reaches(block[2], key_pos),
                grads_work,
                keep,
                (query_grads[number], scale_part, key_part, value_part),
            )
            new_grads.append(query_grad)
        return (tuple(new_grads), scale_part, key_part, value_part)

    empty_stats = (
        jnp.full((kv_heads, group, half), -1e30, jnp.float32),
        jnp.zeros((kv_heads, group, half), jnp.float32),
        jnp.zeros((kv_heads, group, half), jnp.float32),
    )
    stats_start = (empty_stats, empty_stats)
    grads_start = (jnp.zeros((half, width), jnp.float32), jnp.zeros((half, width), jnp.float32))
    scale_start = jnp.zeros((kv_heads, group), jnp.float32)
    finals = []

    def finish(stats):
        for number in range(2):
            top, total, weighted = stats[number]
            live = blocks[number][2] >= 0
            safe_total = jnp.where(live, total, 1.0)
            finals.append(
                (
                    jnp.where(live, top + jnp.log(safe_total), 0.0),
                    jnp.where(live, weighted / safe_total, 0.0),
                )
            )

    key_every_slot, value_every_slot = (
        lax.all_gather(key_rows, "ctx", axis=0, tiled=True),
        lax.all_gather(value_rows, "ctx", axis=0, tiled=True),
    )

    def tile_at(step):
        return (
            lax.dynamic_slice_in_dim(key_every_slot, step * rows, rows),
            lax.dynamic_slice_in_dim(value_every_slot, step * rows, rows),
            lax.dynamic_slice_in_dim(all_pos, step * rows, rows),
        )

    def stats_step(step, stats):
        key_tile, value_tile, key_pos = tile_at(step)
        return stats_tile(stats, key_tile, value_tile, key_pos)

    finish(lax.fori_loop(0, cycle, stats_step, stats_start))

    def grad_step(step, state):
        query_grads, scale_part, key_sums, value_sums = state
        key_tile, value_tile, key_pos = tile_at(step)
        key_part = lax.dynamic_slice_in_dim(key_sums, step * rows, rows)
        value_part = lax.dynamic_slice_in_dim(value_sums, step * rows, rows)
        query_grads, scale_part, key_part, value_part = grads_tile(
            (query_grads, scale_part, key_part, value_part), key_tile, value_tile, key_pos
        )
        key_sums = lax.dynamic_update_slice_in_dim(key_sums, key_part, step * rows, 0)
        value_sums = lax.dynamic_update_slice_in_dim(value_sums, value_part, step * rows, 0)
        return (query_grads, scale_part, key_sums, value_sums)

    whole = jnp.zeros((rows * cycle, kv_width), jnp.float32)
    query_grads, scale_part, key_sums, value_sums = lax.fori_loop(
        0, cycle, grad_step, (grads_start, scale_start, whole, whole)
    )
    key_total, value_total = (
        lax.psum_scatter(
            key_sums.astype(jnp.bfloat16), "ctx", scatter_dimension=0, tiled=True
        ).astype(jnp.float32),
        lax.psum_scatter(
            value_sums.astype(jnp.bfloat16), "ctx", scatter_dimension=0, tiled=True
        ).astype(jnp.float32),
    )
    first_grad = query_grads[0].astype(jnp.bfloat16)
    second_grad = query_grads[1].astype(jnp.bfloat16)
    query_out = jnp.concatenate([first_grad, second_grad], axis=0)
    scale_total = lax.psum(scale_part.reshape(heads), ("dp", "ctx"))
    return (
        query_out[None],
        key_total.astype(jnp.bfloat16)[None],
        value_total.astype(jnp.bfloat16)[None],
        scale_total,
    )


def solution(mesh):
    in_specs = (
        P("dp", "ctx", None),
        P("dp", "ctx", None),
        P("dp", "ctx", None),
        P("dp", "ctx", None),
        P("dp", "ctx"),
        P(),
    )
    out_specs = (P("dp", "ctx", None), P("dp", "ctx", None), P("dp", "ctx", None), P())
    return jax.shard_map(local, mesh=mesh, in_specs=in_specs, out_specs=out_specs, check_vma=False)
```

profile of v0, /device:TPU:38, one launch (start us, length us, event | category | flops | bytes accessed | tf_op | source)
XLA Modules:
  0.0 1049.5 jit_solution(5599732259798462172)
XLA Ops:
  9.4 33.6 %all-gather = s32[1,2048]{1,0:T(1,128)} all-gather(s32[1,128]{1,0:T(1,128)} %param.22), channel_id=2, replica_groups=mesh['dp'=16,'ctx'=16] {'ctx'}, dimensions={1}, use_global_device_ids=true | all-gather | bytes 8704 | tf_op jit(solution)/shard_map/all_gather | solution.py:27
  45.9 2.5 slice_bitcast_fusion
  48.4 34.1 %all-gather.6.cloned.1.call-done = bf16[1,2048,512]{2,1,0:T(8,128)(2,1)} async-done(((bf16[1,128,512]{2,1,0:T(8,128)(2,1)}), bf16[1,2048,512]{2,1,0:T(8,128)(2,1)}) %all-gather.6.cloned.1.call-update) | async-done | bytes 2097168 | tf_op jit(solution)/shard_map/all_gather | solution.py:157
  82.5 70.3 %all-gather.8.cloned.1.call-done = bf16[1,2048,512]{2,1,0:T(8,128)(2,1)} async-done(((bf16[1,128,512]{2,1,0:T(8,128)(2,1)}), bf16[1,2048,512]{2,1,0:T(8,128)(2,1)}) %all-gather.8.cloned.1.call-update) | async-done | bytes 2097168 | tf_op jit(solution)/shard_map/all_gather | solution.py:158
  152.9 177.6 %while.46 = (s32[]{:T(128)}, f32[4,7,64]{2,1,0:T(8,128)S(1)}, f32[4,7,64]{2,1,0:T(8,128)S(1)}, f32[4,7,64]{2,1,0:T(8,128)S(1)}, f32[4,7,64]{2,1,0:T(8,128)S(1)},...) while((s32[]{:T(128)}, f32[4,7,64]{2,1,0:T(8,128)S(1)}, ...), condition=%wide.region_14.0_spmd, body=%wide.region_2.14_spmd.sunk | while | flops 239529280 | bytes 13436883 | solution.py:172
  157.9 5.5 conditional.8
  163.4 4.2 conditional.9
  172.6 5.5 conditional.8
  178.1 4.2 conditional.9
  187.3 5.5 conditional.8
  192.8 4.2 conditional.9
  202.0 5.5 conditional.8
  207.5 4.2 conditional.9
  216.8 5.5 conditional.8
  222.3 4.2 conditional.9
  231.5 5.5 conditional.8
  237.0 4.2 conditional.9
  246.2 5.5 conditional.8
  251.7 4.2 conditional.9
  260.9 5.5 conditional.8
  266.4 4.2 conditional.9
  275.6 5.5 conditional.8
  281.1 4.2 conditional.9
  290.3 5.5 conditional.8
  295.8 4.2 conditional.9
  333.8 2.5 broadcast_in_dim.110.clone2
  336.3 2.5 broadcast_in_dim.110.clone
  338.7 371.1 %while.47 = (s32[]{:T(128)}, f32[64,3584]{1,0:T(8,128)}, f32[64,3584]{1,0:T(8,128)}, f32[4,7]{1,0:T(4,128)S(1)}, f32[2048,512]{1,0:T(8,128)}, /*index=5*/f32[204...) while((s32[]{:T(128)}, f32[64,3584]{1,0:T(8,128)}, ...), condition=%wide.region_23.24_spmd, body=%wide.region_15.23_spmd.sunk | while | flops 596230976 | bytes 43935392 | solution.py:187
  347.4 11.7 %conditional.10 = ((f32[64,3584]{1,0:T(8,128)}, f32[4,7]{1,0:T(4,128)S(1)}, f32[128,512]{0,1:T(8,128)S(1)}, f32[128,512]{0,1:T(8,128)S(1)})) conditional(s32[]{:T(128)} %convert_element_type.80, (f32[64,3584]{1,0:T(8,128)}, f32[4,7]{1,0:T(4,128)S(1)}, f32[128,512]{0,1:T(8,128)S(1)}, f32[128,512]{0,1:T(8,128)S(1)}) %tuple.134, (s32[64]{0:T(128)}, ...), branch_computations={%region_17.17_spmd, %region_18.19_spmd} | conditional | flops 298115296 | bytes 19578888 | solution.py:125
  359.1 9.7 conditional.11
  366.5 2.3 add.100
  378.6 11.7 %conditional.10 = ((f32[64,3584]{1,0:T(8,128)}, f32[4,7]{1,0:T(4,128)S(1)}, f32[128,512]{0,1:T(8,128)S(1)}, f32[128,512]{0,1:T(8,128)S(1)})) conditional(s32[]{:T(128)} %convert_element_type.80, (f32[64,3584]{1,0:T(8,128)}, f32[4,7]{1,0:T(4,128)S(1)}, f32[128,512]{0,1:T(8,128)S(1)}, f32[128,512]{0,1:T(8,128)S(1)}) %tuple.134, (s32[64]{0:T(128)}, ...), branch_computations={%region_17.17_spmd, %region_18.19_spmd} | conditional | flops 298115296 | bytes 19578888 | solution.py:125
  390.3 9.7 conditional.11
  397.7 2.3 add.100
  409.8 11.7 %conditional.10 = ((f32[64,3584]{1,0:T(8,128)}, f32[4,7]{1,0:T(4,128)S(1)}, f32[128,512]{0,1:T(8,128)S(1)}, f32[128,512]{0,1:T(8,128)S(1)})) conditional(s32[]{:T(128)} %convert_element_type.80, (f32[64,3584]{1,0:T(8,128)}, f32[4,7]{1,0:T(4,128)S(1)}, f32[128,512]{0,1:T(8,128)S(1)}, f32[128,512]{0,1:T(8,128)S(1)}) %tuple.134, (s32[64]{0:T(128)}, ...), branch_computations={%region_17.17_spmd, %region_18.19_spmd} | conditional | flops 298115296 | bytes 19578888 | solution.py:125
  419.2 2.3 add.96
  421.5 9.7 conditional.11
  428.9 2.3 add.100
  441.0 11.7 %conditional.10 = ((f32[64,3584]{1,0:T(8,128)}, f32[4,7]{1,0:T(4,128)S(1)}, f32[128,512]{0,1:T(8,128)S(1)}, f32[128,512]{0,1:T(8,128)S(1)})) conditional(s32[]{:T(128)} %convert_element_type.80, (f32[64,3584]{1,0:T(8,128)}, f32[4,7]{1,0:T(4,128)S(1)}, f32[128,512]{0,1:T(8,128)S(1)}, f32[128,512]{0,1:T(8,128)S(1)}) %tuple.134, (s32[64]{0:T(128)}, ...), branch_computations={%region_17.17_spmd, %region_18.19_spmd} | conditional | flops 298115296 | bytes 19578888 | solution.py:125
  452.7 9.7 conditional.11
  460.1 2.3 add.100
  472.2 11.7 %conditional.10 = ((f32[64,3584]{1,0:T(8,128)}, f32[4,7]{1,0:T(4,128)S(1)}, f32[128,512]{0,1:T(8,128)S(1)}, f32[128,512]{0,1:T(8,128)S(1)})) conditional(s32[]{:T(128)} %convert_element_type.80, (f32[64,3584]{1,0:T(8,128)}, f32[4,7]{1,0:T(4,128)S(1)}, f32[128,512]{0,1:T(8,128)S(1)}, f32[128,512]{0,1:T(8,128)S(1)}) %tuple.134, (s32[64]{0:T(128)}, ...), branch_computations={%region_17.17_spmd, %region_18.19_spmd} | conditional | flops 298115296 | bytes 19578888 | solution.py:125
  483.9 9.7 conditional.11
  491.3 2.3 add.100
  503.4 11.7 %conditional.10 = ((f32[64,3584]{1,0:T(8,128)}, f32[4,7]{1,0:T(4,128)S(1)}, f32[128,512]{0,1:T(8,128)S(1)}, f32[128,512]{0,1:T(8,128)S(1)})) conditional(s32[]{:T(128)} %convert_element_type.80, (f32[64,3584]{1,0:T(8,128)}, f32[4,7]{1,0:T(4,128)S(1)}, f32[128,512]{0,1:T(8,128)S(1)}, f32[128,512]{0,1:T(8,128)S(1)}) %tuple.134, (s32[64]{0:T(128)}, ...), branch_computations={%region_17.17_spmd, %region_18.19_spmd} | conditional | flops 298115296 | bytes 19578888 | solution.py:125
  512.9 2.3 add.96
  515.1 9.7 conditional.11
  522.5 2.3 add.100
  534.6 11.7 %conditional.10 = ((f32[64,3584]{1,0:T(8,128)}, f32[4,7]{1,0:T(4,128)S(1)}, f32[128,512]{0,1:T(8,128)S(1)}, f32[128,512]{0,1:T(8,128)S(1)})) conditional(s32[]{:T(128)} %convert_element_type.80, (f32[64,3584]{1,0:T(8,128)}, f32[4,7]{1,0:T(4,128)S(1)}, f32[128,512]{0,1:T(8,128)S(1)}, f32[128,512]{0,1:T(8,128)S(1)}) %tuple.134, (s32[64]{0:T(128)}, ...), branch_computations={%region_17.17_spmd, %region_18.19_spmd} | conditional | flops 298115296 | bytes 19578888 | solution.py:125
  546.3 9.7 conditional.11
  553.7 2.3 add.100
  565.8 11.7 %conditional.10 = ((f32[64,3584]{1,0:T(8,128)}, f32[4,7]{1,0:T(4,128)S(1)}, f32[128,512]{0,1:T(8,128)S(1)}, f32[128,512]{0,1:T(8,128)S(1)})) conditional(s32[]{:T(128)} %convert_element_type.80, (f32[64,3584]{1,0:T(8,128)}, f32[4,7]{1,0:T(4,128)S(1)}, f32[128,512]{0,1:T(8,128)S(1)}, f32[128,512]{0,1:T(8,128)S(1)}) %tuple.134, (s32[64]{0:T(128)}, ...), branch_computations={%region_17.17_spmd, %region_18.19_spmd} | conditional | flops 298115296 | bytes 19578888 | solution.py:125
  577.5 9.7 conditional.11
  584.9 2.3 add.100
  597.0 11.7 %conditional.10 = ((f32[64,3584]{1,0:T(8,128)}, f32[4,7]{1,0:T(4,128)S(1)}, f32[128,512]{0,1:T(8,128)S(1)}, f32[128,512]{0,1:T(8,128)S(1)})) conditional(s32[]{:T(128)} %convert_element_type.80, (f32[64,3584]{1,0:T(8,128)}, f32[4,7]{1,0:T(4,128)S(1)}, f32[128,512]{0,1:T(8,128)S(1)}, f32[128,512]{0,1:T(8,128)S(1)}) %tuple.134, (s32[64]{0:T(128)}, ...), branch_computations={%region_17.17_spmd, %region_18.19_spmd} | conditional | flops 298115296 | bytes 19578888 | solution.py:125
  608.7 9.7 conditional.11
  616.1 2.3 add.100
  628.3 11.7 %conditional.10 = ((f32[64,3584]{1,0:T(8,128)}, f32[4,7]{1,0:T(4,128)S(1)}, f32[128,512]{0,1:T(8,128)S(1)}, f32[128,512]{0,1:T(8,128)S(1)})) conditional(s32[]{:T(128)} %convert_element_type.80, (f32[64,3584]{1,0:T(8,128)}, f32[4,7]{1,0:T(4,128)S(1)}, f32[128,512]{0,1:T(8,128)S(1)}, f32[128,512]{0,1:T(8,128)S(1)}) %tuple.134, (s32[64]{0:T(128)}, ...), branch_computations={%region_17.17_spmd, %region_18.19_spmd} | conditional | flops 298115296 | bytes 19578888 | solution.py:125
  640.0 9.7 conditional.11
  647.3 2.3 add.100
  709.9 3.8 convert_element_type.63
  713.8 3.9 convert_element_type.62
  717.7 258.9 %psum.7 = f32[28]{0:T(128)} all-reduce(f32[28]{0:T(128)S(1)} %reshape.121), channel_id=1, replica_groups=mesh['dp'=16,'ctx'=16] {'dp','ctx'}, use_global_device_ids=true, to_apply=%region_26.27 | all-reduce | flops 28 | bytes 224 | tf_op jit(solution)/shard_map/psum | solution.py:201
  978.9 64.1 %reduce-scatter.3.cloned.1.call-done = bf16[128,512]{1,0:T(8,128)(2,1)} async-done(((bf16[2048,512]{1,0:T(8,128)(2,1)}), bf16[128,512]{1,0:T(8,128)(2,1)}) %reduce-scatter.3.cloned.1.call-update) | async-done | bytes 131088 | tf_op jit(solution)/shard_map/reduce_scatter | solution.py:191
  (913 shorter events, 443.1 us)
Async XLA Ops:
  7.2 75.4 %all-gather.6.cloned.1.call-start = ((), (), s32[]{:S(2)}) async-start(), calls=%async_computation.4 | async-start | bytes 2228224 | tf_op jit(solution)/shard_map/all_gather | solution.py:157
  7.9 144.9 %all-gather.8.cloned.1.call-start = ((), (), s32[]{:S(2)}) async-start(), calls=%async_computation.5 | async-start | bytes 2228224 | tf_op jit(solution)/shard_map/all_gather | solution.py:158
  8.6 970.2 %reduce-scatter.5.cloned.1.call-start = ((), (), s32[]{:S(2)}) async-start(), calls=%async_computation.3 | async-start | bytes 2228224 | tf_op jit(solution)/shard_map/reduce_scatter | solution.py:194
  359.1 5.0 copy-start.1
  359.1 5.0 copy-start.2
  390.3 5.0 copy-start.1
  390.3 5.0 copy-start.2
  421.5 5.0 copy-start.1
  421.5 5.0 copy-start.2
  452.7 5.0 copy-start.1
  452.7 5.0 copy-start.2
  483.9 5.0 copy-start.1
  483.9 5.0 copy-start.2
  515.1 5.0 copy-start.1
  515.1 5.0 copy-start.2
  546.3 5.0 copy-start.1
  546.3 5.0 copy-start.2
  577.5 5.0 copy-start.1
  577.5 5.0 copy-start.2
  608.7 5.0 copy-start.1
  608.7 5.0 copy-start.2
  640.0 5.0 copy-start.1
  640.0 5.0 copy-start.2
  713.7 329.3 %reduce-scatter.3.cloned.1.call-start = ((), (), s32[]{:S(2)}) async-start(), calls=%async_computation.2 | async-start | bytes 2228224 | tf_op jit(solution)/shard_map/reduce_scatter | solution.py:191
  713.8 264.1 %copy-start = (f32[64,3584]{1,0:T(8,128)S(1)}, f32[64,3584]{1,0:T(8,128)}, u32[]{:S(2)}) copy-start(f32[64,3584]{1,0:T(8,128)} %get-tuple-element.986) | copy-start | bytes 2752516
Sparse Core Ops, SparseCore 0:
  9.8 72.6 all-gather.5
  84.3 68.4 all-gather.7
  713.8 255.7 reduce-scatter.4
  972.6 70.3 reduce-scatter.2
where the time goes:
time: 1070 us; the launch traced here: 1050 us
  blocking collectives  292 us (27%)
  local copies, waits for them, and re-layouts  240 us (22%)
  waiting for transfers between devices  170 us (16%)
  other arithmetic  150 us (14%)
  matrix products  94 us (9%)
  loops' own time  89 us (8%)
  between operations  13.8 us (1%)
    psum x1, blocking collectives, local(): scale_total = lax.psum(scale_part.reshape(heads), ('dp', 'ctx'))  259 us
    all_gather x1, waiting for transfers between devices, local(): lax.all_gather(value_rows, 'ctx', axis=0, tiled=True)  70.3 us
    reduce_scatter x1, waiting for transfers between devices, local(): lax.psum_scatter(key_sums.astype(jnp.bfloat16), 'ctx', scatter_dimension=...  64.1 us
    reshape x40, local copies, waits for them, and re-layouts, products(): query_head_rows = block[0].reshape(half, kv_heads, group, HEAD_SIZE)  63.5 us
    add x20, other arithmetic, grads_work(): query_grad + jnp.einsum('ghqk,kga->qgha', score_lowered, key_head_rows, p...  46.1 us
    reduce_min x32, other arithmetic, reaches(): jnp.min(jnp.where(key_pos >= 0, key_pos, 2 ** 30))  44.5 us
    another operation x1, loops' own time, local(): lax.fori_loop(0, cycle, grad_step, (grads_start, scale_start, whole, whole))  42.5 us
    another operation x1, loops' own time, local(): finish(lax.fori_loop(0, cycle, stats_step, stats_start))  42.4 us
  transfers between devices with their start and end apart: 4, of which 3 were waited for; matrix products, arithmetic and copies ran while one was open for 1% of the time, Pallas kernels for 0%

commit v1 on v0

v1 whole, which is shorter than its diff:
```python
import functools
import math

import jax
import jax.numpy as jnp
from jax import lax
from jax.experimental import pallas as pl
from jax.experimental.pallas import tpu as pltpu
from jax.sharding import PartitionSpec as P

F32 = jnp.float32
BF16 = jnp.bfloat16
HEAD = 128
ROWS = 128
KV_HEADS = 2
GROUP = 7
HEADS = KV_HEADS * GROUP
WIDE = GROUP * ROWS
POS = 16
MESSAGE = POS + 2 * ROWS
TILE = 128
FAR = 32768.0
LOW = -1e30
LOG2E = 1.4426950408889634
NT = (((1,), (1,)), ((), ()))
NN = (((1,), (0,)), ((), ()))
TN = (((0,), (0,)), ((), ()))


def product(a, b, dims):
    return lax.dot_general(a, b, dims, preferred_element_type=F32)


def call(body, outs, scratch, flops, moved, operands):
    return pl.pallas_call(
        body,
        out_shape=outs,
        in_specs=operands,
        scratch_shapes=scratch,
        cost_estimate=pl.CostEstimate(
            flops=flops, bytes_accessed=moved, transcendentals=flops // 1024
        ),
        compiler_params=pltpu.CompilerParams(vmem_limit_bytes=48 * 1024 * 1024),
    )


def pack_keys_body(x_ref, key_ref, value_ref, pos_ref, keep_ref, send_ref):
    x = x_ref[0]
    pos = pos_ref[...]
    dead = pos < 0
    high = jnp.where(dead, 256, pos >> 7)
    low = jnp.where(dead, 0, pos & 127)
    row = jnp.concatenate([high, low], axis=1).astype(F32)
    rows = jnp.broadcast_to(row, (POS, 2 * ROWS)).astype(BF16)
    for ref, half in ((keep_ref, x), (send_ref, 1 - x)):
        at = pl.multiple_of(half * KV_HEADS * HEAD, KV_HEADS * HEAD)
        ref[0:POS, :] = rows
        ref[POS : POS + ROWS, :] = key_ref[:, pl.ds(at, KV_HEADS * HEAD)]
        ref[POS + ROWS : MESSAGE, :] = value_ref[:, pl.ds(at, KV_HEADS * HEAD)]


def pack_queries_body(x_ref, query_ref, grad_ref, keep_ref, send_ref):
    x = x_ref[0]
    for ref, half in ((keep_ref, x), (send_ref, 1 - x)):
        for number, source in enumerate((query_ref, grad_ref)):
            for head in range(HEADS):
                at = pl.multiple_of(half * HEADS * HEAD + head * HEAD, HEAD)
                ref[number, head * ROWS : (head + 1) * ROWS, :] = source[:, pl.ds(at, HEAD)]


def unpack_queries_body(x_ref, keep_ref, got_ref, out_ref):
    x = x_ref[0]
    for ref, half in ((keep_ref, x), (got_ref, 1 - x)):
        for head in range(HEADS):
            at = pl.multiple_of(half * HEADS * HEAD + head * HEAD, HEAD)
            out_ref[:, pl.ds(at, HEAD)] = ref[head * ROWS : (head + 1) * ROWS, :]


def positions(ref, slot):
    row = ref[slot, 0:POS, :].astype(F32)[0:1, :]
    return row[:, :ROWS] * 128.0 + row[:, ROWS:]


def query_side(own_ref):
    rows = [positions(own_ref, slot) for slot in range(2)]
    rows = [jnp.where(row >= FAR, -1.0, row) for row in rows]
    tops = [jnp.max(row) for row in rows]
    first = jnp.where(tops[0] < tops[1], 0, 1)
    return rows, tops, first


def place(blocks, first, top, key_c, value_c, pos_c, turned):
    key_c[...] = jnp.zeros_like(key_c)
    value_c[...] = jnp.zeros_like(value_c)
    pos_c[...] = jnp.full_like(pos_c, 1e9)
    start = jnp.int32(0)
    entries = []
    for phase in range(2):
        slot = first if phase == 0 else 1 - first
        rows = [positions(ref, slot) for ref in blocks]
        begins = [jnp.min(row) for row in rows]
        counts = [jnp.sum(jnp.where(row < FAR, 1.0, 0.0)).astype(jnp.int32) for row in rows]
        counts = [jnp.where(begin <= top, n, 0) for begin, n in zip(begins, counts)]
        spans = [(n + 15) >> 4 for n in counts]
        if len(blocks) == 2:
            ahead = begins[0] < begins[1]
            starts = [
                start + jnp.where(ahead, 0, spans[1] * 16),
                start + jnp.where(ahead, spans[0] * 16, 0),
            ]
        else:
            starts = []
            total = start
            for span in spans:
                starts.append(total)
                total = total + span * 16
        for ref, row, at, span in zip(blocks, rows, starts, spans):
            turned[...] = jnp.broadcast_to(row, (ROWS, ROWS)).T

            def chunk(step, _, ref=ref, at=at, slot=slot):
                source = pl.multiple_of(step * 16, 16)
                target = pl.multiple_of(at + step * 16, 16)
                pos_c[pl.ds(target, 16), :] = turned[pl.ds(source, 16), :]
                for g in range(KV_HEADS):
                    lanes = slice(g * HEAD, (g + 1) * HEAD)
                    key_c[g, pl.ds(target, 16), :] = ref[slot, pl.ds(POS + source, 16), lanes]
                    value_c[g, pl.ds(target, 16), :] = ref[
                        slot, pl.ds(POS + ROWS + source, 16), lanes
                    ]
                return 0

            lax.fori_loop(0, span, chunk, 0)
        entries.append((slot, starts, counts))
        start = start + sum(spans) * 16
    return start, entries


def stats_body(count, is_first, is_last, *refs):
    rate_ref, own_ref, kept_ref, got_ref = refs[:4]
    blocks = refs[4 : 4 + count]
    refs = refs[4 + count :]
    if not is_first:
        prior_ref, refs = refs[0], refs[1:]
    if is_last:
        final_ref, scale_ref, state, key_c, value_c, pos_c, turned = refs
    else:
        state, key_c, value_c, pos_c, turned = refs
    query_rows, tops, first = query_side(own_ref)
    length, _ = place(
        blocks, first, jnp.maximum(tops[0], tops[1]), key_c, value_c, pos_c, turned
    )
    if is_first:
        state[...] = jnp.zeros_like(state)
        state[:, 0:1, :] = jnp.full((2 * KV_HEADS, 1, WIDE), LOW, F32)
    else:
        state[...] = prior_ref[...]

    def tile(step, _):
        at = pl.multiple_of(step * TILE, TILE)
        key_pos = pos_c[pl.ds(at, TILE), :]
        lowest = jnp.min(key_pos)
        for slot in range(2):
            work_ref = (kept_ref, got_ref)[slot]

            @pl.when(lowest <= tops[slot])
            def _(slot=slot, work_ref=work_ref):
                mask = key_pos <= query_rows[slot]

                def group(g, _):
                    some = pl.ds(pl.multiple_of(g * WIDE, WIDE), WIDE)
                    keys = key_c[g, pl.ds(at, TILE), :]
                    values = value_c[g, pl.ds(at, TILE), :]
                    raw = product(keys, work_ref[0, some, :], NT)
                    dots = product(values, work_ref[1, some, :], NT)
                    for head in range(GROUP):
                        lanes = slice(head * ROWS, (head + 1) * ROWS)
                        scores = jnp.where(
                            mask, raw[:, lanes] * rate_ref[g, 0:1, lanes], LOW
                        )
                        held = state[slot * KV_HEADS + g, :, lanes]
                        top, total, weighted = held[0:1], held[1:2], held[2:3]
                        shifted, both = held[3:4], held[4:5]
                        new_top = jnp.maximum(top, jnp.max(scores, axis=0, keepdims=True))
                        above = scores - new_top
                        weights = jnp.exp2(above)
                        weighted_dots = weights * dots[:, lanes]
                        step_down = top - new_top
                        factor = jnp.exp2(step_down)
                        shifted = factor * (shifted + step_down * total) + jnp.sum(
                            weights * above, axis=0, keepdims=True
                        )
                        both = factor * (both + step_down * weighted) + jnp.sum(
                            weighted_dots * above, axis=0, keepdims=True
                        )
                        total = factor * total + jnp.sum(weights, axis=0, keepdims=True)
                        weighted = factor * weighted + jnp.sum(
                            weighted_dots, axis=0, keepdims=True
                        )
                        state[slot * KV_HEADS + g, 0:5, lanes] = jnp.concatenate(
                            [new_top, total, weighted, shifted, both], axis=0
                        )
                    return 0

                lax.fori_loop(0, KV_HEADS, group, 0)

        return 0

    lax.fori_loop(0, (length + TILE - 1) // TILE, tile, 0)
    if not is_last:
        return
    lane = lax.broadcasted_iota(jnp.int32, (8, ROWS), 1)
    scale_row = jnp.zeros((8, ROWS), F32)
    for slot in range(2):
        live = query_rows[slot] >= 0.0
        for g in range(KV_HEADS):
            for head in range(GROUP):
                lanes = slice(head * ROWS, (head + 1) * ROWS)
                held = state[slot * KV_HEADS + g, :, lanes]
                top, total, weighted = held[0:1], held[1:2], held[2:3]
                shifted, both = held[3:4], held[4:5]
                total = jnp.where(live, total, 1.0)
                mean = weighted / total
                spread = (both - mean * shifted) / total
                rate = rate_ref[g, 0:1, lanes] * math.sqrt(HEAD)
                spread = jnp.where(live, spread / rate, 0.0)
                final_ref[slot * KV_HEADS + g, 0:2, lanes] = jnp.concatenate(
                    [
                        jnp.where(live, top + jnp.log2(total), -LOW),
                        jnp.where(live, mean, 0.0),
                    ],
                    axis=0,
                )
                place_at = first * HEADS + g * GROUP + head
                scale_row = scale_row + jnp.where(
                    lane == place_at, jnp.sum(spread, axis=1, keepdims=True), 0.0
                )
    scale_ref[...] = scale_row


def grads_body(count, is_first, is_last, *refs):
    rate_ref, own_ref, kept_ref, got_ref, final_ref = refs[:5]
    blocks = refs[5 : 5 + count]
    refs = refs[5 + count :]
    if not is_first:
        prior_ref, refs = refs[0], refs[1:]
    outs, refs = refs[:count], refs[count:]
    if is_last:
        query_outs, refs = refs[:2], refs[2:]
    query_sum, key_c, value_c, pos_c, turned, key_sum, value_sum = refs
    query_rows, tops, first = query_side(own_ref)
    length, entries = place(
        blocks, first, jnp.maximum(tops[0], tops[1]), key_c, value_c, pos_c, turned
    )
    key_sum[...] = jnp.zeros_like(key_sum)
    value_sum[...] = jnp.zeros_like(value_sum)
    if is_first:
        query_sum[...] = jnp.zeros_like(query_sum)
    else:
        query_sum[...] = prior_ref[...]

    def tile(step, _):
        at = pl.multiple_of(step * TILE, TILE)
        key_pos = pos_c[pl.ds(at, TILE), :]
        lowest = jnp.min(key_pos)
        for slot in range(2):
            work_ref = (kept_ref, got_ref)[slot]

            @pl.when(lowest <= tops[slot])
            def _(slot=slot, work_ref=work_ref):
                mask = key_pos <= query_rows[slot]

                def group(g, _):
                    some = pl.ds(pl.multiple_of(g * WIDE, WIDE), WIDE)
                    keys = key_c[g, pl.ds(at, TILE), :]
                    values = value_c[g, pl.ds(at, TILE), :]
                    queries = work_ref[0, some, :]
                    gradients = work_ref[1, some, :]
                    raw = product(keys, queries, NT)
                    dots = product(values, gradients, NT)
                    probs, score_grads = [], []
                    for head in range(GROUP):
                        lanes = slice(head * ROWS, (head + 1) * ROWS)
                        rate = rate_ref[g, 0:1, lanes]
                        held = final_ref[slot * KV_HEADS + g, :, lanes]
                        prob = jnp.where(
                            mask, jnp.exp2(raw[:, lanes] * rate - held[0:1]), 0.0
                        )
                        grad = prob * (dots[:, lanes] - held[1:2])
                        probs.append(prob.astype(BF16))
                        score_grads.append((grad * (rate * (1.0 / LOG2E))).astype(BF16))
                    prob_low = jnp.concatenate(probs, axis=1)
                    score_low = jnp.concatenate(score_grads, axis=1)
                    rows = pl.ds(at, TILE)
                    value_sum[g, rows, :] += product(prob_low, gradients, NN)
                    key_sum[g, rows, :] += product(score_low, queries, NN)
                    query_sum[slot * KV_HEADS + g] += product(keys, score_low, TN)
                    return 0

                lax.fori_loop(0, KV_HEADS, group, 0)

        return 0

    lax.fori_loop(0, (length + TILE - 1) // TILE, tile, 0)
    row = lax.broadcasted_iota(jnp.int32, (ROWS, HEAD), 0)
    for slot, starts, counts in entries:
        for out, at, n in zip(outs, starts, counts):
            at = pl.multiple_of(at, 16)
            for g in range(KV_HEADS):
                lanes = slice(g * HEAD, (g + 1) * HEAD)
                for number, total in enumerate((key_sum, value_sum)):
                    out[slot, number * ROWS : (number + 1) * ROWS, lanes] = jnp.where(
                        row < n, total[g, pl.ds(at, ROWS), :], 0.0
                    )
    if is_last:
        for slot in range(2):
            for g in range(KV_HEADS):
                for head in range(GROUP):
                    lanes = slice(head * ROWS, (head + 1) * ROWS)
                    rows = slice((g * GROUP + head) * ROWS, (g * GROUP + head + 1) * ROWS)
                    query_outs[slot][rows, :] = query_sum[slot * KV_HEADS + g, :, lanes].T.astype(
                        BF16
                    )


def compact_scratch(count):
    size = (2 * count + 1) * ROWS
    return [
        pltpu.VMEM((KV_HEADS, size, HEAD), BF16),
        pltpu.VMEM((KV_HEADS, size, HEAD), BF16),
        pltpu.VMEM((size, ROWS), F32),
        pltpu.VMEM((ROWS, ROWS), F32),
    ]


STATE = jax.ShapeDtypeStruct((2 * KV_HEADS, 8, WIDE), F32)


def stats(rate, own, kept, got, blocks, prior=None, is_last=False):
    count = len(blocks)
    if is_last:
        outs = [STATE, jax.ShapeDtypeStruct((8, ROWS), F32)]
        scratch = [pltpu.VMEM(STATE.shape, F32)]
    else:
        outs, scratch = [STATE], []
    operands = [rate, own, kept, got, *blocks] + ([] if prior is None else [prior])
    return call(
        functools.partial(stats_body, count, prior is None, is_last),
        outs,
        scratch + compact_scratch(count),
        count * 2 * ROWS * 2 * HEADS * ROWS * 2 * HEAD * 2,
        4 << 20,
        [pl.BlockSpec(memory_space=pltpu.VMEM)] * len(operands),
    )(*operands)


def grads(rate, own, kept, got, final, blocks, prior=None, is_last=False):
    count = len(blocks)
    outs = [jax.ShapeDtypeStruct((2, 2 * ROWS, KV_HEADS * HEAD), F32)] * count
    sums = jax.ShapeDtypeStruct((2 * KV_HEADS, HEAD, WIDE), F32)
    operands = [rate, own, kept, got, final, *blocks] + ([] if prior is None else [prior])
    if is_last:
        outs = outs + [jax.ShapeDtypeStruct((HEADS * ROWS, HEAD), BF16)] * 2
        scratch = [pltpu.VMEM(sums.shape, F32)]
    else:
        outs, scratch = outs + [sums], []
    size = (2 * count + 1) * ROWS
    scratch = (
        scratch
        + compact_scratch(count)
        + [pltpu.VMEM((KV_HEADS, size, HEAD), F32), pltpu.VMEM((KV_HEADS, size, HEAD), F32)]
    )
    return call(
        functools.partial(grads_body, count, prior is None, is_last),
        outs,
        scratch,
        count * 2 * ROWS * 2 * HEADS * ROWS * 2 * HEAD * 5,
        6 << 20,
        [pl.BlockSpec(memory_space=pltpu.VMEM)] * len(operands),
    )(*operands)


def local(queries, keys, values, out_grad, routes, per_head_scale):
    me = lax.axis_index("ctx")
    size = lax.axis_size("ctx")
    ring = size // 2
    x = (me // ring).astype(jnp.int32)
    x_ref = x.reshape(1)
    across = [(i, (i + ring) % size) for i in range(size)]

    def neighbour(i, up):
        base, z = i // ring * ring, i % ring
        return base + (z + (1 if up == (z % 2 == 0) else -1)) % ring

    even = [(i, neighbour(i, True)) for i in range(size)]
    odd = [(i, neighbour(i, False)) for i in range(size)]

    def swap(array, pairs, axis="ctx"):
        return lax.ppermute(array, axis, pairs)

    smem = pl.BlockSpec(memory_space=pltpu.SMEM)
    vmem = pl.BlockSpec(memory_space=pltpu.VMEM)
    message = jax.ShapeDtypeStruct((MESSAGE, KV_HEADS * HEAD), BF16)
    keys_kept, keys_sent = call(
        pack_keys_body,
        [message, message],
        [],
        1024,
        1 << 20,
        operands=[smem, vmem, vmem, vmem],
    )(x_ref, keys[0], values[0], routes)
    keys_got = swap(keys_sent, across)
    work = jax.ShapeDtypeStruct((2, HEADS * ROWS, HEAD), BF16)
    kept, sent = call(
        pack_queries_body, [work, work], [], 1024, 4 << 20, operands=[smem, vmem, vmem]
    )(x_ref, queries[0], out_grad[0])
    got = swap(sent, across)
    own = jnp.stack([keys_kept, keys_got])

    half_scale = lax.dynamic_slice_in_dim(per_head_scale, x * HEADS, HEADS)
    rate = jnp.repeat(half_scale * (LOG2E / math.sqrt(HEAD)), ROWS).reshape(KV_HEADS, 1, WIDE)
    rate = jnp.broadcast_to(rate, (KV_HEADS, 8, WIDE))

    a, b = [own], [own]
    for step in range(1, 4):
        a.append(swap(b[step - 1], even))
        b.append(swap(a[step - 1], odd))
    a.append(swap(b[3], even))

    (state,) = stats(rate, own, kept, got, [own, a[1], b[1], a[2], b[2]])
    final, scale_part = stats(rate, own, kept, got, [a[3], b[3], a[4]], state, is_last=True)

    def exchange_sum(array):
        for bit in range(4):
            pairs = [(i, i ^ (1 << bit)) for i in range(16)]
            array = array + swap(array, pairs, "ctx")
        for bit in range(4):
            pairs = [(i, i ^ (1 << bit)) for i in range(16)]
            array = array + swap(array, pairs, "dp")
        return array

    scale_total = exchange_sum(scale_part)

    far, sums = grads(rate, own, kept, got, final, [a[4]])
    from_even = swap(far.astype(BF16), even)
    part_a, part_b, sums = grads(rate, own, kept, got, final, [a[3], b[3]], sums)
    sent_a = swap(part_a.astype(BF16), even)
    to_b = (part_b + from_even).astype(BF16)
    sent_b = swap(to_b, odd)
    for step in (2, 1):
        if step == 2:
            part_a, part_b, sums = grads(rate, own, kept, got, final, [a[2], b[2]], sums)
        else:
            near, sums = grads(rate, own, kept, got, final, [own], sums)
            part_a, part_b, query_kept, query_sent = grads(
                rate, own, kept, got, final, [a[1], b[1]], sums, is_last=True
            )
        to_a = (part_a + sent_b).astype(BF16)
        to_b = (part_b + sent_a).astype(BF16)
        sent_a, sent_b = swap(to_a, even), swap(to_b, odd)
    query_got = swap(query_sent, across)
    total = (near + sent_a + sent_b).astype(BF16)
    other = swap(total[1], across)
    left = jnp.where(x == 0, total[0], other)
    right = jnp.where(x == 0, other, total[0])
    both = jnp.concatenate([left, right], axis=1)
    query_out = call(
        unpack_queries_body,
        jax.ShapeDtypeStruct((ROWS, 2 * HEADS * HEAD), BF16),
        [],
        1024,
        2 << 20,
        operands=[smem, vmem, vmem],
    )(x_ref, query_kept, query_got)
    return (
        query_out[None],
        both[None, :ROWS],
        both[None, ROWS:],
        scale_total[0, : 2 * HEADS],
    )


def solution(mesh):
    in_specs = (
        P("dp", "ctx", None),
        P("dp", "ctx", None),
        P("dp", "ctx", None),
        P("dp", "ctx", None),
        P("dp", "ctx"),
        P(),
    )
    out_specs = (P("dp", "ctx", None), P("dp", "ctx", None), P("dp", "ctx", None), P())
    return jax.shard_map(local, mesh=mesh, in_specs=in_specs, out_specs=out_specs, check_vma=False)
```

time: 1070 us -> 157 us (0.15); the launches traced: 1050 us -> 155 us
  blocking collectives: 292 us -> 0 us
  local copies, waits for them, and re-layouts: 240 us -> 9.31 us
  other arithmetic: 150 us -> 1.34 us
  waiting for transfers between devices: 170 us -> 46.3 us
  matrix products: 94 us -> 0 us
  loops' own time: 89 us -> 0 us
  starting transfers between devices: 0.16 us -> 58 us
  Pallas kernels: 0 us -> 39.3 us
  between operations: 13.8 us -> 0.91 us
    psum x1 -> x0, blocking collectives: 259 us -> none  [local(): scale_total = lax.psum(scale_part.reshape(heads), ('dp', 'ctx'))]
    reshape x182 -> x0, local copies, waits for them, and re-layouts: 112 us -> none  [the longest x40 63.5 us: products(): query_head_rows = block[0].reshape(half, kv_heads, group, HEAD_SIZE)]
    all_gather x2 -> x0, waiting for transfers between devices: 104 us -> none  [the longest x1 70.3 us: local(): lax.all_gather(value_rows, 'ctx', axis=0, tiled=True)]
    dot_general x140 -> x0, matrix products: 94 us -> none  [the longest x40 34.8 us: products(): jnp.einsum('qgha,kga->ghqk', gradient_heads, value_head_rows, preferred_e...]
    dynamic_slice x112 -> x0, local copies, waits for them, and re-layouts: 90.8 us -> none  [the longest x32 30.6 us: tile_at(): lax.dynamic_slice_in_dim(value_every_slot, step * rows, rows)]
    another operation x66 -> x0, loops' own time: 89 us -> none  [the longest x1 42.5 us: local(): lax.fori_loop(0, cycle, grad_step, (grads_start, scale_start, whole, whole))]
    reduce_scatter x2 -> x0, waiting for transfers between devices: 64.1 us -> none  [the longest x1 64.1 us: local(): lax.psum_scatter(key_sums.astype(jnp.bfloat16), 'ctx', scatter_dimension=...]
    ppermute x0 -> x26, starting transfers between devices: none -> 58 us  [swap(): return lax.ppermute(array, axis, pairs)]
  transfers between devices with their start and end apart: 4 -> 26, of which waited for: 3 -> 15; matrix products, arithmetic and copies ran while one was open for 1% -> 1% of each run, Pallas kernels for 0% -> 22%
where the time goes in v1:
time: 157 us; the launch traced here: 155 us
  starting transfers between devices  58 us (37%)
  waiting for transfers between devices  46.3 us (29%)
  Pallas kernels  39.3 us (25%)
  local copies, waits for them, and re-layouts  9.31 us (6%)
    ppermute x26, starting transfers between devices, swap(): return lax.ppermute(array, axis, pairs)  58 us
    ppermute x26, waiting for transfers between devices, swap(): return lax.ppermute(array, axis, pairs)  46.3 us
    pallas_call x5, Pallas kernels, grads(): call(functools.partial(grads_body, count, prior is None, is_last), outs,...  23.3 us
    pallas_call x2, Pallas kernels, stats(): call(functools.partial(stats_body, count, prior is None, is_last), outs,...  14.6 us
    unnamed x26, local copies, waits for them, and re-layouts  8.69 us
  transfers between devices with their start and end apart: 26, of which 15 were waited for; matrix products, arithmetic and copies ran while one was open for 1% of the time, Pallas kernels for 22%

profile of v1, /device:TPU:38, one launch (start us, length us, event | category | flops | bytes accessed | tf_op | source)
XLA Modules:
  0.0 155.2 jit_solution(17948062676418766047)
XLA Ops:
  0.7 0.9 copy-done.3
  1.6 0.9 copy-done.4
  2.5 0.7 copy-done.5
  3.1 0.9 collective-permute-start
  4.1 4.6 %collective-permute-done = bf16[272,256]{1,0:T(8,128)(2,1)S(1)} collective-permute-done((bf16[272,256]{1,0:T(8,128)(2,1)S(1)}, bf16[272,256]{1,0:T(8,128)(2,1)S(1)}, u32[]{:S(2)}, u32[]{:S(2)}) %collective-permute-start) | collective-permute-done | bytes 139296 | tf_op jit(solution)/shard_map/ppermute | solution.py:398
  8.7 2.0 %collective-permute-start.5 = (bf16[2,272,256]{2,1,0:T(8,128)(2,1)S(1)}, bf16[2,272,256]{2,1,0:T(8,128)(2,1)S(1)}, u32[]{:S(2)}, u32[]{:S(2)}) collective-permute-start(bf16[2,272,256]{2,1,0:T(8,128)(2,1)S(1)} %pad_maximum_fusion.refs_1_.refs_4_.refs_5_), channel_id=1, source_target_pairs={{0,7},{1,2},{2,1},{3,4},{4,3},{5,6},{6,5},{7,0},{8,15},{9,10},{10,... | collective-permute-start | bytes 835592 | tf_op jit(solution)/shard_map/ppermute | solution.py:398
  10.7 1.2 copy-done.1
  11.9 1.2 copy-done.2
  13.0 0.3 shard_map.94
  13.4 0.9 collective-permute-start.1
  14.3 4.0 %collective-permute-start.2 = (bf16[2,272,256]{2,1,0:T(8,128)(2,1)S(1)}, bf16[2,272,256]{2,1,0:T(8,128)(2,1)}, u32[]{:S(2)}, u32[]{:S(2)}) collective-permute-start(bf16[2,272,256]{2,1,0:T(8,128)(2,1)S(1)} %pad_maximum_fusion.refs_1_.refs_4_.refs_5_), channel_id=1, source_target_pairs={{0,1},{1,0},{2,3},{3,2},{4,5},{5,4},{6,7},{7,6},{8,9},{9,8},{10,11... | collective-permute-start | bytes 835592 | tf_op jit(solution)/shard_map/ppermute | solution.py:398
  18.3 2.2 %collective-permute-start.6 = (bf16[2,272,256]{2,1,0:T(8,128)(2,1)S(1)}, bf16[2,272,256]{2,1,0:T(8,128)(2,1)}, u32[]{:S(2)}, u32[]{:S(2)}) collective-permute-start(bf16[2,272,256]{2,1,0:T(8,128)(2,1)S(1)} %collective-permute-done.5.refs_6_), channel_id=1, source_target_pairs={{0,1},{1,0},{2,3},{3,2},{4,5},{5,4},{6,7},{7,6},{8,9},{9,8},{10,11... | collective-permute-start | bytes 835592 | tf_op jit(solution)/shard_map/ppermute | solution.py:398
  20.5 5.5 %collective-permute-done.2.refs_5_ = bf16[2,272,256]{2,1,0:T(8,128)(2,1)} collective-permute-done((bf16[2,272,256]{2,1,0:T(8,128)(2,1)S(1)}, bf16[2,272,256]{2,1,0:T(8,128)(2,1)}, u32[]{:S(2)}, u32[]{:S(2)}) %collective-permute-start.2) | collective-permute-done | bytes 278560 | tf_op jit(solution)/shard_map/ppermute | solution.py:398
  26.0 1.0 collective-permute-start.3
  27.0 2.6 %collective-permute-done.6.refs_7_.refs_5_ = bf16[2,272,256]{2,1,0:T(8,128)(2,1)} collective-permute-done((bf16[2,272,256]{2,1,0:T(8,128)(2,1)S(1)}, bf16[2,272,256]{2,1,0:T(8,128)(2,1)}, u32[]{:S(2)}, u32[]{:S(2)}) %collective-permute-start.6) | collective-permute-done | bytes 278560 | tf_op jit(solution)/shard_map/ppermute | solution.py:398
  29.6 1.0 collective-permute-start.7
  30.6 0.1 dynamic-slice_multiply_fusion
  30.7 0.1 broadcast_in_dim.21
  30.8 4.7 %collective-permute-done.3.refs_8_.refs_6_ = bf16[2,272,256]{2,1,0:T(8,128)(2,1)} collective-permute-done((bf16[2,272,256]{2,1,0:T(8,128)(2,1)}, bf16[2,272,256]{2,1,0:T(8,128)(2,1)}, u32[]{:S(2)}, u32[]{:S(2)}) %collective-permute-start.3) | collective-permute-done | bytes 278560 | tf_op jit(solution)/shard_map/ppermute | solution.py:398
  35.5 3.4 %collective-permute-start.4 = (bf16[2,272,256]{2,1,0:T(8,128)(2,1)}, bf16[2,272,256]{2,1,0:T(8,128)(2,1)S(1)}, u32[]{:S(2)}, u32[]{:S(2)}) collective-permute-start(bf16[2,272,256]{2,1,0:T(8,128)(2,1)} %collective-permute-done.3.refs_8_.refs_6_), channel_id=1, source_target_pairs={{0,1},{1,0},{2,3},{3,2},{4,5},{5,4},{6,7},{7,6},{8,9},{9,8},{10,11... | collective-permute-start | bytes 835592 | tf_op jit(solution)/shard_map/ppermute | solution.py:398
  38.9 3.0 %collective-permute-start.8 = (bf16[2,272,256]{2,1,0:T(8,128)(2,1)}, bf16[2,272,256]{2,1,0:T(8,128)(2,1)S(1)}, u32[]{:S(2)}, u32[]{:S(2)}) collective-permute-start(bf16[2,272,256]{2,1,0:T(8,128)(2,1)} %collective-permute-done.7.refs_5_.refs_6_), channel_id=1, source_target_pairs={{0,1},{1,0},{2,3},{3,2},{4,5},{5,4},{6,7},{7,6},{8,9},{9,8},{10,11... | collective-permute-start | bytes 835592 | tf_op jit(solution)/shard_map/ppermute | solution.py:398
  41.9 0.1 broadcast_bitcast_fusion
  42.0 10.5 %shard_map.95.refs_7_ = f32[4,8,896]{2,1,0:T(8,128)S(1)} custom-call(f32[2,8,896]{2,1,0:T(8,128)S(1)} %broadcast_in_dim.24.refs_0_, bf16[2,272,256]{2,1,0:T(8,128)(2,1)S(1)} %pad_maximum_fusion.refs_1_.refs_4_.refs_5_, bf16[2,1792,128]{2,1,0:T(8,128)(2,1)S(1)} %get-tuple-element.26.refs_2_, bf16[2,1792,128]{2,1,0:T(8,128)(2,1)S(1)} %collective-permute-done.1.refs_3_, ...), custom_call_target="tpu_custom_call" | custom-call | flops 2348810240 | bytes 4194304 | tf_op jit(solution)/shard_map/pallas_call | solution.py:346
  52.5 4.1 %shard_map.96 = (f32[4,8,896]{2,1,0:T(8,128)S(1)}, f32[8,128]{1,0:T(8,128)S(1)}) custom-call(f32[2,8,896]{2,1,0:T(8,128)S(1)} %broadcast_in_dim.24.refs_0_, bf16[2,272,256]{2,1,0:T(8,128)(2,1)S(1)} %pad_maximum_fusion.refs_1_.refs_4_.refs_5_, bf16[2,1792,128]{2,1,0:T(8,128)(2,1)S(1)} %get-tuple-element.26.refs_2_, ...), custom_call_target="tpu_custom_call" | custom-call | flops 1409286144 | bytes 4194304 | tf_op jit(solution)/shard_map/pallas_call | solution.py:346
  56.6 1.8 %shard_map.97 = (f32[2,256,256]{2,1,0:T(8,128)S(1)}, f32[4,128,896]{2,1,0:T(8,128)S(1)}) custom-call(f32[2,8,896]{2,1,0:T(8,128)S(1)} %broadcast_in_dim.24.refs_0_, bf16[2,272,256]{2,1,0:T(8,128)(2,1)S(1)} %pad_maximum_fusion.refs_1_.refs_4_.refs_5_, bf16[2,1792,128]{2,1,0:T(8,128)(2,1)S(1)} %get-tuple-element.26.refs_2_, ...), custom_call_target="tpu_custom_call" | custom-call | flops 1174405120 | bytes 6291456 | tf_op jit(solution)/shard_map/pallas_call | solution.py:372
  58.4 1.3 copy-done.9
  59.7 0.1 collective-permute-start.13
  59.8 3.7 %shard_map.98 = (f32[2,256,256]{2,1,0:T(8,128)S(1)}, f32[2,256,256]{2,1,0:T(8,128)S(1)}, f32[4,128,896]{2,1,0:T(8,128)S(1)}) custom-call(f32[2,8,896]{2,1,0:T(8,128)S(1)} %broadcast_in_dim.24.refs_0_, bf16[2,272,256]{2,1,0:T(8,128)(2,1)S(1)} %pad_maximum_fusion.refs_1_.refs_4_.refs_5_, bf16[2,1792,128]{2,1,0:T(8,128)(2,1)S(1)} %get-tuple-element.26.refs_2_, ...), custom_call_target="tpu_custom_call" | custom-call | flops 2348810240 | bytes 6291456 | tf_op jit(solution)/shard_map/pallas_call | solution.py:372
  63.5 1.3 copy-done.10
  64.8 2.3 %collective-permute-start.10 = (bf16[2,256,256]{2,1,0:T(8,128)(2,1)S(1)}, bf16[2,256,256]{2,1,0:T(8,128)(2,1)S(1)}, u32[]{:S(2)}, u32[]{:S(2)}) collective-permute-start(bf16[2,256,256]{2,1,0:T(8,128)(2,1)S(1)} %convert_element_type.45), channel_id=1, source_target_pairs={{0,1},{1,0},{2,3},{3,2},{4,5},{5,4},{6,7},{7,6},{8,9},{9,8},{10,11... | collective-permute-start | bytes 786440 | tf_op jit(solution)/shard_map/ppermute | solution.py:398
  67.1 5.0 %shard_map.99 = (f32[2,256,256]{2,1,0:T(8,128)S(1)}, f32[2,256,256]{2,1,0:T(8,128)S(1)}, f32[4,128,896]{2,1,0:T(8,128)S(1)}) custom-call(f32[2,8,896]{2,1,0:T(8,128)S(1)} %broadcast_in_dim.24.refs_0_, bf16[2,272,256]{2,1,0:T(8,128)(2,1)S(1)} %pad_maximum_fusion.refs_1_.refs_4_.refs_5_, bf16[2,1792,128]{2,1,0:T(8,128)(2,1)S(1)} %get-tuple-element.26.refs_2_, ...), custom_call_target="tpu_custom_call" | custom-call | flops 2348810240 | bytes 6291456 | tf_op jit(solution)/shard_map/pallas_call | solution.py:372
  72.1 1.3 copy-done
  73.4 7.4 %collective-permute-start.14 = (bf16[2,256,256]{2,1,0:T(8,128)(2,1)S(1)}, bf16[2,256,256]{2,1,0:T(8,128)(2,1)S(1)}, u32[]{:S(2)}, u32[]{:S(2)}) collective-permute-start(bf16[2,256,256]{2,1,0:T(8,128)(2,1)S(1)} %add_convert_fusion.3), channel_id=1, source_target_pairs={{0,7},{1,2},{2,1},{3,4},{4,3},{5,6},{6,5},{7,0},{8,15},{9,10},{10,... | collective-permute-start | bytes 786440 | tf_op jit(solution)/shard_map/ppermute | solution.py:398
  80.8 5.5 %shard_map.100 = (f32[2,256,256]{2,1,0:T(8,128)S(1)}, f32[4,128,896]{2,1,0:T(8,128)S(1)}) custom-call(f32[2,8,896]{2,1,0:T(8,128)S(1)} %broadcast_in_dim.24.refs_0_, bf16[2,272,256]{2,1,0:T(8,128)(2,1)S(1)} %pad_maximum_fusion.refs_1_.refs_4_.refs_5_, bf16[2,1792,128]{2,1,0:T(8,128)(2,1)S(1)} %get-tuple-element.26.refs_2_, ...), custom_call_target="tpu_custom_call" | custom-call | flops 1174405120 | bytes 6291456 | tf_op jit(solution)/shard_map/pallas_call | solution.py:372
  86.5 0.1 collective-permute-start.11
  86.6 0.5 collective-permute-done.14
  87.1 0.1 add_convert_fusion.2
  87.1 11.5 %collective-permute-start.15 = (bf16[2,256,256]{2,1,0:T(8,128)(2,1)S(1)}, bf16[2,256,256]{2,1,0:T(8,128)(2,1)S(1)}, u32[]{:S(2)}, u32[]{:S(2)}) collective-permute-start(bf16[2,256,256]{2,1,0:T(8,128)(2,1)S(1)} %add_convert_fusion.2), channel_id=1, source_target_pairs={{0,1},{1,0},{2,3},{3,2},{4,5},{5,4},{6,7},{7,6},{8,9},{9,8},{10,11... | collective-permute-start | bytes 786440 | tf_op jit(solution)/shard_map/ppermute | solution.py:398
  98.6 7.4 %shard_map.101 = (f32[2,256,256]{2,1,0:T(8,128)S(1)}, f32[2,256,256]{2,1,0:T(8,128)S(1)}, bf16[1792,128]{1,0:T(8,128)(2,1)S(1)}, bf16[1792,128]{1,0:T(8,128)(2,1)S(1)}) custom-call(f32[2,8,896]{2,1,0:T(8,128)S(1)} %broadcast_in_dim.24.refs_0_, bf16[2,272,256]{2,1,0:T(8,128)(2,1)S(1)} %pad_maximum_fusion.refs_1_.refs_4_.refs_5_, ...), custom_call_target="tpu_custom_call" | custom-call | flops 2348810240 | bytes 6291456 | tf_op jit(solution)/shard_map/pallas_call | solution.py:372
  106.1 1.9 %collective-permute-start.12 = (bf16[2,256,256]{2,1,0:T(8,128)(2,1)S(1)}, bf16[2,256,256]{2,1,0:T(8,128)(2,1)S(1)}, u32[]{:S(2)}, u32[]{:S(2)}) collective-permute-start(bf16[2,256,256]{2,1,0:T(8,128)(2,1)S(1)} %add_convert_fusion.4), channel_id=1, source_target_pairs={{0,1},{1,0},{2,3},{3,2},{4,5},{5,4},{6,7},{7,6},{8,9},{9,8},{10,11... | collective-permute-start | bytes 786440 | tf_op jit(solution)/shard_map/ppermute | solution.py:398
  108.0 0.1 add_convert_fusion.1
  108.1 0.1 collective-permute-start.16
  108.2 3.0 %collective-permute-start.18 = (f32[8,128]{1,0:T(8,128)S(1)}, f32[8,128]{1,0:T(8,128)S(1)}, u32[]{:S(2)}, u32[]{:S(2)}) collective-permute-start(f32[8,128]{1,0:T(8,128)S(1)} %get-tuple-element.43), channel_id=1, source_target_pairs={{0,1},{1,0},{2,3},{3,2},{4,5},{5,4},{6,7},{7,6},{8,9},{9,8},{10,11... | collective-permute-start | bytes 12296 | tf_op jit(solution)/shard_map/ppermute | solution.py:398
  111.2 1.6 %collective-permute-done.18 = f32[8,128]{1,0:T(8,128)S(1)} collective-permute-done((f32[8,128]{1,0:T(8,128)S(1)}, f32[8,128]{1,0:T(8,128)S(1)}, u32[]{:S(2)}, u32[]{:S(2)}) %collective-permute-start.18) | collective-permute-done | bytes 4128 | tf_op jit(solution)/shard_map/ppermute | solution.py:398
  112.8 0.8 collective-permute-start.19
  113.6 3.7 %collective-permute-done.19 = f32[8,128]{1,0:T(8,128)S(1)} collective-permute-done((f32[8,128]{1,0:T(8,128)S(1)}, f32[8,128]{1,0:T(8,128)S(1)}, u32[]{:S(2)}, u32[]{:S(2)}) %collective-permute-start.19) | collective-permute-done | bytes 4128 | tf_op jit(solution)/shard_map/ppermute | solution.py:398
  117.3 4.2 %collective-permute-start.20 = (f32[8,128]{1,0:T(8,128)S(1)}, f32[8,128]{1,0:T(8,128)S(1)}, u32[]{:S(2)}, u32[]{:S(2)}) collective-permute-start(f32[8,128]{1,0:T(8,128)S(1)} %add.58), channel_id=1, source_target_pairs={{0,4},{1,5},{2,6},{3,7},{4,0},{5,1},{6,2},{7,3},{8,12},{9,13},{10,... | collective-permute-start | bytes 12296 | tf_op jit(solution)/shard_map/ppermute | solution.py:398
  121.5 3.3 %collective-permute-done.20 = f32[8,128]{1,0:T(8,128)S(1)} collective-permute-done((f32[8,128]{1,0:T(8,128)S(1)}, f32[8,128]{1,0:T(8,128)S(1)}, u32[]{:S(2)}, u32[]{:S(2)}) %collective-permute-start.20) | collective-permute-done | bytes 4128 | tf_op jit(solution)/shard_map/ppermute | solution.py:398
  124.8 1.5 collective-permute-start.21
  126.3 2.1 %collective-permute-done.21 = f32[8,128]{1,0:T(8,128)S(1)} collective-permute-done((f32[8,128]{1,0:T(8,128)S(1)}, f32[8,128]{1,0:T(8,128)S(1)}, u32[]{:S(2)}, u32[]{:S(2)}) %collective-permute-start.21) | collective-permute-done | bytes 4128 | tf_op jit(solution)/shard_map/ppermute | solution.py:398
  128.4 1.2 collective-permute-done.22
  129.6 1.0 collective-permute-start.23
  130.6 4.1 %collective-permute-done.23 = f32[8,128]{1,0:T(8,128)S(1)} collective-permute-done((f32[8,128]{1,0:T(8,128)S(1)}, f32[8,128]{1,0:T(8,128)S(1)}, u32[]{:S(2)}, u32[]{:S(2)}) %collective-permute-start.23) | collective-permute-done | bytes 4128 | tf_op jit(solution)/shard_map/ppermute | solution.py:398
  134.7 3.6 %collective-permute-done.24 = f32[8,128]{1,0:T(8,128)S(1)} collective-permute-done((f32[8,128]{1,0:T(8,128)S(1)}, f32[8,128]{1,0:T(8,128)S(1)}, u32[]{:S(2)}, u32[]{:S(2)}) %collective-permute-start.24) | collective-permute-done | bytes 4128 | tf_op jit(solution)/shard_map/ppermute | solution.py:398
  138.3 3.3 %collective-permute-start.25 = (f32[8,128]{1,0:T(8,128)S(1)}, f32[8,128]{1,0:T(8,128)S(1)}, u32[]{:S(2)}, u32[]{:S(2)}) collective-permute-start(f32[8,128]{1,0:T(8,128)S(1)} %add.63), channel_id=1, source_target_pairs={{0,128},{16,144},{32,160},{48,176},{64,192},{80,208},{96,224},{112... | collective-permute-start | bytes 12296 | tf_op jit(solution)/shard_map/ppermute | solution.py:398
  141.6 0.9 collective-permute-start.9
  142.5 0.9 collective-permute-done.25
  143.4 0.1 add_convert_fusion
  143.6 1.5 collective-permute-start.17
  145.1 0.5 slice_bitcast_fusion.2
  145.6 7.5 %collective-permute-done.9.got_ref = bf16[1792,128]{1,0:T(8,128)(2,1)S(1)} collective-permute-done((bf16[1792,128]{1,0:T(8,128)(2,1)S(1)}, bf16[1792,128]{1,0:T(8,128)(2,1)S(1)}, u32[]{:S(2)}, u32[]{:S(2)}) %collective-permute-start.9) | collective-permute-done | bytes 458784 | tf_op jit(solution)/shard_map/ppermute | solution.py:398
  153.1 1.1 shard_map.102
  154.2 0.3 collective-permute-done.17
  154.5 0.7 fusion.2
  (48 shorter events, 0.4 us)
Async XLA Ops:
  0.6 30.0 %copy-start.11 = (f32[28]{0:T(128)S(1)}, f32[28]{0:T(128)}, u32[]{:S(2)}) copy-start(f32[28]{0:T(128)} %param.11) | copy-start | bytes 340
  0.7 0.9 copy-start.3
  1.6 0.9 copy-start.4
  2.5 0.7 copy-start.5
  3.1 5.5 %collective-permute-start = (bf16[272,256]{1,0:T(8,128)(2,1)S(1)}, bf16[272,256]{1,0:T(8,128)(2,1)S(1)}, u32[]{:S(2)}, u32[]{:S(2)}) collective-permute-start(bf16[272,256]{1,0:T(8,128)(2,1)S(1)} %get-tuple-element.25), channel_id=1, source_target_pairs={{0,8},{1,9},{2,10},{3,11},{4,12},{5,13},{6,14},{7,15},{8,0},{9,1},... | collective-permute-start | bytes 417800 | tf_op jit(solution)/shard_map/ppermute | solution.py:398
  8.7 9.7 %collective-permute-start.5 = (bf16[2,272,256]{2,1,0:T(8,128)(2,1)S(1)}, bf16[2,272,256]{2,1,0:T(8,128)(2,1)S(1)}, u32[]{:S(2)}, u32[]{:S(2)}) collective-permute-start(bf16[2,272,256]{2,1,0:T(8,128)(2,1)S(1)} %pad_maximum_fusion.refs_1_.refs_4_.refs_5_), channel_id=1, source_target_pairs={{0,7},{1,2},{2,1},{3,4},{4,3},{5,6},{6,5},{7,0},{8,15},{9,10},{10,... | collective-permute-start | bytes 835592 | tf_op jit(solution)/shard_map/ppermute | solution.py:398
  10.7 1.2 copy-start.1
  11.9 1.2 copy-start.2
  13.4 28.6 %collective-permute-start.1 = (bf16[2,1792,128]{2,1,0:T(8,128)(2,1)S(1)}, bf16[2,1792,128]{2,1,0:T(8,128)(2,1)S(1)}, u32[]{:S(2)}, u32[]{:S(2)}) collective-permute-start(bf16[2,1792,128]{2,1,0:T(8,128)(2,1)S(1)} %get-tuple-element.27), channel_id=1, source_target_pairs={{0,8},{1,9},{2,10},{3,11},{4,12},{5,13},{6,14},{7,15},{8,0},{9,1},... | collective-permute-start | bytes 2752520 | tf_op jit(solution)/shard_map/ppermute | solution.py:398
  14.3 11.7 %collective-permute-start.2 = (bf16[2,272,256]{2,1,0:T(8,128)(2,1)S(1)}, bf16[2,272,256]{2,1,0:T(8,128)(2,1)}, u32[]{:S(2)}, u32[]{:S(2)}) collective-permute-start(bf16[2,272,256]{2,1,0:T(8,128)(2,1)S(1)} %pad_maximum_fusion.refs_1_.refs_4_.refs_5_), channel_id=1, source_target_pairs={{0,1},{1,0},{2,3},{3,2},{4,5},{5,4},{6,7},{7,6},{8,9},{9,8},{10,11... | collective-permute-start | bytes 835592 | tf_op jit(solution)/shard_map/ppermute | solution.py:398
  18.3 34.2 %copy-start.7 = (bf16[2,272,256]{2,1,0:T(8,128)(2,1)}, bf16[2,272,256]{2,1,0:T(8,128)(2,1)S(1)}, u32[]{:S(2)}) copy-start(bf16[2,272,256]{2,1,0:T(8,128)(2,1)S(1)} %collective-permute-done.5.refs_6_) | copy-start | bytes 835588
  18.3 11.3 %collective-permute-start.6 = (bf16[2,272,256]{2,1,0:T(8,128)(2,1)S(1)}, bf16[2,272,256]{2,1,0:T(8,128)(2,1)}, u32[]{:S(2)}, u32[]{:S(2)}) collective-permute-start(bf16[2,272,256]{2,1,0:T(8,128)(2,1)S(1)} %collective-permute-done.5.refs_6_), channel_id=1, source_target_pairs={{0,1},{1,0},{2,3},{3,2},{4,5},{5,4},{6,7},{7,6},{8,9},{9,8},{10,11... | collective-permute-start | bytes 835592 | tf_op jit(solution)/shard_map/ppermute | solution.py:398
  26.0 9.5 %collective-permute-start.3 = (bf16[2,272,256]{2,1,0:T(8,128)(2,1)}, bf16[2,272,256]{2,1,0:T(8,128)(2,1)}, u32[]{:S(2)}, u32[]{:S(2)}) collective-permute-start(bf16[2,272,256]{2,1,0:T(8,128)(2,1)} %collective-permute-done.2.refs_5_), channel_id=1, source_target_pairs={{0,7},{1,2},{2,1},{3,4},{4,3},{5,6},{6,5},{7,0},{8,15},{9,10},{10,... | collective-permute-start | bytes 835592 | tf_op jit(solution)/shard_map/ppermute | solution.py:398
  29.6 9.3 %collective-permute-start.7 = (bf16[2,272,256]{2,1,0:T(8,128)(2,1)}, bf16[2,272,256]{2,1,0:T(8,128)(2,1)}, u32[]{:S(2)}, u32[]{:S(2)}) collective-permute-start(bf16[2,272,256]{2,1,0:T(8,128)(2,1)} %collective-permute-done.6.refs_7_.refs_5_), channel_id=1, source_target_pairs={{0,7},{1,2},{2,1},{3,4},{4,3},{5,6},{6,5},{7,0},{8,15},{9,10},{10,... | collective-permute-start | bytes 835592 | tf_op jit(solution)/shard_map/ppermute | solution.py:398
  35.5 17.0 %collective-permute-start.4 = (bf16[2,272,256]{2,1,0:T(8,128)(2,1)}, bf16[2,272,256]{2,1,0:T(8,128)(2,1)S(1)}, u32[]{:S(2)}, u32[]{:S(2)}) collective-permute-start(bf16[2,272,256]{2,1,0:T(8,128)(2,1)} %collective-permute-done.3.refs_8_.refs_6_), channel_id=1, source_target_pairs={{0,1},{1,0},{2,3},{3,2},{4,5},{5,4},{6,7},{7,6},{8,9},{9,8},{10,11... | collective-permute-start | bytes 835592 | tf_op jit(solution)/shard_map/ppermute | solution.py:398
  38.9 13.6 %collective-permute-start.8 = (bf16[2,272,256]{2,1,0:T(8,128)(2,1)}, bf16[2,272,256]{2,1,0:T(8,128)(2,1)S(1)}, u32[]{:S(2)}, u32[]{:S(2)}) collective-permute-start(bf16[2,272,256]{2,1,0:T(8,128)(2,1)} %collective-permute-done.7.refs_5_.refs_6_), channel_id=1, source_target_pairs={{0,1},{1,0},{2,3},{3,2},{4,5},{5,4},{6,7},{7,6},{8,9},{9,8},{10,11... | collective-permute-start | bytes 835592 | tf_op jit(solution)/shard_map/ppermute | solution.py:398
  58.4 1.3 copy-start.9
  59.7 13.6 %collective-permute-start.13 = (bf16[2,256,256]{2,1,0:T(8,128)(2,1)S(1)}, bf16[2,256,256]{2,1,0:T(8,128)(2,1)S(1)}, u32[]{:S(2)}, u32[]{:S(2)}) collective-permute-start(bf16[2,256,256]{2,1,0:T(8,128)(2,1)S(1)} %convert_element_type.51), channel_id=1, source_target_pairs={{0,1},{1,0},{2,3},{3,2},{4,5},{5,4},{6,7},{7,6},{8,9},{9,8},{10,11... | collective-permute-start | bytes 786440 | tf_op jit(solution)/shard_map/ppermute | solution.py:398
  63.5 1.3 copy-start.10
  64.8 21.5 %collective-permute-start.10 = (bf16[2,256,256]{2,1,0:T(8,128)(2,1)S(1)}, bf16[2,256,256]{2,1,0:T(8,128)(2,1)S(1)}, u32[]{:S(2)}, u32[]{:S(2)}) collective-permute-start(bf16[2,256,256]{2,1,0:T(8,128)(2,1)S(1)} %convert_element_type.45), channel_id=1, source_target_pairs={{0,1},{1,0},{2,3},{3,2},{4,5},{5,4},{6,7},{7,6},{8,9},{9,8},{10,11... | collective-permute-start | bytes 786440 | tf_op jit(solution)/shard_map/ppermute | solution.py:398
  72.1 1.3 copy-start
  73.4 13.7 %collective-permute-start.14 = (bf16[2,256,256]{2,1,0:T(8,128)(2,1)S(1)}, bf16[2,256,256]{2,1,0:T(8,128)(2,1)S(1)}, u32[]{:S(2)}, u32[]{:S(2)}) collective-permute-start(bf16[2,256,256]{2,1,0:T(8,128)(2,1)S(1)} %add_convert_fusion.3), channel_id=1, source_target_pairs={{0,7},{1,2},{2,1},{3,4},{4,3},{5,6},{6,5},{7,0},{8,15},{9,10},{10,... | collective-permute-start | bytes 786440 | tf_op jit(solution)/shard_map/ppermute | solution.py:398
  86.4 12.3 %copy-start.6 = (f32[4,128,896]{2,1,0:T(8,128)}, f32[4,128,896]{2,1,0:T(8,128)S(1)}, u32[]{:S(2)}) copy-start(f32[4,128,896]{2,1,0:T(8,128)S(1)} %get-tuple-element.32.refs_7_) | copy-start | bytes 5505028
  86.4 12.3 %copy-start.8 = (bf16[2,272,256]{2,1,0:T(8,128)(2,1)S(1)}, bf16[2,272,256]{2,1,0:T(8,128)(2,1)}, u32[]{:S(2)}) copy-start(bf16[2,272,256]{2,1,0:T(8,128)(2,1)} %copy-done.7) | copy-start | bytes 835588
  86.5 19.6 %collective-permute-start.11 = (bf16[2,256,256]{2,1,0:T(8,128)(2,1)S(1)}, bf16[2,256,256]{2,1,0:T(8,128)(2,1)S(1)}, u32[]{:S(2)}, u32[]{:S(2)}) collective-permute-start(bf16[2,256,256]{2,1,0:T(8,128)(2,1)S(1)} %add_convert_fusion.5), channel_id=1, source_target_pairs={{0,7},{1,2},{2,1},{3,4},{4,3},{5,6},{6,5},{7,0},{8,15},{9,10},{10,... | collective-permute-start | bytes 786440 | tf_op jit(solution)/shard_map/ppermute | solution.py:398
  87.1 20.9 %collective-permute-start.15 = (bf16[2,256,256]{2,1,0:T(8,128)(2,1)S(1)}, bf16[2,256,256]{2,1,0:T(8,128)(2,1)S(1)}, u32[]{:S(2)}, u32[]{:S(2)}) collective-permute-start(bf16[2,256,256]{2,1,0:T(8,128)(2,1)S(1)} %add_convert_fusion.2), channel_id=1, source_target_pairs={{0,1},{1,0},{2,3},{3,2},{4,5},{5,4},{6,7},{7,6},{8,9},{9,8},{10,11... | collective-permute-start | bytes 786440 | tf_op jit(solution)/shard_map/ppermute | solution.py:398
  106.1 37.3 %collective-permute-start.12 = (bf16[2,256,256]{2,1,0:T(8,128)(2,1)S(1)}, bf16[2,256,256]{2,1,0:T(8,128)(2,1)S(1)}, u32[]{:S(2)}, u32[]{:S(2)}) collective-permute-start(bf16[2,256,256]{2,1,0:T(8,128)(2,1)S(1)} %add_convert_fusion.4), channel_id=1, source_target_pairs={{0,1},{1,0},{2,3},{3,2},{4,5},{5,4},{6,7},{7,6},{8,9},{9,8},{10,11... | collective-permute-start | bytes 786440 | tf_op jit(solution)/shard_map/ppermute | solution.py:398
  108.1 35.4 %collective-permute-start.16 = (bf16[2,256,256]{2,1,0:T(8,128)(2,1)S(1)}, bf16[2,256,256]{2,1,0:T(8,128)(2,1)S(1)}, u32[]{:S(2)}, u32[]{:S(2)}) collective-permute-start(bf16[2,256,256]{2,1,0:T(8,128)(2,1)S(1)} %add_convert_fusion.1), channel_id=1, source_target_pairs={{0,7},{1,2},{2,1},{3,4},{4,3},{5,6},{6,5},{7,0},{8,15},{9,10},{10,... | collective-permute-start | bytes 786440 | tf_op jit(solution)/shard_map/ppermute | solution.py:398
  108.2 4.6 %collective-permute-start.18 = (f32[8,128]{1,0:T(8,128)S(1)}, f32[8,128]{1,0:T(8,128)S(1)}, u32[]{:S(2)}, u32[]{:S(2)}) collective-permute-start(f32[8,128]{1,0:T(8,128)S(1)} %get-tuple-element.43), channel_id=1, source_target_pairs={{0,1},{1,0},{2,3},{3,2},{4,5},{5,4},{6,7},{7,6},{8,9},{9,8},{10,11... | collective-permute-start | bytes 12296 | tf_op jit(solution)/shard_map/ppermute | solution.py:398
  112.8 4.5 %collective-permute-start.19 = (f32[8,128]{1,0:T(8,128)S(1)}, f32[8,128]{1,0:T(8,128)S(1)}, u32[]{:S(2)}, u32[]{:S(2)}) collective-permute-start(f32[8,128]{1,0:T(8,128)S(1)} %add.57), channel_id=1, source_target_pairs={{0,2},{1,3},{2,0},{3,1},{4,6},{5,7},{6,4},{7,5},{8,10},{9,11},{10,... | collective-permute-start | bytes 12296 | tf_op jit(solution)/shard_map/ppermute | solution.py:398
  117.3 7.5 %collective-permute-start.20 = (f32[8,128]{1,0:T(8,128)S(1)}, f32[8,128]{1,0:T(8,128)S(1)}, u32[]{:S(2)}, u32[]{:S(2)}) collective-permute-start(f32[8,128]{1,0:T(8,128)S(1)} %add.58), channel_id=1, source_target_pairs={{0,4},{1,5},{2,6},{3,7},{4,0},{5,1},{6,2},{7,3},{8,12},{9,13},{10,... | collective-permute-start | bytes 12296 | tf_op jit(solution)/shard_map/ppermute | solution.py:398
  124.8 3.6 %collective-permute-start.21 = (f32[8,128]{1,0:T(8,128)S(1)}, f32[8,128]{1,0:T(8,128)S(1)}, u32[]{:S(2)}, u32[]{:S(2)}) collective-permute-start(f32[8,128]{1,0:T(8,128)S(1)} %add.59), channel_id=1, source_target_pairs={{0,8},{1,9},{2,10},{3,11},{4,12},{5,13},{6,14},{7,15},{8,0},{9,1},... | collective-permute-start | bytes 12296 | tf_op jit(solution)/shard_map/ppermute | solution.py:398
  128.4 1.2 collective-permute-start.22
  129.6 5.1 %collective-permute-start.23 = (f32[8,128]{1,0:T(8,128)S(1)}, f32[8,128]{1,0:T(8,128)S(1)}, u32[]{:S(2)}, u32[]{:S(2)}) collective-permute-start(f32[8,128]{1,0:T(8,128)S(1)} %add.61), channel_id=1, source_target_pairs={{0,32},{16,48},{32,0},{48,16},{64,96},{80,112},{96,64},{112,80},{1... | collective-permute-start | bytes 12296 | tf_op jit(solution)/shard_map/ppermute | solution.py:398
  134.7 3.6 %collective-permute-start.24 = (f32[8,128]{1,0:T(8,128)S(1)}, f32[8,128]{1,0:T(8,128)S(1)}, u32[]{:S(2)}, u32[]{:S(2)}) collective-permute-start(f32[8,128]{1,0:T(8,128)S(1)} %add.62), channel_id=1, source_target_pairs={{0,64},{16,80},{32,96},{48,112},{64,0},{80,16},{96,32},{112,48},{1... | collective-permute-start | bytes 12296 | tf_op jit(solution)/shard_map/ppermute | solution.py:398
  138.3 5.1 %collective-permute-start.25 = (f32[8,128]{1,0:T(8,128)S(1)}, f32[8,128]{1,0:T(8,128)S(1)}, u32[]{:S(2)}, u32[]{:S(2)}) collective-permute-start(f32[8,128]{1,0:T(8,128)S(1)} %add.63), channel_id=1, source_target_pairs={{0,128},{16,144},{32,160},{48,176},{64,192},{80,208},{96,224},{112... | collective-permute-start | bytes 12296 | tf_op jit(solution)/shard_map/ppermute | solution.py:398
  141.6 11.4 %collective-permute-start.9 = (bf16[1792,128]{1,0:T(8,128)(2,1)S(1)}, bf16[1792,128]{1,0:T(8,128)(2,1)S(1)}, u32[]{:S(2)}, u32[]{:S(2)}) collective-permute-start(bf16[1792,128]{1,0:T(8,128)(2,1)S(1)} %get-tuple-element.34), channel_id=1, source_target_pairs={{0,8},{1,9},{2,10},{3,11},{4,12},{5,13},{6,14},{7,15},{8,0},{9,1},... | collective-permute-start | bytes 1376264 | tf_op jit(solution)/shard_map/ppermute | solution.py:398
  143.6 10.9 %collective-permute-start.17 = (bf16[256,256]{1,0:T(8,128)(2,1)S(1)}, bf16[256,256]{1,0:T(8,128)(2,1)S(1)}, u32[]{:S(2)}, u32[]{:S(2)}) collective-permute-start(bf16[256,256]{1,0:T(8,128)(2,1)S(1)} %slice_bitcast_fusion), channel_id=1, source_target_pairs={{0,8},{1,9},{2,10},{3,11},{4,12},{5,13},{6,14},{7,15},{8,0},{9,1},... | collective-permute-start | bytes 393224 | tf_op jit(solution)/shard_map/ppermute | solution.py:398

commit v2 on v1

v2 whole, which is shorter than its diff:
```python
import functools
import math

import jax
import jax.numpy as jnp
from jax import lax
from jax.experimental import pallas as pl
from jax.experimental.pallas import tpu as pltpu
from jax.sharding import PartitionSpec as P

F32 = jnp.float32
BF16 = jnp.bfloat16
HEAD = 128
ROWS = 128
KV_HEADS = 2
GROUP = 7
HEADS = KV_HEADS * GROUP
WIDE = GROUP * ROWS
POS = 16
MESSAGE = POS + 2 * ROWS
TILE = 128
FAR = 32768.0
LOW = -1e30
LOG2E = 1.4426950408889634
NT = (((1,), (1,)), ((), ()))
NN = (((1,), (0,)), ((), ()))
TN = (((0,), (0,)), ((), ()))


def product(a, b, dims):
    return lax.dot_general(a, b, dims, preferred_element_type=F32)


def call(body, outs, scratch, flops, moved, operands):
    return pl.pallas_call(
        body,
        out_shape=outs,
        in_specs=operands,
        scratch_shapes=scratch,
        cost_estimate=pl.CostEstimate(
            flops=flops, bytes_accessed=moved, transcendentals=flops // 1024
        ),
        compiler_params=pltpu.CompilerParams(vmem_limit_bytes=20 * 1024 * 1024),
    )


def fetch(sources, targets, sem):
    copies = [
        pltpu.make_async_copy(source, target, sem.at[n])
        for n, (source, target) in enumerate(zip(sources, targets))
    ]
    for copy in copies:
        copy.start()
    for copy in copies:
        copy.wait()


def pack_keys_body(x_ref, key_in, value_in, pos_in, keep_ref, send_ref, key_ref, value_ref, pos_ref, sem):
    x = x_ref[0]
    fetch((key_in, value_in, pos_in), (key_ref, value_ref, pos_ref), sem)
    pos = pos_ref[...]
    dead = pos < 0
    high = jnp.where(dead, 256, pos >> 7)
    low = jnp.where(dead, 0, pos & 127)
    row = jnp.concatenate([high, low], axis=1).astype(F32)
    rows = jnp.broadcast_to(row, (POS, 2 * ROWS)).astype(BF16)
    for ref, half in ((keep_ref, x), (send_ref, 1 - x)):
        at = pl.multiple_of(half * KV_HEADS * HEAD, KV_HEADS * HEAD)
        ref[0:POS, :] = rows
        ref[POS : POS + ROWS, :] = key_ref[:, pl.ds(at, KV_HEADS * HEAD)]
        ref[POS + ROWS : MESSAGE, :] = value_ref[:, pl.ds(at, KV_HEADS * HEAD)]


def pack_queries_body(x_ref, after_ref, query_in, grad_in, keep_ref, send_ref, query_ref, grad_ref, sem):
    x = x_ref[0]
    fetch((query_in, grad_in), (query_ref, grad_ref), sem)
    for ref, half in ((send_ref, 1 - x), (keep_ref, x)):
        for number, source in enumerate((query_ref, grad_ref)):
            for head in range(HEADS):
                at = pl.multiple_of(half * HEADS * HEAD + head * HEAD, HEAD)
                ref[number, head * ROWS : (head + 1) * ROWS, :] = source[:, pl.ds(at, HEAD)]


def join_body(after_ref, keep_ref, got_ref, out_ref):
    out_ref[0] = keep_ref[...]
    out_ref[1] = got_ref[...]


def finish_body(count, x_ref, keep_ref, got_ref, own_ref, other_ref, *refs):
    scale_refs = refs[:count]
    query_out, key_out, value_out, scale_out = refs[count:]
    x = x_ref[0]
    scale = sum([ref[0:1, :] for ref in scale_refs[1:]], scale_refs[0][0:1, :])
    scale_out[...] = scale[:, : 2 * HEADS]
    for ref, half in ((own_ref, x), (other_ref, 1 - x)):
        at = pl.multiple_of(half * KV_HEADS * HEAD, KV_HEADS * HEAD)
        key_out[:, pl.ds(at, KV_HEADS * HEAD)] = ref[:ROWS, :]
        value_out[:, pl.ds(at, KV_HEADS * HEAD)] = ref[ROWS:, :]
    for ref, half in ((keep_ref, x), (got_ref, 1 - x)):
        for head in range(HEADS):
            at = pl.multiple_of(half * HEADS * HEAD + head * HEAD, HEAD)
            query_out[:, pl.ds(at, HEAD)] = ref[head * ROWS : (head + 1) * ROWS, :]


def positions(ref, slot):
    row = ref[slot, 0:POS, :].astype(F32)[0:1, :]
    return row[:, :ROWS] * 128.0 + row[:, ROWS:]


def query_side(own_ref):
    rows = [positions(own_ref, slot) for slot in range(2)]
    rows = [jnp.where(row >= FAR, -1.0, row) for row in rows]
    tops = [jnp.max(row) for row in rows]
    first = jnp.where(tops[0] < tops[1], 0, 1)
    return rows, tops, first


def place(blocks, first, top, key_c, value_c, pos_c, turned):
    start = jnp.int32(0)
    entries = []
    for phase in range(2):
        slot = first if phase == 0 else 1 - first
        rows = [positions(ref, slot) for ref in blocks]
        begins = [jnp.min(row) for row in rows]
        counts = [jnp.sum(jnp.where(row < FAR, 1.0, 0.0)).astype(jnp.int32) for row in rows]
        counts = [jnp.where(begin <= top, n, 0) for begin, n in zip(begins, counts)]
        spans = [(n + 15) >> 4 for n in counts]
        if len(blocks) == 2:
            ahead = begins[0] < begins[1]
            starts = [
                start + jnp.where(ahead, 0, spans[1] * 16),
                start + jnp.where(ahead, spans[0] * 16, 0),
            ]
        else:
            starts = []
            total = start
            for span in spans:
                starts.append(total)
                total = total + span * 16
        for ref, row, at, span in zip(blocks, rows, starts, spans):
            turned[...] = jnp.broadcast_to(row, (ROWS, ROWS)).T

            def chunk(step, _, ref=ref, at=at, slot=slot):
                source = pl.multiple_of(step * 16, 16)
                target = pl.multiple_of(at + step * 16, 16)
                pos_c[pl.ds(target, 16), :] = turned[pl.ds(source, 16), :]
                for g in range(KV_HEADS):
                    lanes = slice(g * HEAD, (g + 1) * HEAD)
                    key_c[g, pl.ds(target, 16), :] = ref[slot, pl.ds(POS + source, 16), lanes]
                    value_c[g, pl.ds(target, 16), :] = ref[
                        slot, pl.ds(POS + ROWS + source, 16), lanes
                    ]
                return 0

            lax.fori_loop(0, span, chunk, 0)
        entries.append((slot, starts, counts))
        start = start + sum(spans) * 16
    rest = pl.ds(pl.multiple_of(start, 16), TILE)
    pos_c[rest, :] = jnp.full((TILE, ROWS), 1e9, F32)
    for g in range(KV_HEADS):
        key_c[g, rest, :] = jnp.zeros((TILE, HEAD), BF16)
        value_c[g, rest, :] = jnp.zeros((TILE, HEAD), BF16)
    return start, entries


def stats_tile(rate_ref, work_ref, state, key_c, value_c, mask, at, slot, g):
    some = slice(g * WIDE, (g + 1) * WIDE)
    raw = product(key_c[g, pl.ds(at, TILE), :], work_ref[0, some, :], NT)
    dots = product(value_c[g, pl.ds(at, TILE), :], work_ref[1, some, :], NT)
    for head in range(GROUP):
        lanes = slice(head * ROWS, (head + 1) * ROWS)
        scores = jnp.where(mask, raw[:, lanes] * rate_ref[g, 0:1, lanes], LOW)
        held = [state[slot * KV_HEADS + g, n, :, lanes] for n in range(5)]
        top, total, weighted, shifted, both = held
        scores = scores.reshape(TILE // 8, 8, ROWS)
        new_top = jnp.maximum(top, jnp.max(scores, axis=0))
        above = scores - new_top[None]
        weights = jnp.exp2(above)
        weighted_dots = weights * dots[:, lanes].reshape(TILE // 8, 8, ROWS)
        step_down = top - new_top
        factor = jnp.exp2(step_down)
        held = [
            new_top,
            factor * total + jnp.sum(weights, axis=0),
            factor * weighted + jnp.sum(weighted_dots, axis=0),
            factor * (shifted + step_down * total) + jnp.sum(weights * above, axis=0),
            factor * (both + step_down * weighted) + jnp.sum(weighted_dots * above, axis=0),
        ]
        for n in range(5):
            state[slot * KV_HEADS + g, n, :, lanes] = held[n]


def stats_body(jobs, is_first, is_last, *refs):
    rate_ref, own_ref, kept_ref, got_ref = refs[:4]
    refs = refs[4:]
    work = []
    for count, slots in jobs:
        work.append((refs[:count], slots))
        refs = refs[count:]
    if not is_first:
        prior_ref, refs = refs[0], refs[1:]
    if is_last:
        final_ref, scale_ref, state, key_c, value_c, pos_c, turned = refs
    else:
        state, key_c, value_c, pos_c, turned = refs
    query_rows, tops, first = query_side(own_ref)
    if is_first:
        state[...] = jnp.zeros_like(state)
        state[:, 0] = jnp.full((2 * KV_HEADS, 8, WIDE), LOW, F32)
    else:
        state[...] = prior_ref[...]
    for blocks, slots in work:
        top = jnp.maximum(tops[0], tops[1]) if len(slots) == 2 else tops[slots[0]]
        length, _ = place(blocks, first, top, key_c, value_c, pos_c, turned)

        def tile(step, _, slots=slots):
            at = pl.multiple_of(step * TILE, TILE)
            key_pos = pos_c[pl.ds(at, TILE), :]
            lowest = jnp.min(key_pos)
            for slot in slots:

                @pl.when(lowest <= tops[slot])
                def _(slot=slot):
                    mask = key_pos <= query_rows[slot]
                    for g in range(KV_HEADS):
                        stats_tile(
                            rate_ref, (kept_ref, got_ref)[slot], state, key_c, value_c, mask, at, slot, g
                        )

            return 0

        lax.fori_loop(0, (length + TILE - 1) // TILE, tile, 0)
    if not is_last:
        return
    lane = lax.broadcasted_iota(jnp.int32, (8, ROWS), 1)
    scale_row = jnp.zeros((8, ROWS), F32)
    for slot in range(2):
        live = query_rows[slot] >= 0.0
        for g in range(KV_HEADS):
            for head in range(GROUP):
                lanes = slice(head * ROWS, (head + 1) * ROWS)
                held = [state[slot * KV_HEADS + g, n, :, lanes] for n in range(5)]
                tops_in, total, weighted, shifted, both = held
                top = jnp.max(tops_in, axis=0, keepdims=True)
                step_down = tops_in - top
                factor = jnp.exp2(step_down)
                both = jnp.sum(factor * (both + step_down * weighted), axis=0, keepdims=True)
                shifted = jnp.sum(factor * (shifted + step_down * total), axis=0, keepdims=True)
                weighted = jnp.sum(factor * weighted, axis=0, keepdims=True)
                total = jnp.sum(factor * total, axis=0, keepdims=True)
                total = jnp.where(live, total, 1.0)
                mean = weighted / total
                spread = (both - mean * shifted) / total
                rate = rate_ref[g, 0:1, lanes] * math.sqrt(HEAD)
                spread = jnp.where(live, spread / rate, 0.0)
                final_ref[slot * KV_HEADS + g, 0:2, lanes] = jnp.concatenate(
                    [
                        jnp.where(live, top + jnp.log2(total), -LOW),
                        jnp.where(live, mean, 0.0),
                    ],
                    axis=0,
                )
                place_at = first * HEADS + g * GROUP + head
                scale_row = scale_row + jnp.where(
                    lane == place_at, jnp.sum(spread, axis=1, keepdims=True), 0.0
                )
    scale_ref[...] = scale_row


def grads_tile(
    rate_ref,
    work_ref,
    final_ref,
    key_c,
    value_c,
    key_sum,
    value_sum,
    query_sum,
    mask,
    at,
    slot,
    g,
):
    some = slice(g * WIDE, (g + 1) * WIDE)
    rows = pl.ds(at, TILE)
    keys = key_c[g, rows, :]
    values = value_c[g, rows, :]
    queries = work_ref[0, some, :]
    gradients = work_ref[1, some, :]
    raw = product(keys, queries, NT)
    dots = product(values, gradients, NT)
    probs, score_grads = [], []
    for head in range(GROUP):
        lanes = slice(head * ROWS, (head + 1) * ROWS)
        rate = rate_ref[g, 0:1, lanes]
        held = final_ref[slot * KV_HEADS + g, :, lanes]
        prob = jnp.where(mask, jnp.exp2(raw[:, lanes] * rate - held[0:1]), 0.0)
        grad = prob * (dots[:, lanes] - held[1:2])
        probs.append(prob.astype(BF16))
        score_grads.append((grad * (rate * (1.0 / LOG2E))).astype(BF16))
    prob_low = jnp.concatenate(probs, axis=1)
    score_low = jnp.concatenate(score_grads, axis=1)
    value_sum[g, rows, :] += product(prob_low, gradients, NN)
    key_sum[g, rows, :] += product(score_low, queries, NN)
    query_sum[slot * KV_HEADS + g] += product(keys, score_low, TN)


def grads_body(count, added, is_first, is_last, *refs):
    rate_ref, own_ref, kept_ref, got_ref, final_ref = refs[:5]
    blocks = refs[5 : 5 + count]
    refs = refs[5 + count :]
    scale_refs, refs = refs[:added], refs[added:]
    if not is_first:
        prior_ref, refs = refs[0], refs[1:]
    outs, refs = refs[:count], refs[count:]
    if added:
        scale_ref, refs = refs[0], refs[1:]
        scale_ref[...] = sum([ref[...] for ref in scale_refs[1:]], scale_refs[0][...])
    if is_last:
        query_outs, refs = refs[:2], refs[2:]
    query_sum, key_c, value_c, pos_c, turned, key_sum, value_sum = refs
    query_rows, tops, first = query_side(own_ref)
    length, entries = place(
        blocks, first, jnp.maximum(tops[0], tops[1]), key_c, value_c, pos_c, turned
    )
    if is_first:
        query_sum[...] = jnp.zeros_like(query_sum)
    else:
        query_sum[...] = prior_ref[...]

    def tile(step, _):
        at = pl.multiple_of(step * TILE, TILE)
        key_pos = pos_c[pl.ds(at, TILE), :]
        lowest = jnp.min(key_pos)
        for g in range(KV_HEADS):
            key_sum[g, pl.ds(at, TILE), :] = jnp.zeros((TILE, HEAD), F32)
            value_sum[g, pl.ds(at, TILE), :] = jnp.zeros((TILE, HEAD), F32)
        for slot in range(2):

            @pl.when(lowest <= tops[slot])
            def _(slot=slot):
                mask = key_pos <= query_rows[slot]
                for g in range(KV_HEADS):
                    grads_tile(
                        rate_ref,
                        (kept_ref, got_ref)[slot],
                        final_ref,
                        key_c,
                        value_c,
                        key_sum,
                        value_sum,
                        query_sum,
                        mask,
                        at,
                        slot,
                        g,
                    )

        return 0

    lax.fori_loop(0, (length + TILE - 1) // TILE, tile, 0)
    row = lax.broadcasted_iota(jnp.int32, (ROWS, HEAD), 0)
    for slot, starts, counts in entries:
        for out, at, n in zip(outs, starts, counts):
            at = pl.multiple_of(at, 16)
            for g in range(KV_HEADS):
                lanes = slice(g * HEAD, (g + 1) * HEAD)
                for number, total in enumerate((key_sum, value_sum)):
                    out[slot, number * ROWS : (number + 1) * ROWS, lanes] = jnp.where(
                        row < n, total[g, pl.ds(at, ROWS), :], 0.0
                    )
    if is_last:
        for slot in range(2):
            for g in range(KV_HEADS):
                for head in range(GROUP):
                    lanes = slice(head * ROWS, (head + 1) * ROWS)
                    rows = slice((g * GROUP + head) * ROWS, (g * GROUP + head + 1) * ROWS)
                    query_outs[slot][rows, :] = query_sum[slot * KV_HEADS + g, :, lanes].T.astype(
                        BF16
                    )


def compact_scratch(count):
    size = (2 * count + 1) * ROWS
    return [
        pltpu.VMEM((KV_HEADS, size, HEAD), BF16),
        pltpu.VMEM((KV_HEADS, size, HEAD), BF16),
        pltpu.VMEM((size, ROWS), F32),
        pltpu.VMEM((ROWS, ROWS), F32),
    ]


STATE = jax.ShapeDtypeStruct((2 * KV_HEADS, 5, 8, WIDE), F32)
FINAL = jax.ShapeDtypeStruct((2 * KV_HEADS, 8, WIDE), F32)


def stats(rate, own, kept, got, jobs, prior=None, is_last=False):
    if is_last:
        outs = [FINAL, jax.ShapeDtypeStruct((8, ROWS), F32)]
        scratch = [pltpu.VMEM(STATE.shape, F32)]
    else:
        outs, scratch = [STATE], []
    blocks = [block for some, _ in jobs for block in some]
    operands = [rate, own, kept, got, *blocks] + ([] if prior is None else [prior])
    sizes = [(len(some), slots) for some, slots in jobs]
    return call(
        functools.partial(stats_body, sizes, prior is None, is_last),
        outs,
        scratch + compact_scratch(max(count for count, _ in sizes)),
        sum(count * len(slots) for count, slots in sizes) * ROWS * 2 * HEADS * ROWS * HEAD * 4,
        4 << 20,
        [pl.BlockSpec(memory_space=pltpu.VMEM)] * len(operands),
    )(*operands)


def grads(rate, own, kept, got, final, blocks, scales=(), prior=None, is_last=False):
    count = len(blocks)
    outs = [jax.ShapeDtypeStruct((2, 2 * ROWS, KV_HEADS * HEAD), F32)] * count
    sums = jax.ShapeDtypeStruct((2 * KV_HEADS, HEAD, WIDE), F32)
    operands = [rate, own, kept, got, final, *blocks, *scales]
    operands = operands + ([] if prior is None else [prior])
    if scales:
        outs = outs + [jax.ShapeDtypeStruct((8, ROWS), F32)]
    if is_last:
        outs = outs + [jax.ShapeDtypeStruct((HEADS * ROWS, HEAD), BF16)] * 2
        scratch = [pltpu.VMEM(sums.shape, F32)]
    else:
        outs, scratch = outs + [sums], []
    size = (2 * count + 1) * ROWS
    scratch = (
        scratch
        + compact_scratch(count)
        + [pltpu.VMEM((KV_HEADS, size, HEAD), F32), pltpu.VMEM((KV_HEADS, size, HEAD), F32)]
    )
    return call(
        functools.partial(grads_body, count, len(scales), prior is None, is_last),
        outs,
        scratch,
        count * 2 * ROWS * 2 * HEADS * ROWS * 2 * HEAD * 5,
        6 << 20,
        [pl.BlockSpec(memory_space=pltpu.VMEM)] * len(operands),
    )(*operands)


def local(queries, keys, values, out_grad, routes, per_head_scale):
    me = lax.axis_index("ctx")
    size = lax.axis_size("ctx")
    ring = size // 2
    x = (me // ring).astype(jnp.int32)
    x_ref = x.reshape(1)
    across = [(i, (i + ring) % size) for i in range(size)]

    def neighbour(i, up):
        base, z = i // ring * ring, i % ring
        return base + (z + (1 if up == (z % 2 == 0) else -1)) % ring

    even = [(i, neighbour(i, True)) for i in range(size)]
    odd = [(i, neighbour(i, False)) for i in range(size)]

    def swap(array, pairs, axis="ctx"):
        return lax.ppermute(array, axis, pairs)

    smem = pl.BlockSpec(memory_space=pltpu.SMEM)
    vmem = pl.BlockSpec(memory_space=pltpu.VMEM)
    anywhere = pl.BlockSpec(memory_space=pl.ANY)
    width = KV_HEADS * HEAD
    message = jax.ShapeDtypeStruct((MESSAGE, width), BF16)
    keys_kept, keys_sent = call(
        pack_keys_body,
        [message, message],
        [
            pltpu.VMEM((ROWS, 2 * width), BF16),
            pltpu.VMEM((ROWS, 2 * width), BF16),
            pltpu.VMEM((1, ROWS), jnp.int32),
            pltpu.SemaphoreType.DMA((3,)),
        ],
        1024,
        1 << 20,
        [smem, anywhere, anywhere, anywhere],
    )(x_ref, keys[0], values[0], routes)
    keys_got = swap(keys_sent, across)
    work = jax.ShapeDtypeStruct((2, HEADS * ROWS, HEAD), BF16)
    kept, sent = call(
        pack_queries_body,
        [work, work],
        [
            pltpu.VMEM((ROWS, 2 * HEADS * HEAD), BF16),
            pltpu.VMEM((ROWS, 2 * HEADS * HEAD), BF16),
            pltpu.SemaphoreType.DMA((2,)),
        ],
        1024,
        4 << 20,
        [smem, anywhere, anywhere, anywhere],
    )(x_ref, keys_sent, queries[0], out_grad[0])
    got = swap(sent, across)
    own = call(
        join_body,
        jax.ShapeDtypeStruct((2, MESSAGE, width), BF16),
        [],
        1024,
        1 << 20,
        [anywhere, vmem, vmem],
    )(kept, keys_kept, keys_got)

    half_scale = lax.dynamic_slice_in_dim(per_head_scale, x * HEADS, HEADS)
    rate = jnp.repeat(half_scale * (LOG2E / math.sqrt(HEAD)), ROWS).reshape(KV_HEADS, 1, WIDE)
    rate = jnp.broadcast_to(rate, (KV_HEADS, 8, WIDE))

    a, b = [own], [own]
    for step in range(1, 4):
        a.append(swap(b[step - 1], even))
        b.append(swap(a[step - 1], odd))
    a.append(swap(b[3], even))

    (state,) = stats(rate, own, kept, kept, [([own, a[1], b[1]], (0,))])
    (state,) = stats(
        rate, own, kept, got, [([own, a[1], b[1]], (1,)), ([a[2], b[2]], (0, 1))], state
    )
    (state,) = stats(rate, own, kept, got, [([a[3], b[3]], (0, 1))], state)
    final, scale = stats(rate, own, kept, got, [([a[4]], (0, 1))], state, is_last=True)

    total_devices = lax.axis_size("dp") * size

    def exchange(array, masks):
        pairs = [[(i, i ^ mask) for i in range(total_devices)] for mask in masks]
        return [array] + [swap(array, pair, ("dp", "ctx")) for pair in pairs]

    scales = exchange(scale, (8,))
    far, sums = grads(rate, own, kept, got, final, [a[4]])
    from_even = swap(far.astype(BF16), even)
    part_a, part_b, scale, sums = grads(
        rate, own, kept, got, final, [a[3], b[3]], scales, sums
    )
    scales = exchange(scale, (16,))
    sent_a = swap(part_a.astype(BF16), even)
    sent_b = swap((part_b + from_even).astype(BF16), odd)
    part_a, part_b, near, scale, sums = grads(
        rate, own, kept, got, final, [a[2], b[2], own], scales, sums
    )
    scales = exchange(scale, (1, 2, 3))
    to_a = (part_a + sent_b).astype(BF16)
    to_b = (part_b + sent_a).astype(BF16)
    sent_a, sent_b = swap(to_a, even), swap(to_b, odd)
    part_a, part_b, scale, query_kept, query_sent = grads(
        rate, own, kept, got, final, [a[1], b[1]], scales, sums, is_last=True
    )
    query_got = swap(query_sent, across)
    scales = exchange(scale, (4, 32, 36))
    to_a = (part_a + sent_b).astype(BF16)
    to_b = (part_b + sent_a).astype(BF16)
    sent_a, sent_b = swap(to_a, even), swap(to_b, odd)
    scales = exchange(sum(scales[1:], scales[0]), (64, 128, 192))
    ours = (near[0] + sent_a[0] + sent_b[0]).astype(BF16)
    theirs = (near[1] + sent_a[1] + sent_b[1]).astype(BF16)
    other = swap(theirs, across)
    query_out, key_out, value_out, scale_out = call(
        functools.partial(finish_body, len(scales)),
        [
            jax.ShapeDtypeStruct((ROWS, 2 * HEADS * HEAD), BF16),
            jax.ShapeDtypeStruct((ROWS, 2 * width), BF16),
            jax.ShapeDtypeStruct((ROWS, 2 * width), BF16),
            jax.ShapeDtypeStruct((1, 2 * HEADS), F32),
        ],
        [],
        1024,
        2 << 20,
        [smem] + [vmem] * (4 + len(scales)),
    )(x_ref, query_kept, query_got, ours, other, *scales)
    return query_out[None], key_out[None], value_out[None], scale_out.reshape(2 * HEADS)


def solution(mesh):
    in_specs = (
        P("dp", "ctx", None),
        P("dp", "ctx", None),
        P("dp", "ctx", None),
        P("dp", "ctx", None),
        P("dp", "ctx"),
        P(),
    )
    out_specs = (P("dp", "ctx", None), P("dp", "ctx", None), P("dp", "ctx", None), P())
    return jax.shard_map(local, mesh=mesh, in_specs=in_specs, out_specs=out_specs, check_vma=False)
```

time: 157 us -> 119 us (0.76)
  waiting for transfers between devices: 46.3 us -> 21.6 us
  Pallas kernels: 39.3 us -> 28.6 us
  local copies, waits for them, and re-layouts: 9.31 us -> 4.98 us
  starting transfers between devices: 58 us -> 61.2 us
    ppermute x26 -> x29, waiting for transfers between devices: 46.3 us -> 21.6 us  [swap(): return lax.ppermute(array, axis, pairs)]
    pallas_call x10 -> x12, Pallas kernels: 39.3 us -> 28.6 us  [the longest x4 14.8 us: grads(): call(functools.partial(grads_body, count, len(scales), prior is None, is_...]
    unnamed x26 -> x14, local copies, waits for them, and re-layouts: 8.69 us -> 4.89 us
    ppermute x26 -> x29, starting transfers between devices: 58 us -> 61.2 us  [swap(): return lax.ppermute(array, axis, pairs)]
  transfers between devices with their start and end apart: 26 -> 29, of which waited for: 15 -> 11; matrix products, arithmetic and copies ran while one was open for 1% -> 1% of each run, Pallas kernels for 22% -> 20%
where the time goes in v2:
time: 119 us; the launch traced here: 118 us
  starting transfers between devices  61.2 us (51%)
  Pallas kernels  28.6 us (24%)
  waiting for transfers between devices  21.6 us (18%)
  local copies, waits for them, and re-layouts  4.98 us (4%)
    ppermute x29, starting transfers between devices, swap(): return lax.ppermute(array, axis, pairs)  61.2 us
    ppermute x29, waiting for transfers between devices, swap(): return lax.ppermute(array, axis, pairs)  21.6 us
    pallas_call x4, Pallas kernels, grads(): call(functools.partial(grads_body, count, len(scales), prior is None, is_...  14.8 us
    pallas_call x4, Pallas kernels, stats(): call(functools.partial(stats_body, sizes, prior is None, is_last), outs,...  10.5 us
    unnamed x14, local copies, waits for them, and re-layouts  4.89 us
  transfers between devices with their start and end apart: 29, of which 11 were waited for; matrix products, arithmetic and copies ran while one was open for 1% of the time, Pallas kernels for 20%

profile of v2, /device:TPU:38, one launch (start us, length us, event | category | flops | bytes accessed | tf_op | source)
XLA Modules:
  0.0 117.8 jit_solution(7485359681964891774)
XLA Ops:
  0.7 0.9 copy-done.2
  1.6 0.9 copy-done.3
  2.5 0.7 copy-done.4
  3.1 0.4 shard_map.93
  3.5 0.9 collective-permute-start
  4.4 1.2 copy-done
  5.6 1.2 copy-done.1
  6.8 1.7 %shard_map.94 = (bf16[2,1792,128]{2,1,0:T(8,128)(2,1)S(1)}, bf16[2,1792,128]{2,1,0:T(8,128)(2,1)}) custom-call(s32[1]{0:T(128)} %bitcast.x_ref, bf16[272,256]{1,0:T(8,128)(2,1)S(1)} %get-tuple-element.30.after_ref, bf16[128,3584]{1,0:T(8,128)(2,1)S(1)} %bitcast.18, bf16[128,3584]{1,0:T(8,128)(2,1)S(1)} %bitcast.19), custom_call_target="tpu_custom_call" | custom-call | flops 1024 | bytes 4194304 | tf_op jit(solution)/shard_map/pallas_call | solution.py:483
  8.5 0.5 collective-permute-done.got_ref
  9.0 2.0 %collective-permute-start.2 = (bf16[2,272,256]{2,1,0:T(8,128)(2,1)S(1)}, bf16[2,272,256]{2,1,0:T(8,128)(2,1)S(1)}, u32[]{:S(2)}, u32[]{:S(2)}) collective-permute-start(bf16[2,272,256]{2,1,0:T(8,128)(2,1)S(1)} %shard_map.95.refs_1_.refs_4_.refs_7_), channel_id=1, source_target_pairs={{0,7},{1,2},{2,1},{3,4},{4,3},{5,6},{6,5},{7,0},{8,15},{9,10},{10,... | collective-permute-start | bytes 835592 | tf_op jit(solution)/shard_map/ppermute | solution.py:461
  11.0 0.8 collective-permute-start.1
  11.8 4.0 %collective-permute-start.6 = (bf16[2,272,256]{2,1,0:T(8,128)(2,1)S(1)}, bf16[2,272,256]{2,1,0:T(8,128)(2,1)S(1)}, u32[]{:S(2)}, u32[]{:S(2)}) collective-permute-start(bf16[2,272,256]{2,1,0:T(8,128)(2,1)S(1)} %shard_map.95.refs_1_.refs_4_.refs_7_), channel_id=1, source_target_pairs={{0,1},{1,0},{2,3},{3,2},{4,5},{5,4},{6,7},{7,6},{8,9},{9,8},{10,11... | collective-permute-start | bytes 835592 | tf_op jit(solution)/shard_map/ppermute | solution.py:461
  15.9 1.0 collective-permute-done.2.refs_6_
  16.9 4.0 %collective-permute-start.3 = (bf16[2,272,256]{2,1,0:T(8,128)(2,1)S(1)}, bf16[2,272,256]{2,1,0:T(8,128)(2,1)S(1)}, u32[]{:S(2)}, u32[]{:S(2)}) collective-permute-start(bf16[2,272,256]{2,1,0:T(8,128)(2,1)S(1)} %collective-permute-done.2.refs_6_), channel_id=1, source_target_pairs={{0,1},{1,0},{2,3},{3,2},{4,5},{5,4},{6,7},{7,6},{8,9},{9,8},{10,11... | collective-permute-start | bytes 835592 | tf_op jit(solution)/shard_map/ppermute | solution.py:461
  21.0 1.9 %collective-permute-done.6.refs_5_ = bf16[2,272,256]{2,1,0:T(8,128)(2,1)S(1)} collective-permute-done((bf16[2,272,256]{2,1,0:T(8,128)(2,1)S(1)}, bf16[2,272,256]{2,1,0:T(8,128)(2,1)S(1)}, u32[]{:S(2)}, u32[]{:S(2)}) %collective-permute-start.6) | collective-permute-done | bytes 278560 | tf_op jit(solution)/shard_map/ppermute | solution.py:461
  22.9 1.1 collective-permute-start.7
  24.0 3.6 %collective-permute-done.3.refs_7_.refs_5_ = bf16[2,272,256]{2,1,0:T(8,128)(2,1)S(1)} collective-permute-done((bf16[2,272,256]{2,1,0:T(8,128)(2,1)S(1)}, bf16[2,272,256]{2,1,0:T(8,128)(2,1)S(1)}, u32[]{:S(2)}, u32[]{:S(2)}) %collective-permute-start.3) | collective-permute-done | bytes 278560 | tf_op jit(solution)/shard_map/ppermute | solution.py:461
  27.6 1.0 collective-permute-start.4
  28.6 0.1 dynamic-slice_multiply_fusion
  28.6 0.1 broadcast_in_dim.21
  28.7 1.1 collective-permute-done.7.refs_8_.refs_6_
  29.8 3.0 %collective-permute-start.8 = (bf16[2,272,256]{2,1,0:T(8,128)(2,1)S(1)}, bf16[2,272,256]{2,1,0:T(8,128)(2,1)S(1)}, u32[]{:S(2)}, u32[]{:S(2)}) collective-permute-start(bf16[2,272,256]{2,1,0:T(8,128)(2,1)S(1)} %collective-permute-done.7.refs_8_.refs_6_), channel_id=1, source_target_pairs={{0,1},{1,0},{2,3},{3,2},{4,5},{5,4},{6,7},{7,6},{8,9},{9,8},{10,11... | collective-permute-start | bytes 835592 | tf_op jit(solution)/shard_map/ppermute | solution.py:461
  32.7 0.1 broadcast_bitcast_fusion
  32.8 2.6 %collective-permute-done.4.refs_5_.refs_6_ = bf16[2,272,256]{2,1,0:T(8,128)(2,1)S(1)} collective-permute-done((bf16[2,272,256]{2,1,0:T(8,128)(2,1)S(1)}, bf16[2,272,256]{2,1,0:T(8,128)(2,1)S(1)}, u32[]{:S(2)}, u32[]{:S(2)}) %collective-permute-start.4) | collective-permute-done | bytes 278560 | tf_op jit(solution)/shard_map/ppermute | solution.py:461
  35.4 3.0 %collective-permute-start.5 = (bf16[2,272,256]{2,1,0:T(8,128)(2,1)S(1)}, bf16[2,272,256]{2,1,0:T(8,128)(2,1)S(1)}, u32[]{:S(2)}, u32[]{:S(2)}) collective-permute-start(bf16[2,272,256]{2,1,0:T(8,128)(2,1)S(1)} %collective-permute-done.4.refs_5_.refs_6_), channel_id=1, source_target_pairs={{0,1},{1,0},{2,3},{3,2},{4,5},{5,4},{6,7},{7,6},{8,9},{9,8},{10,11... | collective-permute-start | bytes 835592 | tf_op jit(solution)/shard_map/ppermute | solution.py:461
  38.3 3.2 %shard_map.96.refs_9_ = f32[4,5,8,896]{3,2,1,0:T(8,128)S(1)} custom-call(f32[2,8,896]{2,1,0:T(8,128)S(1)} %broadcast_in_dim.24.refs_0_, bf16[2,272,256]{2,1,0:T(8,128)(2,1)S(1)} %shard_map.95.refs_1_.refs_4_.refs_7_, bf16[2,1792,128]{2,1,0:T(8,128)(2,1)S(1)} %get-tuple-element.31.after_ref.refs_2_.refs_3_, ...), custom_call_target="tpu_custom_call" | custom-call | flops 704643072 | bytes 4194304 | tf_op jit(solution)/shard_map/pallas_call | solution.py:406
  41.6 3.7 %shard_map.97.refs_6_ = f32[4,5,8,896]{3,2,1,0:T(8,128)S(1)} custom-call(f32[2,8,896]{2,1,0:T(8,128)S(1)} %broadcast_in_dim.24.refs_0_, bf16[2,272,256]{2,1,0:T(8,128)(2,1)S(1)} %shard_map.95.refs_1_.refs_4_.refs_7_, bf16[2,1792,128]{2,1,0:T(8,128)(2,1)S(1)} %get-tuple-element.31.after_ref.refs_2_.refs_3_, ...), custom_call_target="tpu_custom_call" | custom-call | flops 1644167168 | bytes 4194304 | tf_op jit(solution)/shard_map/pallas_call | solution.py:406
  45.3 2.2 %shard_map.98.refs_5_ = f32[4,5,8,896]{3,2,1,0:T(8,128)S(1)} custom-call(f32[2,8,896]{2,1,0:T(8,128)S(1)} %broadcast_in_dim.24.refs_0_, bf16[2,272,256]{2,1,0:T(8,128)(2,1)S(1)} %shard_map.95.refs_1_.refs_4_.refs_7_, bf16[2,1792,128]{2,1,0:T(8,128)(2,1)S(1)} %get-tuple-element.31.after_ref.refs_2_.refs_3_, ...), custom_call_target="tpu_custom_call" | custom-call | flops 939524096 | bytes 4194304 | tf_op jit(solution)/shard_map/pallas_call | solution.py:406
  47.5 1.4 %shard_map.99 = (f32[4,8,896]{2,1,0:T(8,128)S(1)}, f32[8,128]{1,0:T(8,128)S(1)}) custom-call(f32[2,8,896]{2,1,0:T(8,128)S(1)} %broadcast_in_dim.24.refs_0_, bf16[2,272,256]{2,1,0:T(8,128)(2,1)S(1)} %shard_map.95.refs_1_.refs_4_.refs_7_, bf16[2,1792,128]{2,1,0:T(8,128)(2,1)S(1)} %get-tuple-element.31.after_ref.refs_2_.refs_3_, ...), custom_call_target="tpu_custom_call" | custom-call | flops 469762048 | bytes 4194304 | tf_op jit(solution)/shard_map/pallas_call | solution.py:406
  48.9 1.7 %shard_map.100 = (f32[2,256,256]{2,1,0:T(8,128)S(1)}, f32[4,128,896]{2,1,0:T(8,128)S(1)}) custom-call(f32[2,8,896]{2,1,0:T(8,128)S(1)} %broadcast_in_dim.24.refs_0_, bf16[2,272,256]{2,1,0:T(8,128)(2,1)S(1)} %shard_map.95.refs_1_.refs_4_.refs_7_, bf16[2,1792,128]{2,1,0:T(8,128)(2,1)S(1)} %get-tuple-element.31.after_ref.refs_2_.refs_3_, ...), custom_call_target="tpu_custom_call" | custom-call | flops 1174405120 | bytes 6291456 | tf_op jit(solution)/shard_map/pallas_call | solution.py:435
  50.7 0.1 collective-permute-start.18
  50.8 0.2 collective-permute-start.9
  51.0 3.5 %collective-permute-done.9.refs_8_ = f32[8,128]{1,0:T(8,128)S(1)} collective-permute-done((f32[8,128]{1,0:T(8,128)S(1)}, f32[8,128]{1,0:T(8,128)S(1)}, u32[]{:S(2)}, u32[]{:S(2)}) %collective-permute-start.9) | collective-permute-done | bytes 4128 | tf_op jit(solution)/shard_map/ppermute | solution.py:461
  54.5 2.9 %shard_map.101 = (f32[2,256,256]{2,1,0:T(8,128)S(1)}, f32[2,256,256]{2,1,0:T(8,128)S(1)}, f32[8,128]{1,0:T(8,128)S(1)}, f32[4,128,896]{2,1,0:T(8,128)S(1)}) custom-call(f32[2,8,896]{2,1,0:T(8,128)S(1)} %broadcast_in_dim.24.refs_0_, bf16[2,272,256]{2,1,0:T(8,128)(2,1)S(1)} %shard_map.95.refs_1_.refs_4_.refs_7_, ...), custom_call_target="tpu_custom_call" | custom-call | flops 2348810240 | bytes 6291456 | tf_op jit(solution)/shard_map/pallas_call | solution.py:435
  57.4 0.1 collective-permute-start.10
  57.6 1.0 collective-permute-start.15
  58.5 0.2 collective-permute-done.18
  58.8 0.1 add_convert_fusion.2
  58.8 4.0 %collective-permute-start.19 = (bf16[2,256,256]{2,1,0:T(8,128)(2,1)S(1)}, bf16[2,256,256]{2,1,0:T(8,128)(2,1)S(1)}, u32[]{:S(2)}, u32[]{:S(2)}) collective-permute-start(bf16[2,256,256]{2,1,0:T(8,128)(2,1)S(1)} %add_convert_fusion.2), channel_id=1, source_target_pairs={{0,7},{1,2},{2,1},{3,4},{4,3},{5,6},{6,5},{7,0},{8,15},{9,10},{10,... | collective-permute-start | bytes 786440 | tf_op jit(solution)/shard_map/ppermute | solution.py:461
  62.9 5.9 %shard_map.102 = (f32[2,256,256]{2,1,0:T(8,128)S(1)}, f32[2,256,256]{2,1,0:T(8,128)S(1)}, f32[2,256,256]{2,1,0:T(8,128)S(1)}, f32[8,128]{1,0:T(8,128)S(1)}, f32[4,128,896]{2,1,0:T(8,128)S(1)}) custom-call(f32[2,8,896]{2,1,0:T(8,128)S(1)} %broadcast_in_dim.24.refs_0_, bf16[2,272,256]{2,1,0:T(8,128)(2,1)S(1)} %shard_map.95.refs_1_.refs_4_.refs_7_, ...), custom_call_target="tpu_custom_call" | custom-call | flops 3523215360 | bytes 6291456 | tf_op jit(solution)/shard_map/pallas_call | solution.py:435
  68.8 1.2 collective-permute-start.13
  70.0 6.9 %collective-permute-start.12 = (f32[8,128]{1,0:T(8,128)S(1)}, f32[8,128]{1,0:T(8,128)S(1)}, u32[]{:S(2)}, u32[]{:S(2)}) collective-permute-start(f32[8,128]{1,0:T(8,128)S(1)} %get-tuple-element.39.refs_7_), channel_id=1, source_target_pairs={{0,2},{1,3},{2,0},{3,1},{4,6},{5,7},{6,4},{7,5},{8,10},{9,11},{10,... | collective-permute-start | bytes 12296 | tf_op jit(solution)/shard_map/ppermute | solution.py:461
  76.9 1.3 %collective-permute-start.11 = (f32[8,128]{1,0:T(8,128)S(1)}, f32[8,128]{1,0:T(8,128)S(1)}, u32[]{:S(2)}, u32[]{:S(2)}) collective-permute-start(f32[8,128]{1,0:T(8,128)S(1)} %get-tuple-element.39.refs_7_), channel_id=1, source_target_pairs={{0,1},{1,0},{2,3},{3,2},{4,5},{5,4},{6,7},{7,6},{8,9},{9,8},{10,11... | collective-permute-start | bytes 12296 | tf_op jit(solution)/shard_map/ppermute | solution.py:461
  78.2 0.1 add_convert_fusion.4
  78.2 1.6 %collective-permute-start.16 = (bf16[2,256,256]{2,1,0:T(8,128)(2,1)S(1)}, bf16[2,256,256]{2,1,0:T(8,128)(2,1)S(1)}, u32[]{:S(2)}, u32[]{:S(2)}) collective-permute-start(bf16[2,256,256]{2,1,0:T(8,128)(2,1)S(1)} %add_convert_fusion.4), channel_id=1, source_target_pairs={{0,7},{1,2},{2,1},{3,4},{4,3},{5,6},{6,5},{7,0},{8,15},{9,10},{10,... | collective-permute-start | bytes 786440 | tf_op jit(solution)/shard_map/ppermute | solution.py:461
  79.8 0.1 add_convert_fusion.1
  79.9 4.2 %collective-permute-start.20 = (bf16[2,256,256]{2,1,0:T(8,128)(2,1)S(1)}, bf16[2,256,256]{2,1,0:T(8,128)(2,1)S(1)}, u32[]{:S(2)}, u32[]{:S(2)}) collective-permute-start(bf16[2,256,256]{2,1,0:T(8,128)(2,1)S(1)} %add_convert_fusion.1), channel_id=1, source_target_pairs={{0,1},{1,0},{2,3},{3,2},{4,5},{5,4},{6,7},{7,6},{8,9},{9,8},{10,11... | collective-permute-start | bytes 786440 | tf_op jit(solution)/shard_map/ppermute | solution.py:461
  84.1 4.2 %shard_map.103 = (f32[2,256,256]{2,1,0:T(8,128)S(1)}, f32[2,256,256]{2,1,0:T(8,128)S(1)}, f32[8,128]{1,0:T(8,128)S(1)}, bf16[1792,128]{1,0:T(8,128)(2,1)S(1)}, bf16[1792,128]{1,0:T(8,128)(2,1)S(1)}) custom-call(f32[2,8,896]{2,1,0:T(8,128)S(1)} %broadcast_in_dim.24.refs_0_, bf16[2,272,256]{2,1,0:T(8,128)(2,1)S(1)} %shard_map.95.refs_1_.refs_4_.refs_7_, ...), custom_call_target="tpu_custom_call" | custom-call | flops 2348810240 | bytes 6291456 | tf_op jit(solution)/shard_map/pallas_call | solution.py:435
  88.3 0.1 add_convert_fusion.3
  88.4 2.6 %collective-permute-start.17 = (bf16[2,256,256]{2,1,0:T(8,128)(2,1)S(1)}, bf16[2,256,256]{2,1,0:T(8,128)(2,1)S(1)}, u32[]{:S(2)}, u32[]{:S(2)}) collective-permute-start(bf16[2,256,256]{2,1,0:T(8,128)(2,1)S(1)} %add_convert_fusion.3), channel_id=1, source_target_pairs={{0,1},{1,0},{2,3},{3,2},{4,5},{5,4},{6,7},{7,6},{8,9},{9,8},{10,11... | collective-permute-start | bytes 786440 | tf_op jit(solution)/shard_map/ppermute | solution.py:461
  91.1 0.1 collective-permute-start.21
  91.2 4.9 %collective-permute-start.25 = (f32[8,128]{1,0:T(8,128)S(1)}, f32[8,128]{1,0:T(8,128)S(1)}, u32[]{:S(2)}, u32[]{:S(2)}) collective-permute-start(f32[8,128]{1,0:T(8,128)S(1)} %get-tuple-element.51), channel_id=1, source_target_pairs={{0,36},{1,37},{2,38},{3,39},{4,32},{5,33},{6,34},{7,35},{8,44},{9,... | collective-permute-start | bytes 12296 | tf_op jit(solution)/shard_map/ppermute | solution.py:461
  96.1 1.7 %collective-permute-start.24 = (f32[8,128]{1,0:T(8,128)S(1)}, f32[8,128]{1,0:T(8,128)S(1)}, u32[]{:S(2)}, u32[]{:S(2)}) collective-permute-start(f32[8,128]{1,0:T(8,128)S(1)} %get-tuple-element.51), channel_id=1, source_target_pairs={{0,32},{1,33},{2,34},{3,35},{4,36},{5,37},{6,38},{7,39},{8,40},{9,... | collective-permute-start | bytes 12296 | tf_op jit(solution)/shard_map/ppermute | solution.py:461
  97.8 2.3 %collective-permute-start.23 = (f32[8,128]{1,0:T(8,128)S(1)}, f32[8,128]{1,0:T(8,128)S(1)}, u32[]{:S(2)}, u32[]{:S(2)}) collective-permute-start(f32[8,128]{1,0:T(8,128)S(1)} %get-tuple-element.51), channel_id=1, source_target_pairs={{0,4},{1,5},{2,6},{3,7},{4,0},{5,1},{6,2},{7,3},{8,12},{9,13},{10,... | collective-permute-start | bytes 12296 | tf_op jit(solution)/shard_map/ppermute | solution.py:461
  100.1 1.6 %collective-permute-start.14 = (bf16[1792,128]{1,0:T(8,128)(2,1)S(1)}, bf16[1792,128]{1,0:T(8,128)(2,1)S(1)}, u32[]{:S(2)}, u32[]{:S(2)}) collective-permute-start(bf16[1792,128]{1,0:T(8,128)(2,1)S(1)} %get-tuple-element.42), channel_id=1, source_target_pairs={{0,8},{1,9},{2,10},{3,11},{4,12},{5,13},{6,14},{7,15},{8,0},{9,1},... | collective-permute-start | bytes 1376264 | tf_op jit(solution)/shard_map/ppermute | solution.py:461
  101.7 0.1 fusion.1
  101.8 0.6 collective-permute-start.22
  102.4 2.9 %collective-permute-done.23 = f32[8,128]{1,0:T(8,128)S(1)} collective-permute-done((f32[8,128]{1,0:T(8,128)S(1)}, f32[8,128]{1,0:T(8,128)S(1)}, u32[]{:S(2)}, u32[]{:S(2)}) %collective-permute-start.23) | collective-permute-done | bytes 4128 | tf_op jit(solution)/shard_map/ppermute | solution.py:461
  105.3 6.2 %collective-permute-start.28 = (f32[8,128]{1,0:T(8,128)S(1)}, f32[8,128]{1,0:T(8,128)S(1)}, u32[]{:S(2)}, u32[]{:S(2)}) collective-permute-start(f32[8,128]{1,0:T(8,128)S(1)} %add_add_fusion.refs_0_), channel_id=1, source_target_pairs={{0,192},{1,193},{2,194},{3,195},{4,196},{5,197},{6,198},{7,199},{8... | collective-permute-start | bytes 12296 | tf_op jit(solution)/shard_map/ppermute | solution.py:461
  111.5 0.6 collective-permute-start.27
  112.1 0.4 collective-permute-start.26
  112.4 0.6 collective-permute-done.28.refs_3_
  113.1 3.5 %collective-permute-done.27.refs_2_ = f32[8,128]{1,0:T(8,128)S(1)} collective-permute-done((f32[8,128]{1,0:T(8,128)S(1)}, f32[8,128]{1,0:T(8,128)S(1)}, u32[]{:S(2)}, u32[]{:S(2)}) %collective-permute-start.27) | collective-permute-done | bytes 4128 | tf_op jit(solution)/shard_map/ppermute | solution.py:461
  116.6 1.2 %shard_map.104 = (bf16[128,3584]{1,0:T(8,128)(2,1)}, bf16[128,512]{1,0:T(8,128)(2,1)}, bf16[128,512]{1,0:T(8,128)(2,1)}, f32[1,28]{1,0:T(1,128)}) custom-call(s32[1]{0:T(128)} %bitcast.x_ref, bf16[1792,128]{1,0:T(8,128)(2,1)S(1)} %get-tuple-element.41.keep_ref, bf16[1792,128]{1,0:T(8,128)(2,1)S(1)} %collective-permute-done.14.got_ref, ...), custom_call_target="tpu_custom_call" | custom-call | flops 1024 | bytes 2097152 | tf_op jit(solution)/shard_map/pallas_call | solution.py:556
  (32 shorter events, 0.2 us)
Async XLA Ops:
  0.6 0.9 copy-start.2
  1.6 0.9 copy-start.3
  2.5 0.7 copy-start.4
  3.1 25.4 %copy-start.5 = (f32[28]{0:T(128)S(1)}, f32[28]{0:T(128)}, u32[]{:S(2)}) copy-start(f32[28]{0:T(128)} %param.11) | copy-start | bytes 340
  3.5 5.5 %collective-permute-start = (bf16[272,256]{1,0:T(8,128)(2,1)S(1)}, bf16[272,256]{1,0:T(8,128)(2,1)S(1)}, u32[]{:S(2)}, u32[]{:S(2)}) collective-permute-start(bf16[272,256]{1,0:T(8,128)(2,1)S(1)} %get-tuple-element.30.after_ref), channel_id=1, source_target_pairs={{0,8},{1,9},{2,10},{3,11},{4,12},{5,13},{6,14},{7,15},{8,0},{9,1},... | collective-permute-start | bytes 417800 | tf_op jit(solution)/shard_map/ppermute | solution.py:461
  4.4 1.2 %copy-start = (bf16[1,128,3584]{2,1,0:T(8,128)(2,1)S(1)}, bf16[1,128,3584]{2,1,0:T(8,128)(2,1)}, u32[]{:S(2)}) copy-start(bf16[1,128,3584]{2,1,0:T(8,128)(2,1)} %param.6) | copy-start | bytes 2752516
  5.6 1.2 %copy-start.1 = (bf16[1,128,3584]{2,1,0:T(8,128)(2,1)S(1)}, bf16[1,128,3584]{2,1,0:T(8,128)(2,1)}, u32[]{:S(2)}) copy-start(bf16[1,128,3584]{2,1,0:T(8,128)(2,1)} %param.9) | copy-start | bytes 2752516
  9.0 7.9 %collective-permute-start.2 = (bf16[2,272,256]{2,1,0:T(8,128)(2,1)S(1)}, bf16[2,272,256]{2,1,0:T(8,128)(2,1)S(1)}, u32[]{:S(2)}, u32[]{:S(2)}) collective-permute-start(bf16[2,272,256]{2,1,0:T(8,128)(2,1)S(1)} %shard_map.95.refs_1_.refs_4_.refs_7_), channel_id=1, source_target_pairs={{0,7},{1,2},{2,1},{3,4},{4,3},{5,6},{6,5},{7,0},{8,15},{9,10},{10,... | collective-permute-start | bytes 835592 | tf_op jit(solution)/shard_map/ppermute | solution.py:461
  11.0 30.5 %collective-permute-start.1 = (bf16[2,1792,128]{2,1,0:T(8,128)(2,1)}, bf16[2,1792,128]{2,1,0:T(8,128)(2,1)S(1)}, u32[]{:S(2)}, u32[]{:S(2)}) collective-permute-start(bf16[2,1792,128]{2,1,0:T(8,128)(2,1)} %get-tuple-element.33), channel_id=1, source_target_pairs={{0,8},{1,9},{2,10},{3,11},{4,12},{5,13},{6,14},{7,15},{8,0},{9,1},... | collective-permute-start | bytes 2752520 | tf_op jit(solution)/shard_map/ppermute | solution.py:461
  11.8 11.0 %collective-permute-start.6 = (bf16[2,272,256]{2,1,0:T(8,128)(2,1)S(1)}, bf16[2,272,256]{2,1,0:T(8,128)(2,1)S(1)}, u32[]{:S(2)}, u32[]{:S(2)}) collective-permute-start(bf16[2,272,256]{2,1,0:T(8,128)(2,1)S(1)} %shard_map.95.refs_1_.refs_4_.refs_7_), channel_id=1, source_target_pairs={{0,1},{1,0},{2,3},{3,2},{4,5},{5,4},{6,7},{7,6},{8,9},{9,8},{10,11... | collective-permute-start | bytes 835592 | tf_op jit(solution)/shard_map/ppermute | solution.py:461
  16.9 10.7 %collective-permute-start.3 = (bf16[2,272,256]{2,1,0:T(8,128)(2,1)S(1)}, bf16[2,272,256]{2,1,0:T(8,128)(2,1)S(1)}, u32[]{:S(2)}, u32[]{:S(2)}) collective-permute-start(bf16[2,272,256]{2,1,0:T(8,128)(2,1)S(1)} %collective-permute-done.2.refs_6_), channel_id=1, source_target_pairs={{0,1},{1,0},{2,3},{3,2},{4,5},{5,4},{6,7},{7,6},{8,9},{9,8},{10,11... | collective-permute-start | bytes 835592 | tf_op jit(solution)/shard_map/ppermute | solution.py:461
  22.9 6.9 %collective-permute-start.7 = (bf16[2,272,256]{2,1,0:T(8,128)(2,1)S(1)}, bf16[2,272,256]{2,1,0:T(8,128)(2,1)S(1)}, u32[]{:S(2)}, u32[]{:S(2)}) collective-permute-start(bf16[2,272,256]{2,1,0:T(8,128)(2,1)S(1)} %collective-permute-done.6.refs_5_), channel_id=1, source_target_pairs={{0,7},{1,2},{2,1},{3,4},{4,3},{5,6},{6,5},{7,0},{8,15},{9,10},{10,... | collective-permute-start | bytes 835592 | tf_op jit(solution)/shard_map/ppermute | solution.py:461
  27.6 7.8 %collective-permute-start.4 = (bf16[2,272,256]{2,1,0:T(8,128)(2,1)S(1)}, bf16[2,272,256]{2,1,0:T(8,128)(2,1)S(1)}, u32[]{:S(2)}, u32[]{:S(2)}) collective-permute-start(bf16[2,272,256]{2,1,0:T(8,128)(2,1)S(1)} %collective-permute-done.3.refs_7_.refs_5_), channel_id=1, source_target_pairs={{0,7},{1,2},{2,1},{3,4},{4,3},{5,6},{6,5},{7,0},{8,15},{9,10},{10,... | collective-permute-start | bytes 835592 | tf_op jit(solution)/shard_map/ppermute | solution.py:461
  29.8 15.5 %collective-permute-start.8 = (bf16[2,272,256]{2,1,0:T(8,128)(2,1)S(1)}, bf16[2,272,256]{2,1,0:T(8,128)(2,1)S(1)}, u32[]{:S(2)}, u32[]{:S(2)}) collective-permute-start(bf16[2,272,256]{2,1,0:T(8,128)(2,1)S(1)} %collective-permute-done.7.refs_8_.refs_6_), channel_id=1, source_target_pairs={{0,1},{1,0},{2,3},{3,2},{4,5},{5,4},{6,7},{7,6},{8,9},{9,8},{10,11... | collective-permute-start | bytes 835592 | tf_op jit(solution)/shard_map/ppermute | solution.py:461
  35.4 12.1 %collective-permute-start.5 = (bf16[2,272,256]{2,1,0:T(8,128)(2,1)S(1)}, bf16[2,272,256]{2,1,0:T(8,128)(2,1)S(1)}, u32[]{:S(2)}, u32[]{:S(2)}) collective-permute-start(bf16[2,272,256]{2,1,0:T(8,128)(2,1)S(1)} %collective-permute-done.4.refs_5_.refs_6_), channel_id=1, source_target_pairs={{0,1},{1,0},{2,3},{3,2},{4,5},{5,4},{6,7},{7,6},{8,9},{9,8},{10,11... | collective-permute-start | bytes 835592 | tf_op jit(solution)/shard_map/ppermute | solution.py:461
  50.7 8.0 %collective-permute-start.18 = (bf16[2,256,256]{2,1,0:T(8,128)(2,1)S(1)}, bf16[2,256,256]{2,1,0:T(8,128)(2,1)S(1)}, u32[]{:S(2)}, u32[]{:S(2)}) collective-permute-start(bf16[2,256,256]{2,1,0:T(8,128)(2,1)S(1)} %convert_element_type.69), channel_id=1, source_target_pairs={{0,1},{1,0},{2,3},{3,2},{4,5},{5,4},{6,7},{7,6},{8,9},{9,8},{10,11... | collective-permute-start | bytes 786440 | tf_op jit(solution)/shard_map/ppermute | solution.py:461
  50.8 3.7 %collective-permute-start.9 = (f32[8,128]{1,0:T(8,128)S(1)}, f32[8,128]{1,0:T(8,128)S(1)}, u32[]{:S(2)}, u32[]{:S(2)}) collective-permute-start(f32[8,128]{1,0:T(8,128)S(1)} %get-tuple-element.35.refs_7_), channel_id=1, source_target_pairs={{0,8},{1,9},{2,10},{3,11},{4,12},{5,13},{6,14},{7,15},{8,0},{9,1},... | collective-permute-start | bytes 12296 | tf_op jit(solution)/shard_map/ppermute | solution.py:461
  57.4 5.5 %collective-permute-start.10 = (f32[8,128]{1,0:T(8,128)S(1)}, f32[8,128]{1,0:T(8,128)S(1)}, u32[]{:S(2)}, u32[]{:S(2)}) collective-permute-start(f32[8,128]{1,0:T(8,128)S(1)} %get-tuple-element.37.refs_8_), channel_id=1, source_target_pairs={{0,16},{1,17},{2,18},{3,19},{4,20},{5,21},{6,22},{7,23},{8,24},{9,... | collective-permute-start | bytes 12296 | tf_op jit(solution)/shard_map/ppermute | solution.py:461
  57.6 20.6 %collective-permute-start.15 = (bf16[2,256,256]{2,1,0:T(8,128)(2,1)S(1)}, bf16[2,256,256]{2,1,0:T(8,128)(2,1)S(1)}, u32[]{:S(2)}, u32[]{:S(2)}) collective-permute-start(bf16[2,256,256]{2,1,0:T(8,128)(2,1)S(1)} %convert_element_type.63), channel_id=1, source_target_pairs={{0,1},{1,0},{2,3},{3,2},{4,5},{5,4},{6,7},{7,6},{8,9},{9,8},{10,11... | collective-permute-start | bytes 786440 | tf_op jit(solution)/shard_map/ppermute | solution.py:461
  58.8 20.9 %collective-permute-start.19 = (bf16[2,256,256]{2,1,0:T(8,128)(2,1)S(1)}, bf16[2,256,256]{2,1,0:T(8,128)(2,1)S(1)}, u32[]{:S(2)}, u32[]{:S(2)}) collective-permute-start(bf16[2,256,256]{2,1,0:T(8,128)(2,1)S(1)} %add_convert_fusion.2), channel_id=1, source_target_pairs={{0,7},{1,2},{2,1},{3,4},{4,3},{5,6},{6,5},{7,0},{8,15},{9,10},{10,... | collective-permute-start | bytes 786440 | tf_op jit(solution)/shard_map/ppermute | solution.py:461
  68.8 15.3 %collective-permute-start.13 = (f32[8,128]{1,0:T(8,128)S(1)}, f32[8,128]{1,0:T(8,128)S(1)}, u32[]{:S(2)}, u32[]{:S(2)}) collective-permute-start(f32[8,128]{1,0:T(8,128)S(1)} %get-tuple-element.39.refs_7_), channel_id=1, source_target_pairs={{0,3},{1,2},{2,1},{3,0},{4,7},{5,6},{6,5},{7,4},{8,11},{9,10},{10,... | collective-permute-start | bytes 12296 | tf_op jit(solution)/shard_map/ppermute | solution.py:461
  70.0 14.1 %collective-permute-start.12 = (f32[8,128]{1,0:T(8,128)S(1)}, f32[8,128]{1,0:T(8,128)S(1)}, u32[]{:S(2)}, u32[]{:S(2)}) collective-permute-start(f32[8,128]{1,0:T(8,128)S(1)} %get-tuple-element.39.refs_7_), channel_id=1, source_target_pairs={{0,2},{1,3},{2,0},{3,1},{4,6},{5,7},{6,4},{7,5},{8,10},{9,11},{10,... | collective-permute-start | bytes 12296 | tf_op jit(solution)/shard_map/ppermute | solution.py:461
  76.9 7.2 %collective-permute-start.11 = (f32[8,128]{1,0:T(8,128)S(1)}, f32[8,128]{1,0:T(8,128)S(1)}, u32[]{:S(2)}, u32[]{:S(2)}) collective-permute-start(f32[8,128]{1,0:T(8,128)S(1)} %get-tuple-element.39.refs_7_), channel_id=1, source_target_pairs={{0,1},{1,0},{2,3},{3,2},{4,5},{5,4},{6,7},{7,6},{8,9},{9,8},{10,11... | collective-permute-start | bytes 12296 | tf_op jit(solution)/shard_map/ppermute | solution.py:461
  78.2 10.1 %collective-permute-start.16 = (bf16[2,256,256]{2,1,0:T(8,128)(2,1)S(1)}, bf16[2,256,256]{2,1,0:T(8,128)(2,1)S(1)}, u32[]{:S(2)}, u32[]{:S(2)}) collective-permute-start(bf16[2,256,256]{2,1,0:T(8,128)(2,1)S(1)} %add_convert_fusion.4), channel_id=1, source_target_pairs={{0,7},{1,2},{2,1},{3,4},{4,3},{5,6},{6,5},{7,0},{8,15},{9,10},{10,... | collective-permute-start | bytes 786440 | tf_op jit(solution)/shard_map/ppermute | solution.py:461
  79.9 11.1 %collective-permute-start.20 = (bf16[2,256,256]{2,1,0:T(8,128)(2,1)S(1)}, bf16[2,256,256]{2,1,0:T(8,128)(2,1)S(1)}, u32[]{:S(2)}, u32[]{:S(2)}) collective-permute-start(bf16[2,256,256]{2,1,0:T(8,128)(2,1)S(1)} %add_convert_fusion.1), channel_id=1, source_target_pairs={{0,1},{1,0},{2,3},{3,2},{4,5},{5,4},{6,7},{7,6},{8,9},{9,8},{10,11... | collective-permute-start | bytes 786440 | tf_op jit(solution)/shard_map/ppermute | solution.py:461
  88.4 11.7 %collective-permute-start.17 = (bf16[2,256,256]{2,1,0:T(8,128)(2,1)S(1)}, bf16[2,256,256]{2,1,0:T(8,128)(2,1)S(1)}, u32[]{:S(2)}, u32[]{:S(2)}) collective-permute-start(bf16[2,256,256]{2,1,0:T(8,128)(2,1)S(1)} %add_convert_fusion.3), channel_id=1, source_target_pairs={{0,1},{1,0},{2,3},{3,2},{4,5},{5,4},{6,7},{7,6},{8,9},{9,8},{10,11... | collective-permute-start | bytes 786440 | tf_op jit(solution)/shard_map/ppermute | solution.py:461
  91.1 10.7 %collective-permute-start.21 = (bf16[2,256,256]{2,1,0:T(8,128)(2,1)S(1)}, bf16[2,256,256]{2,1,0:T(8,128)(2,1)S(1)}, u32[]{:S(2)}, u32[]{:S(2)}) collective-permute-start(bf16[2,256,256]{2,1,0:T(8,128)(2,1)S(1)} %add_convert_fusion), channel_id=1, source_target_pairs={{0,7},{1,2},{2,1},{3,4},{4,3},{5,6},{6,5},{7,0},{8,15},{9,10},{10,... | collective-permute-start | bytes 786440 | tf_op jit(solution)/shard_map/ppermute | solution.py:461
  91.2 11.2 %collective-permute-start.25 = (f32[8,128]{1,0:T(8,128)S(1)}, f32[8,128]{1,0:T(8,128)S(1)}, u32[]{:S(2)}, u32[]{:S(2)}) collective-permute-start(f32[8,128]{1,0:T(8,128)S(1)} %get-tuple-element.51), channel_id=1, source_target_pairs={{0,36},{1,37},{2,38},{3,39},{4,32},{5,33},{6,34},{7,35},{8,44},{9,... | collective-permute-start | bytes 12296 | tf_op jit(solution)/shard_map/ppermute | solution.py:461
  96.1 6.3 %collective-permute-start.24 = (f32[8,128]{1,0:T(8,128)S(1)}, f32[8,128]{1,0:T(8,128)S(1)}, u32[]{:S(2)}, u32[]{:S(2)}) collective-permute-start(f32[8,128]{1,0:T(8,128)S(1)} %get-tuple-element.51), channel_id=1, source_target_pairs={{0,32},{1,33},{2,34},{3,35},{4,36},{5,37},{6,38},{7,39},{8,40},{9,... | collective-permute-start | bytes 12296 | tf_op jit(solution)/shard_map/ppermute | solution.py:461
  97.8 7.5 %collective-permute-start.23 = (f32[8,128]{1,0:T(8,128)S(1)}, f32[8,128]{1,0:T(8,128)S(1)}, u32[]{:S(2)}, u32[]{:S(2)}) collective-permute-start(f32[8,128]{1,0:T(8,128)S(1)} %get-tuple-element.51), channel_id=1, source_target_pairs={{0,4},{1,5},{2,6},{3,7},{4,0},{5,1},{6,2},{7,3},{8,12},{9,13},{10,... | collective-permute-start | bytes 12296 | tf_op jit(solution)/shard_map/ppermute | solution.py:461
  100.1 16.5 %collective-permute-start.14 = (bf16[1792,128]{1,0:T(8,128)(2,1)S(1)}, bf16[1792,128]{1,0:T(8,128)(2,1)S(1)}, u32[]{:S(2)}, u32[]{:S(2)}) collective-permute-start(bf16[1792,128]{1,0:T(8,128)(2,1)S(1)} %get-tuple-element.42), channel_id=1, source_target_pairs={{0,8},{1,9},{2,10},{3,11},{4,12},{5,13},{6,14},{7,15},{8,0},{9,1},... | collective-permute-start | bytes 1376264 | tf_op jit(solution)/shard_map/ppermute | solution.py:461
  101.8 14.8 %collective-permute-start.22 = (bf16[256,256]{1,0:T(8,128)(2,1)S(1)}, bf16[256,256]{1,0:T(8,128)(2,1)S(1)}, u32[]{:S(2)}, u32[]{:S(2)}) collective-permute-start(bf16[256,256]{1,0:T(8,128)(2,1)S(1)} %get-tuple-element.56), channel_id=1, source_target_pairs={{0,8},{1,9},{2,10},{3,11},{4,12},{5,13},{6,14},{7,15},{8,0},{9,1},... | collective-permute-start | bytes 393224 | tf_op jit(solution)/shard_map/ppermute | solution.py:461
  105.3 7.8 %collective-permute-start.28 = (f32[8,128]{1,0:T(8,128)S(1)}, f32[8,128]{1,0:T(8,128)S(1)}, u32[]{:S(2)}, u32[]{:S(2)}) collective-permute-start(f32[8,128]{1,0:T(8,128)S(1)} %add_add_fusion.refs_0_), channel_id=1, source_target_pairs={{0,192},{1,193},{2,194},{3,195},{4,196},{5,197},{6,198},{7,199},{8... | collective-permute-start | bytes 12296 | tf_op jit(solution)/shard_map/ppermute | solution.py:461
  111.5 5.1 %collective-permute-start.27 = (f32[8,128]{1,0:T(8,128)S(1)}, f32[8,128]{1,0:T(8,128)S(1)}, u32[]{:S(2)}, u32[]{:S(2)}) collective-permute-start(f32[8,128]{1,0:T(8,128)S(1)} %add_add_fusion.refs_0_), channel_id=1, source_target_pairs={{0,128},{1,129},{2,130},{3,131},{4,132},{5,133},{6,134},{7,135},{8... | collective-permute-start | bytes 12296 | tf_op jit(solution)/shard_map/ppermute | solution.py:461
  112.1 4.5 %collective-permute-start.26 = (f32[8,128]{1,0:T(8,128)S(1)}, f32[8,128]{1,0:T(8,128)S(1)}, u32[]{:S(2)}, u32[]{:S(2)}) collective-permute-start(f32[8,128]{1,0:T(8,128)S(1)} %add_add_fusion.refs_0_), channel_id=1, source_target_pairs={{0,64},{1,65},{2,66},{3,67},{4,68},{5,69},{6,70},{7,71},{8,72},{9,... | collective-permute-start | bytes 12296 | tf_op jit(solution)/shard_map/ppermute | solution.py:461

commit v3 on v2

--- a/solution.py
+++ b/solution.py
@@ -86,16 +86,22 @@
     out_ref[1] = got_ref[...]
 
 
-def finish_body(count, x_ref, keep_ref, got_ref, own_ref, other_ref, *refs):
-    scale_refs = refs[:count]
-    query_out, key_out, value_out, scale_out = refs[count:]
+def finish_body(
+    x_ref,
+    keep_ref,
+    got_ref,
+    own_ref,
+    other_ref,
+    *refs,
+):
+    scale_refs, (query_out, key_out, value_out, scale_out) = refs[:4], refs[4:]
     x = x_ref[0]
-    scale = sum([ref[0:1, :] for ref in scale_refs[1:]], scale_refs[0][0:1, :])
-    scale_out[...] = scale[:, : 2 * HEADS]
+    scale = four([ref[...] for ref in scale_refs])
+    scale_out[...] = scale[0:1, : 2 * HEADS]
     for ref, half in ((own_ref, x), (other_ref, 1 - x)):
         at = pl.multiple_of(half * KV_HEADS * HEAD, KV_HEADS * HEAD)
         key_out[:, pl.ds(at, KV_HEADS * HEAD)] = ref[:ROWS, :]
-        value_out[:, pl.ds(at, KV_HEADS * HEAD)] = ref[ROWS:, :]
+        value_out[:, pl.ds(at, KV_HEADS * HEAD)] = ref[ROWS : 2 * ROWS, :]
     for ref, half in ((keep_ref, x), (got_ref, 1 - x)):
         for head in range(HEADS):
             at = pl.multiple_of(half * HEADS * HEAD + head * HEAD, HEAD)
@@ -115,7 +121,76 @@
     return rows, tops, first
 
 
-def place(blocks, first, top, key_c, value_c, pos_c, turned):
+def four(parts):
+    return (parts[0] + parts[1]) + (parts[2] + parts[3])
+
+
+def code(value):
+    high = value.astype(BF16)
+    value = value - high.astype(F32)
+    middle = value.astype(BF16)
+    return [high, middle, (value - middle.astype(F32)).astype(BF16)]
+
+
+def put_scale(ref, scale):
+    for number, part in enumerate(code(scale)):
+        lanes = slice(0, ROWS) if number < 2 else slice(ROWS, 2 * ROWS)
+        rows = jnp.concatenate([part] * 2, axis=0)
+        at = 2 * ROWS + (number % 2) * 16
+        ref[at : at + 16, lanes] = rows
+    ref[2 * ROWS + 16 : 2 * ROWS + 32, ROWS : 2 * ROWS] = jnp.zeros((16, ROWS), BF16)
+
+
+def get_scale(ref):
+    at = 2 * ROWS
+    high = ref[at : at + 16, :ROWS].astype(F32)
+    middle = ref[at + 16 : at + 32, :ROWS].astype(F32)
+    low = ref[at : at + 16, ROWS:].astype(F32)
+    return ((high + middle) + low)[0:8]
+
+
+def hop_body(step, count, *refs):
+    part_a, part_b, sent_a = refs[:3]
+    refs = refs[3:]
+    if step < 3:
+        sent_b, refs = refs[0], refs[1:]
+    scale_refs, (to_a, to_b, scale_out) = refs[:count], refs[count:]
+    plain = slice(0, 2 * ROWS)
+    for slot in range(2):
+        first = part_a[slot]
+        if step < 3:
+            first = first + sent_b[slot, plain, :].astype(F32)
+        to_a[slot, plain, :] = first.astype(BF16)
+        second = part_b[slot] + sent_a[slot, plain, :].astype(F32)
+        to_b[slot, plain, :] = second.astype(BF16)
+    parts = [ref[...] for ref in scale_refs]
+    if step == 3:
+        scale = four(parts)
+        put_scale(to_a.at[0], scale)
+        put_scale(to_b.at[0], scale)
+    elif step == 2:
+        other = get_scale(sent_b.at[0])
+        scale = get_scale(sent_a.at[0]) + other
+        put_scale(to_a.at[0], other)
+        put_scale(to_b.at[0], other)
+    else:
+        scale = (parts[0] + get_scale(sent_a.at[0])) + parts[1]
+    if step > 1:
+        for ref in (to_a, to_b):
+            ref[1, 2 * ROWS :, :] = jnp.zeros((32, 2 * ROWS), BF16)
+    scale_out[...] = scale
+
+
+def last_hop_body(near, sent_a, sent_b, *refs):
+    scale_refs, (ours, theirs, scale_out) = refs[:4], refs[4:]
+    first = near[0] + sent_a[0].astype(F32) + sent_b[0].astype(F32)
+    ours[...] = first.astype(BF16)
+    second = near[1] + sent_a[1].astype(F32) + sent_b[1].astype(F32)
+    theirs[...] = second.astype(BF16)
+    scale_out[...] = four([ref[...] for ref in scale_refs])
+
+
+def place(blocks, first, top, key_c, value_c, pos_c):
     start = jnp.int32(0)
     entries = []
     for phase in range(2):
@@ -125,34 +200,39 @@
         counts = [jnp.sum(jnp.where(row < FAR, 1.0, 0.0)).astype(jnp.int32) for row in rows]
         counts = [jnp.where(begin <= top, n, 0) for begin, n in zip(begins, counts)]
         spans = [(n + 15) >> 4 for n in counts]
+        def put(number, at, slot=slot, rows=rows):
+            ref = blocks[number]
+            target = pl.ds(pl.multiple_of(at, 16), ROWS)
+            pos_c[target, :] = jnp.broadcast_to(rows[number], (ROWS, ROWS)).T
+            for g in range(KV_HEADS):
+                lanes = slice(g * HEAD, (g + 1) * HEAD)
+                key_c[g, target, :] = ref[slot, POS : POS + ROWS, lanes]
+                value_c[g, target, :] = ref[slot, POS + ROWS : MESSAGE, lanes]
+
         if len(blocks) == 2:
             ahead = begins[0] < begins[1]
             starts = [
                 start + jnp.where(ahead, 0, spans[1] * 16),
                 start + jnp.where(ahead, spans[0] * 16, 0),
             ]
+
+            @pl.when(ahead)
+            def _():
+                put(0, starts[0])
+                put(1, starts[1])
+
+            @pl.when(jnp.logical_not(ahead))
+            def _():
+                put(1, starts[1])
+                put(0, starts[0])
+
         else:
             starts = []
             total = start
-            for span in spans:
+            for number, span in enumerate(spans):
                 starts.append(total)
+                put(number, total)
                 total = total + span * 16
-        for ref, row, at, span in zip(blocks, rows, starts, spans):
-            turned[...] = jnp.broadcast_to(row, (ROWS, ROWS)).T
-
-            def chunk(step, _, ref=ref, at=at, slot=slot):
-                source = pl.multiple_of(step * 16, 16)
-                target = pl.multiple_of(at + step * 16, 16)
-                pos_c[pl.ds(target, 16), :] = turned[pl.ds(source, 16), :]
-                for g in range(KV_HEADS):
-                    lanes = slice(g * HEAD, (g + 1) * HEAD)
-                    key_c[g, pl.ds(target, 16), :] = ref[slot, pl.ds(POS + source, 16), lanes]
-                    value_c[g, pl.ds(target, 16), :] = ref[
-                        slot, pl.ds(POS + ROWS + source, 16), lanes
-                    ]
-                return 0
-
-            lax.fori_loop(0, span, chunk, 0)
         entries.append((slot, starts, counts))
         start = start + sum(spans) * 16
     rest = pl.ds(pl.multiple_of(start, 16), TILE)
@@ -200,9 +280,10 @@
     if not is_first:
         prior_ref, refs = refs[0], refs[1:]
     if is_last:
-        final_ref, scale_ref, state, key_c, value_c, pos_c, turned = refs
+        final_ref, scale_ref, state, key_c, value_c, pos_c = refs
     else:
-        state, key_c, value_c, pos_c, turned = refs
+        state, token_ref, key_c, value_c, pos_c = refs
+        token_ref[...] = jnp.zeros_like(token_ref)
     query_rows, tops, first = query_side(own_ref)
     if is_first:
         state[...] = jnp.zeros_like(state)
@@ -211,7 +292,7 @@
         state[...] = prior_ref[...]
     for blocks, slots in work:
         top = jnp.maximum(tops[0], tops[1]) if len(slots) == 2 else tops[slots[0]]
-        length, _ = place(blocks, first, top, key_c, value_c, pos_c, turned)
+        length, _ = place(blocks, first, top, key_c, value_c, pos_c)
 
         def tile(step, _, slots=slots):
             at = pl.multiple_of(step * TILE, TILE)
@@ -305,23 +386,19 @@
     query_sum[slot * KV_HEADS + g] += product(keys, score_low, TN)
 
 
-def grads_body(count, added, is_first, is_last, *refs):
+def grads_body(count, is_first, is_last, *refs):
     rate_ref, own_ref, kept_ref, got_ref, final_ref = refs[:5]
     blocks = refs[5 : 5 + count]
     refs = refs[5 + count :]
-    scale_refs, refs = refs[:added], refs[added:]
     if not is_first:
         prior_ref, refs = refs[0], refs[1:]
     outs, refs = refs[:count], refs[count:]
-    if added:
-        scale_ref, refs = refs[0], refs[1:]
-        scale_ref[...] = sum([ref[...] for ref in scale_refs[1:]], scale_refs[0][...])
     if is_last:
         query_outs, refs = refs[:2], refs[2:]
-    query_sum, key_c, value_c, pos_c, turned, key_sum, value_sum = refs
+    query_sum, key_c, value_c, pos_c, key_sum, value_sum = refs
     query_rows, tops, first = query_side(own_ref)
     length, entries = place(
-        blocks, first, jnp.maximum(tops[0], tops[1]), key_c, value_c, pos_c, turned
+        blocks, first, jnp.maximum(tops[0], tops[1]), key_c, value_c, pos_c
     )
     if is_first:
         query_sum[...] = jnp.zeros_like(query_sum)
@@ -381,16 +458,16 @@
 
 
 def compact_scratch(count):
-    size = (2 * count + 1) * ROWS
+    size = 2 * count * ROWS + TILE
     return [
         pltpu.VMEM((KV_HEADS, size, HEAD), BF16),
         pltpu.VMEM((KV_HEADS, size, HEAD), BF16),
         pltpu.VMEM((size, ROWS), F32),
-        pltpu.VMEM((ROWS, ROWS), F32),
     ]
 
 
 STATE = jax.ShapeDtypeStruct((2 * KV_HEADS, 5, 8, WIDE), F32)
+SMALL = jax.ShapeDtypeStruct((8, ROWS), F32)
 FINAL = jax.ShapeDtypeStruct((2 * KV_HEADS, 8, WIDE), F32)
 
 
@@ -399,7 +476,7 @@
         outs = [FINAL, jax.ShapeDtypeStruct((8, ROWS), F32)]
         scratch = [pltpu.VMEM(STATE.shape, F32)]
     else:
-        outs, scratch = [STATE], []
+        outs, scratch = [STATE, SMALL], []
     blocks = [block for some, _ in jobs for block in some]
     operands = [rate, own, kept, got, *blocks] + ([] if prior is None else [prior])
     sizes = [(len(some), slots) for some, slots in jobs]
@@ -413,27 +490,25 @@
     )(*operands)
 
 
-def grads(rate, own, kept, got, final, blocks, scales=(), prior=None, is_last=False):
+def grads(rate, own, kept, got, final, blocks, prior=None, is_last=False):
     count = len(blocks)
     outs = [jax.ShapeDtypeStruct((2, 2 * ROWS, KV_HEADS * HEAD), F32)] * count
     sums = jax.ShapeDtypeStruct((2 * KV_HEADS, HEAD, WIDE), F32)
-    operands = [rate, own, kept, got, final, *blocks, *scales]
+    operands = [rate, own, kept, got, final, *blocks]
     operands = operands + ([] if prior is None else [prior])
-    if scales:
-        outs = outs + [jax.ShapeDtypeStruct((8, ROWS), F32)]
     if is_last:
         outs = outs + [jax.ShapeDtypeStruct((HEADS * ROWS, HEAD), BF16)] * 2
         scratch = [pltpu.VMEM(sums.shape, F32)]
     else:
         outs, scratch = outs + [sums], []
-    size = (2 * count + 1) * ROWS
+    size = 2 * count * ROWS + TILE
     scratch = (
         scratch
         + compact_scratch(count)
         + [pltpu.VMEM((KV_HEADS, size, HEAD), F32), pltpu.VMEM((KV_HEADS, size, HEAD), F32)]
     )
     return call(
-        functools.partial(grads_body, count, len(scales), prior is None, is_last),
+        functools.partial(grads_body, count, prior is None, is_last),
         outs,
         scratch,
         count * 2 * ROWS * 2 * HEADS * ROWS * 2 * HEAD * 5,
@@ -463,6 +538,7 @@
     smem = pl.BlockSpec(memory_space=pltpu.SMEM)
     vmem = pl.BlockSpec(memory_space=pltpu.VMEM)
     anywhere = pl.BlockSpec(memory_space=pl.ANY)
+    in_hbm = pl.BlockSpec(memory_space=pltpu.HBM)
     width = KV_HEADS * HEAD
     message = jax.ShapeDtypeStruct((MESSAGE, width), BF16)
     keys_kept, keys_sent = call(
@@ -476,7 +552,7 @@
         ],
         1024,
         1 << 20,
-        [smem, anywhere, anywhere, anywhere],
+        [smem, in_hbm, in_hbm, in_hbm],
     )(x_ref, keys[0], values[0], routes)
     keys_got = swap(keys_sent, across)
     work = jax.ShapeDtypeStruct((2, HEADS * ROWS, HEAD), BF16)
@@ -490,7 +566,7 @@
         ],
         1024,
         4 << 20,
-        [smem, anywhere, anywhere, anywhere],
+        [smem, anywhere, in_hbm, in_hbm],
     )(x_ref, keys_sent, queries[0], out_grad[0])
     got = swap(sent, across)
     own = call(
@@ -506,17 +582,36 @@
     rate = jnp.repeat(half_scale * (LOG2E / math.sqrt(HEAD)), ROWS).reshape(KV_HEADS, 1, WIDE)
     rate = jnp.broadcast_to(rate, (KV_HEADS, 8, WIDE))
 
+    def gate(blocks, after):
+        def body(*refs):
+            for source, target in zip(refs, refs[len(blocks) + 1 :]):
+                target[...] = source[...]
+
+        return call(
+            body,
+            [jax.ShapeDtypeStruct(block.shape, block.dtype) for block in blocks],
+            [],
+            1024,
+            1 << 20,
+            [vmem] * (len(blocks) + 1),
+        )(*blocks, after)
+
     a, b = [own], [own]
-    for step in range(1, 4):
-        a.append(swap(b[step - 1], even))
-        b.append(swap(a[step - 1], odd))
+    a.append(swap(own, even))
+    b.append(swap(own, odd))
+    state, token = stats(rate, own, kept, kept, [([own], (0,))])
+    a[1], b[1] = gate([a[1], b[1]], token)
+    a.append(swap(b[1], even))
+    b.append(swap(a[1], odd))
+    state, token = stats(rate, own, kept, kept, [([a[1], b[1]], (0,))], state)
+    a[2], b[2] = gate([a[2], b[2]], token)
+    a.append(swap(b[2], even))
+    b.append(swap(a[2], odd))
+    state, token = stats(rate, own, kept, kept, [([a[2], b[2]], (0,))], state)
+    a[3], b[3] = gate([a[3], b[3]], token)
     a.append(swap(b[3], even))
-
-    (state,) = stats(rate, own, kept, kept, [([own, a[1], b[1]], (0,))])
-    (state,) = stats(
-        rate, own, kept, got, [([own, a[1], b[1]], (1,)), ([a[2], b[2]], (0, 1))], state
-    )
-    (state,) = stats(rate, own, kept, got, [([a[3], b[3]], (0, 1))], state)
+    jobs = [([own, a[1], b[1], a[2], b[2]], (1,)), ([a[3], b[3]], (0, 1))]
+    state, token = stats(rate, own, kept, got, jobs, state)
     final, scale = stats(rate, own, kept, got, [([a[4]], (0, 1))], state, is_last=True)
 
     total_devices = lax.axis_size("dp") * size
@@ -525,36 +620,45 @@
         pairs = [[(i, i ^ mask) for i in range(total_devices)] for mask in masks]
         return [array] + [swap(array, pair, ("dp", "ctx")) for pair in pairs]
 
-    scales = exchange(scale, (8,))
+    def hop(step, parts, arrived, scales=()):
+        out = jax.ShapeDtypeStruct((2, 2 * ROWS + (32 if step > 1 else 0), width), BF16)
+        return call(
+            functools.partial(hop_body, step, len(scales)),
+            [out, out, SMALL],
+            [],
+            1024,
+            2 << 20,
+            [vmem] * (2 + len(arrived) + len(scales)),
+        )(*parts, *arrived, *scales)
+
+    scales = exchange(scale, (4, 8, 12))
     far, sums = grads(rate, own, kept, got, final, [a[4]])
     from_even = swap(far.astype(BF16), even)
-    part_a, part_b, scale, sums = grads(
-        rate, own, kept, got, final, [a[3], b[3]], scales, sums
-    )
-    scales = exchange(scale, (16,))
-    sent_a = swap(part_a.astype(BF16), even)
-    sent_b = swap((part_b + from_even).astype(BF16), odd)
-    part_a, part_b, near, scale, sums = grads(
-        rate, own, kept, got, final, [a[2], b[2], own], scales, sums
-    )
-    scales = exchange(scale, (1, 2, 3))
-    to_a = (part_a + sent_b).astype(BF16)
-    to_b = (part_b + sent_a).astype(BF16)
+    part_a, part_b, sums = grads(rate, own, kept, got, final, [a[3], b[3]], sums)
+    to_a, to_b, scale = hop(3, (part_a, part_b), (from_even,), scales)
     sent_a, sent_b = swap(to_a, even), swap(to_b, odd)
-    part_a, part_b, scale, query_kept, query_sent = grads(
-        rate, own, kept, got, final, [a[1], b[1]], scales, sums, is_last=True
+    part_a, part_b, near, sums = grads(rate, own, kept, got, final, [a[2], b[2], own], sums)
+    to_a, to_b, beside = hop(2, (part_a, part_b), (sent_a, sent_b))
+    sent_a, sent_b = swap(to_a, even), swap(to_b, odd)
+    part_a, part_b, query_kept, query_sent = grads(
+        rate, own, kept, got, final, [a[1], b[1]], sums, is_last=True
     )
     query_got = swap(query_sent, across)
-    scales = exchange(scale, (4, 32, 36))
-    to_a = (part_a + sent_b).astype(BF16)
-    to_b = (part_b + sent_a).astype(BF16)
+    to_a, to_b, scale = hop(1, (part_a, part_b), (sent_a, sent_b), [scale, beside])
     sent_a, sent_b = swap(to_a, even), swap(to_b, odd)
-    scales = exchange(sum(scales[1:], scales[0]), (64, 128, 192))
-    ours = (near[0] + sent_a[0] + sent_b[0]).astype(BF16)
-    theirs = (near[1] + sent_a[1] + sent_b[1]).astype(BF16)
+    scales = exchange(scale, (64, 128, 192))
+    ours, theirs, scale = call(
+        last_hop_body,
+        [jax.ShapeDtypeStruct((2 * ROWS, width), BF16)] * 2 + [SMALL],
+        [],
+        1024,
+        2 << 20,
+        [vmem] * 7,
+    )(near, sent_a, sent_b, *scales)
     other = swap(theirs, across)
+    scales = exchange(scale, (16, 32, 48))
     query_out, key_out, value_out, scale_out = call(
-        functools.partial(finish_body, len(scales)),
+        finish_body,
         [
             jax.ShapeDtypeStruct((ROWS, 2 * HEADS * HEAD), BF16),
             jax.ShapeDtypeStruct((ROWS, 2 * width), BF16),
@@ -564,7 +668,7 @@
         [],
         1024,
         2 << 20,
-        [smem] + [vmem] * (4 + len(scales)),
+        [smem] + [vmem] * 8,
     )(x_ref, query_kept, query_got, ours, other, *scales)
     return query_out[None], key_out[None], value_out[None], scale_out.reshape(2 * HEADS)
 

time: 119 us -> 113 us (0.950)
  the two profiles are of different devices: /device:TPU:38 before, /device:TPU:1 now
where the time goes in v3:
time: 113 us
  starting transfers between devices  53.4 us (47%)
  waiting for transfers between devices  27.9 us (25%)
  Pallas kernels  25.3 us (22%)
  local copies, waits for them, and re-layouts  4.99 us (4%)
    ppermute x27, starting transfers between devices, swap(): return lax.ppermute(array, axis, pairs)  53.4 us
    ppermute x27, waiting for transfers between devices, swap(): return lax.ppermute(array, axis, pairs)  27.9 us
    pallas_call x4, Pallas kernels, grads(): call(functools.partial(grads_body, count, prior is None, is_last), outs,...  11.6 us
    pallas_call x5, Pallas kernels, stats(): call(functools.partial(stats_body, sizes, prior is None, is_last), outs,...  9.79 us
    unnamed x14, local copies, waits for them, and re-layouts  4.9 us
  transfers between devices with their start and end apart: 27, of which 13 were waited for; matrix products, arithmetic and copies ran while one was open for 0% of the time, Pallas kernels for 18%

profile of v3, /device:TPU:1, one launch (start us, length us, event | category | flops | bytes accessed | tf_op | source)
XLA Modules:
  0.0 112.6 jit_solution(4570097662948223269)
XLA Ops:
  0.7 0.9 copy-done.2
  1.6 0.9 copy-done.3
  2.5 0.7 copy-done.4
  3.1 0.4 shard_map.93
  3.5 2.1 %collective-permute-start = (bf16[272,256]{1,0:T(8,128)(2,1)S(1)}, bf16[272,256]{1,0:T(8,128)(2,1)S(1)}, u32[]{:S(2)}, u32[]{:S(2)}) collective-permute-start(bf16[272,256]{1,0:T(8,128)(2,1)S(1)} %get-tuple-element.52.after_ref), channel_id=1, source_target_pairs={{0,8},{1,9},{2,10},{3,11},{4,12},{5,13},{6,14},{7,15},{8,0},{9,1},... | collective-permute-start | bytes 417800 | tf_op jit(solution)/shard_map/ppermute | solution.py:536
  5.6 1.2 %copy-done = bf16[1,128,3584]{2,1,0:T(8,128)(2,1)S(1)} copy-done((bf16[1,128,3584]{2,1,0:T(8,128)(2,1)S(1)}, bf16[1,128,3584]{2,1,0:T(8,128)(2,1)}, u32[]{:S(2)}) %copy-start) | copy-done | bytes 917528
  6.8 1.2 %copy-done.1 = bf16[1,128,3584]{2,1,0:T(8,128)(2,1)S(1)} copy-done((bf16[1,128,3584]{2,1,0:T(8,128)(2,1)S(1)}, bf16[1,128,3584]{2,1,0:T(8,128)(2,1)}, u32[]{:S(2)}) %copy-start.1) | copy-done | bytes 917528
  8.0 1.7 %shard_map.94 = (bf16[2,1792,128]{2,1,0:T(8,128)(2,1)S(1)}, bf16[2,1792,128]{2,1,0:T(8,128)(2,1)}) custom-call(s32[1]{0:T(128)} %bitcast.x_ref, bf16[272,256]{1,0:T(8,128)(2,1)S(1)} %get-tuple-element.52.after_ref, bf16[128,3584]{1,0:T(8,128)(2,1)S(1)} %bitcast.14, bf16[128,3584]{1,0:T(8,128)(2,1)S(1)} %bitcast.15), custom_call_target="tpu_custom_call" | custom-call | flops 1024 | bytes 4194304 | tf_op jit(solution)/shard_map/pallas_call | solution.py:559
  9.7 0.1 collective-permute-start.1
  9.8 0.0 collective-permute-done.got_ref
  9.8 5.9 %collective-permute-start.3 = (bf16[2,272,256]{2,1,0:T(8,128)(2,1)S(1)}, bf16[2,272,256]{2,1,0:T(8,128)(2,1)S(1)}, u32[]{:S(2)}, u32[]{:S(2)}) collective-permute-start(bf16[2,272,256]{2,1,0:T(8,128)(2,1)S(1)} %shard_map.95.refs_1_.refs_4_.refs_7_), channel_id=1, source_target_pairs={{0,7},{1,2},{2,1},{3,4},{4,3},{5,6},{6,5},{7,0},{8,15},{9,10},{10,... | collective-permute-start | bytes 835592 | tf_op jit(solution)/shard_map/ppermute | solution.py:536
  15.7 0.0 collective-permute-start.2
  15.7 0.1 dynamic-slice_multiply_fusion
  15.8 0.1 broadcast_in_dim.21
  15.9 0.1 broadcast_bitcast_fusion
  16.0 1.0 shard_map.96
  17.0 4.4 %collective-permute-done.3.refs_1_ = bf16[2,272,256]{2,1,0:T(8,128)(2,1)S(1)} collective-permute-done((bf16[2,272,256]{2,1,0:T(8,128)(2,1)S(1)}, bf16[2,272,256]{2,1,0:T(8,128)(2,1)S(1)}, u32[]{:S(2)}, u32[]{:S(2)}) %collective-permute-start.3) | collective-permute-done | bytes 278560 | tf_op jit(solution)/shard_map/ppermute | solution.py:536
  21.5 0.9 collective-permute-done.2.refs_0_
  22.4 0.4 collective-permute-start.4
  22.8 1.3 %collective-permute-start.5 = (bf16[2,272,256]{2,1,0:T(8,128)(2,1)S(1)}, bf16[2,272,256]{2,1,0:T(8,128)(2,1)S(1)}, u32[]{:S(2)}, u32[]{:S(2)}) collective-permute-start(bf16[2,272,256]{2,1,0:T(8,128)(2,1)S(1)} %get-tuple-element.58.refs_4_.refs_5_), channel_id=1, source_target_pairs={{0,7},{1,2},{2,1},{3,4},{4,3},{5,6},{6,5},{7,0},{8,15},{9,10},{10,... | collective-permute-start | bytes 835592 | tf_op jit(solution)/shard_map/ppermute | solution.py:536
  24.1 0.6 shard_map.98
  24.7 3.5 %collective-permute-done.4.refs_0_ = bf16[2,272,256]{2,1,0:T(8,128)(2,1)S(1)} collective-permute-done((bf16[2,272,256]{2,1,0:T(8,128)(2,1)S(1)}, bf16[2,272,256]{2,1,0:T(8,128)(2,1)S(1)}, u32[]{:S(2)}, u32[]{:S(2)}) %collective-permute-start.4) | collective-permute-done | bytes 278560 | tf_op jit(solution)/shard_map/ppermute | solution.py:536
  28.2 1.5 %collective-permute-done.5.refs_1_ = bf16[2,272,256]{2,1,0:T(8,128)(2,1)S(1)} collective-permute-done((bf16[2,272,256]{2,1,0:T(8,128)(2,1)S(1)}, bf16[2,272,256]{2,1,0:T(8,128)(2,1)S(1)}, u32[]{:S(2)}, u32[]{:S(2)}) %collective-permute-start.5) | collective-permute-done | bytes 278560 | tf_op jit(solution)/shard_map/ppermute | solution.py:536
  29.7 0.1 collective-permute-start.6
  29.8 1.5 %collective-permute-start.7 = (bf16[2,272,256]{2,1,0:T(8,128)(2,1)S(1)}, bf16[2,272,256]{2,1,0:T(8,128)(2,1)S(1)}, u32[]{:S(2)}, u32[]{:S(2)}) collective-permute-start(bf16[2,272,256]{2,1,0:T(8,128)(2,1)S(1)} %get-tuple-element.62.refs_4_.refs_7_.refs_5_), channel_id=1, source_target_pairs={{0,7},{1,2},{2,1},{3,4},{4,3},{5,6},{6,5},{7,0},{8,15},{9,10},{10,... | collective-permute-start | bytes 835592 | tf_op jit(solution)/shard_map/ppermute | solution.py:536
  31.3 0.6 shard_map.100
  31.9 3.3 %collective-permute-done.6.refs_0_ = bf16[2,272,256]{2,1,0:T(8,128)(2,1)S(1)} collective-permute-done((bf16[2,272,256]{2,1,0:T(8,128)(2,1)S(1)}, bf16[2,272,256]{2,1,0:T(8,128)(2,1)S(1)}, u32[]{:S(2)}, u32[]{:S(2)}) %collective-permute-start.6) | collective-permute-done | bytes 278560 | tf_op jit(solution)/shard_map/ppermute | solution.py:536
  35.2 1.3 %collective-permute-done.7.refs_1_ = bf16[2,272,256]{2,1,0:T(8,128)(2,1)S(1)} collective-permute-done((bf16[2,272,256]{2,1,0:T(8,128)(2,1)S(1)}, bf16[2,272,256]{2,1,0:T(8,128)(2,1)S(1)}, u32[]{:S(2)}, u32[]{:S(2)}) %collective-permute-start.7) | collective-permute-done | bytes 278560 | tf_op jit(solution)/shard_map/ppermute | solution.py:536
  36.6 0.5 collective-permute-start.8
  37.1 0.0 collective-permute-done.1.refs_3_
  37.1 6.0 %shard_map.102 = (f32[4,5,8,896]{3,2,1,0:T(8,128)S(1)}, f32[8,128]{1,0:T(8,128)}) custom-call(f32[2,8,896]{2,1,0:T(8,128)S(1)} %broadcast_in_dim.24.refs_0_, bf16[2,272,256]{2,1,0:T(8,128)(2,1)S(1)} %shard_map.95.refs_1_.refs_4_.refs_7_, bf16[2,1792,128]{2,1,0:T(8,128)(2,1)S(1)} %get-tuple-element.53.after_ref.refs_2_.refs_3_, ...), custom_call_target="tpu_custom_call" | custom-call | flops 2113929216 | bytes 4194304 | tf_op jit(solution)/shard_map/pallas_call | solution.py:483
  43.1 0.0 collective-permute-done.8.refs_4_.refs_5_
  43.1 1.5 %shard_map.103 = (f32[4,8,896]{2,1,0:T(8,128)S(1)}, f32[8,128]{1,0:T(8,128)S(1)}) custom-call(f32[2,8,896]{2,1,0:T(8,128)S(1)} %broadcast_in_dim.24.refs_0_, bf16[2,272,256]{2,1,0:T(8,128)(2,1)S(1)} %shard_map.95.refs_1_.refs_4_.refs_7_, bf16[2,1792,128]{2,1,0:T(8,128)(2,1)S(1)} %get-tuple-element.53.after_ref.refs_2_.refs_3_, ...), custom_call_target="tpu_custom_call" | custom-call | flops 469762048 | bytes 4194304 | tf_op jit(solution)/shard_map/pallas_call | solution.py:483
  44.7 1.4 %shard_map.104 = (f32[2,256,256]{2,1,0:T(8,128)S(1)}, f32[4,128,896]{2,1,0:T(8,128)S(1)}) custom-call(f32[2,8,896]{2,1,0:T(8,128)S(1)} %broadcast_in_dim.24.refs_0_, bf16[2,272,256]{2,1,0:T(8,128)(2,1)S(1)} %shard_map.95.refs_1_.refs_4_.refs_7_, bf16[2,1792,128]{2,1,0:T(8,128)(2,1)S(1)} %get-tuple-element.53.after_ref.refs_2_.refs_3_, ...), custom_call_target="tpu_custom_call" | custom-call | flops 1174405120 | bytes 6291456 | tf_op jit(solution)/shard_map/pallas_call | solution.py:510
  46.1 1.8 %collective-permute-start.10 = (bf16[2,256,256]{2,1,0:T(8,128)(2,1)S(1)}, bf16[2,256,256]{2,1,0:T(8,128)(2,1)S(1)}, u32[]{:S(2)}, u32[]{:S(2)}) collective-permute-start(bf16[2,256,256]{2,1,0:T(8,128)(2,1)S(1)} %convert_element_type.3), channel_id=1, source_target_pairs={{0,1},{1,0},{2,3},{3,2},{4,5},{5,4},{6,7},{7,6},{8,9},{9,8},{10,11... | collective-permute-start | bytes 786440 | tf_op jit(solution)/shard_map/ppermute | solution.py:536
  47.9 5.9 %collective-permute-start.13 = (f32[8,128]{1,0:T(8,128)S(1)}, f32[8,128]{1,0:T(8,128)S(1)}, u32[]{:S(2)}, u32[]{:S(2)}) collective-permute-start(f32[8,128]{1,0:T(8,128)S(1)} %get-tuple-element.83.refs_3_), channel_id=1, source_target_pairs={{0,12},{1,13},{2,14},{3,15},{4,8},{5,9},{6,10},{7,11},{8,4},{9,5},... | collective-permute-start | bytes 12296 | tf_op jit(solution)/shard_map/ppermute | solution.py:536
  53.9 2.4 %collective-permute-start.12 = (f32[8,128]{1,0:T(8,128)S(1)}, f32[8,128]{1,0:T(8,128)S(1)}, u32[]{:S(2)}, u32[]{:S(2)}) collective-permute-start(f32[8,128]{1,0:T(8,128)S(1)} %get-tuple-element.83.refs_3_), channel_id=1, source_target_pairs={{0,8},{1,9},{2,10},{3,11},{4,12},{5,13},{6,14},{7,15},{8,0},{9,1},... | collective-permute-start | bytes 12296 | tf_op jit(solution)/shard_map/ppermute | solution.py:536
  56.3 0.0 collective-permute-start.11
  56.3 2.8 %shard_map.105 = (f32[2,256,256]{2,1,0:T(8,128)S(1)}, f32[2,256,256]{2,1,0:T(8,128)S(1)}, f32[4,128,896]{2,1,0:T(8,128)S(1)}) custom-call(f32[2,8,896]{2,1,0:T(8,128)S(1)} %broadcast_in_dim.24.refs_0_, bf16[2,272,256]{2,1,0:T(8,128)(2,1)S(1)} %shard_map.95.refs_1_.refs_4_.refs_7_, bf16[2,1792,128]{2,1,0:T(8,128)(2,1)S(1)} %get-tuple-element.53.after_ref.refs_2_.refs_3_, ...), custom_call_target="tpu_custom_call" | custom-call | flops 2348810240 | bytes 6291456 | tf_op jit(solution)/shard_map/pallas_call | solution.py:510
  59.1 3.7 %collective-permute-done.11.refs_4_ = f32[8,128]{1,0:T(8,128)S(1)} collective-permute-done((f32[8,128]{1,0:T(8,128)S(1)}, f32[8,128]{1,0:T(8,128)S(1)}, u32[]{:S(2)}, u32[]{:S(2)}) %collective-permute-start.11) | collective-permute-done | bytes 4128 | tf_op jit(solution)/shard_map/ppermute | solution.py:536
  62.8 0.1 shard_map.108
  62.9 0.8 collective-permute-start.14
  63.6 4.4 %collective-permute-start.15 = (bf16[2,288,256]{2,1,0:T(8,128)(2,1)S(1)}, bf16[2,288,256]{2,1,0:T(8,128)(2,1)S(1)}, u32[]{:S(2)}, u32[]{:S(2)}) collective-permute-start(bf16[2,288,256]{2,1,0:T(8,128)(2,1)S(1)} %get-tuple-element.85), channel_id=1, source_target_pairs={{0,7},{1,2},{2,1},{3,4},{4,3},{5,6},{6,5},{7,0},{8,15},{9,10},{10,... | collective-permute-start | bytes 884744 | tf_op jit(solution)/shard_map/ppermute | solution.py:536
  68.1 4.5 %shard_map.106 = (f32[2,256,256]{2,1,0:T(8,128)S(1)}, f32[2,256,256]{2,1,0:T(8,128)S(1)}, f32[2,256,256]{2,1,0:T(8,128)S(1)}, f32[4,128,896]{2,1,0:T(8,128)S(1)}) custom-call(f32[2,8,896]{2,1,0:T(8,128)S(1)} %broadcast_in_dim.24.refs_0_, bf16[2,272,256]{2,1,0:T(8,128)(2,1)S(1)} %shard_map.95.refs_1_.refs_4_.refs_7_, ...), custom_call_target="tpu_custom_call" | custom-call | flops 3523215360 | bytes 6291456 | tf_op jit(solution)/shard_map/pallas_call | solution.py:510
  72.6 0.2 shard_map.109
  72.8 0.1 collective-permute-start.16
  72.9 3.0 %collective-permute-start.17 = (bf16[2,288,256]{2,1,0:T(8,128)(2,1)S(1)}, bf16[2,288,256]{2,1,0:T(8,128)(2,1)S(1)}, u32[]{:S(2)}, u32[]{:S(2)}) collective-permute-start(bf16[2,288,256]{2,1,0:T(8,128)(2,1)S(1)} %get-tuple-element.87), channel_id=1, source_target_pairs={{0,7},{1,2},{2,1},{3,4},{4,3},{5,6},{6,5},{7,0},{8,15},{9,10},{10,... | collective-permute-start | bytes 884744 | tf_op jit(solution)/shard_map/ppermute | solution.py:536
  75.9 3.0 %shard_map.107 = (f32[2,256,256]{2,1,0:T(8,128)S(1)}, f32[2,256,256]{2,1,0:T(8,128)S(1)}, bf16[1792,128]{1,0:T(8,128)(2,1)S(1)}, bf16[1792,128]{1,0:T(8,128)(2,1)S(1)}) custom-call(f32[2,8,896]{2,1,0:T(8,128)S(1)} %broadcast_in_dim.24.refs_0_, bf16[2,272,256]{2,1,0:T(8,128)(2,1)S(1)} %shard_map.95.refs_1_.refs_4_.refs_7_, ...), custom_call_target="tpu_custom_call" | custom-call | flops 2348810240 | bytes 6291456 | tf_op jit(solution)/shard_map/pallas_call | solution.py:510
  78.9 0.1 collective-permute-start.9
  79.0 1.7 %collective-permute-done.17.refs_3_ = bf16[2,288,256]{2,1,0:T(8,128)(2,1)S(1)} collective-permute-done((bf16[2,288,256]{2,1,0:T(8,128)(2,1)S(1)}, bf16[2,288,256]{2,1,0:T(8,128)(2,1)S(1)}, u32[]{:S(2)}, u32[]{:S(2)}) %collective-permute-start.17) | collective-permute-done | bytes 294944 | tf_op jit(solution)/shard_map/ppermute | solution.py:536
  80.7 0.1 shard_map.110
  80.8 0.1 collective-permute-start.18
  80.9 3.4 %collective-permute-start.19 = (bf16[2,256,256]{2,1,0:T(8,128)(2,1)S(1)}, bf16[2,256,256]{2,1,0:T(8,128)(2,1)S(1)}, u32[]{:S(2)}, u32[]{:S(2)}) collective-permute-start(bf16[2,256,256]{2,1,0:T(8,128)(2,1)S(1)} %get-tuple-element.91), channel_id=1, source_target_pairs={{0,7},{1,2},{2,1},{3,4},{4,3},{5,6},{6,5},{7,0},{8,15},{9,10},{10,... | collective-permute-start | bytes 786440 | tf_op jit(solution)/shard_map/ppermute | solution.py:536
  84.3 3.4 %collective-permute-start.22 = (f32[8,128]{1,0:T(8,128)S(1)}, f32[8,128]{1,0:T(8,128)S(1)}, u32[]{:S(2)}, u32[]{:S(2)}) collective-permute-start(f32[8,128]{1,0:T(8,128)S(1)} %get-tuple-element.92.refs_0_), channel_id=1, source_target_pairs={{0,192},{1,193},{2,194},{3,195},{4,196},{5,197},{6,198},{7,199},{8... | collective-permute-start | bytes 12296 | tf_op jit(solution)/shard_map/ppermute | solution.py:536
  87.7 1.3 %collective-permute-done.22.refs_3_ = f32[8,128]{1,0:T(8,128)S(1)} collective-permute-done((f32[8,128]{1,0:T(8,128)S(1)}, f32[8,128]{1,0:T(8,128)S(1)}, u32[]{:S(2)}, u32[]{:S(2)}) %collective-permute-start.22) | collective-permute-done | bytes 4128 | tf_op jit(solution)/shard_map/ppermute | solution.py:536
  89.0 2.7 %collective-permute-done.21.refs_2_ = f32[8,128]{1,0:T(8,128)S(1)} collective-permute-done((f32[8,128]{1,0:T(8,128)S(1)}, f32[8,128]{1,0:T(8,128)S(1)}, u32[]{:S(2)}, u32[]{:S(2)}) %collective-permute-start.21) | collective-permute-done | bytes 4128 | tf_op jit(solution)/shard_map/ppermute | solution.py:536
  91.6 0.1 collective-permute-done.20.refs_1_
  91.7 0.1 shard_map.111
  91.8 1.2 %collective-permute-start.23 = (bf16[256,256]{1,0:T(8,128)(2,1)S(1)}, bf16[256,256]{1,0:T(8,128)(2,1)S(1)}, u32[]{:S(2)}, u32[]{:S(2)}) collective-permute-start(bf16[256,256]{1,0:T(8,128)(2,1)S(1)} %get-tuple-element.94), channel_id=1, source_target_pairs={{0,8},{1,9},{2,10},{3,11},{4,12},{5,13},{6,14},{7,15},{8,0},{9,1},... | collective-permute-start | bytes 393224 | tf_op jit(solution)/shard_map/ppermute | solution.py:536
  93.0 14.4 %collective-permute-start.26 = (f32[8,128]{1,0:T(8,128)S(1)}, f32[8,128]{1,0:T(8,128)S(1)}, u32[]{:S(2)}, u32[]{:S(2)}) collective-permute-start(f32[8,128]{1,0:T(8,128)S(1)} %get-tuple-element.95.refs_0_), channel_id=1, source_target_pairs={{0,48},{1,49},{2,50},{3,51},{4,52},{5,53},{6,54},{7,55},{8,56},{9,... | collective-permute-start | bytes 12296 | tf_op jit(solution)/shard_map/ppermute | solution.py:536
  107.4 0.5 collective-permute-start.24
  107.9 2.2 %collective-permute-done.26.refs_3_ = f32[8,128]{1,0:T(8,128)S(1)} collective-permute-done((f32[8,128]{1,0:T(8,128)S(1)}, f32[8,128]{1,0:T(8,128)S(1)}, u32[]{:S(2)}, u32[]{:S(2)}) %collective-permute-start.26) | collective-permute-done | bytes 4128 | tf_op jit(solution)/shard_map/ppermute | solution.py:536
  110.1 1.3 %collective-permute-done.25.refs_2_ = f32[8,128]{1,0:T(8,128)S(1)} collective-permute-done((f32[8,128]{1,0:T(8,128)S(1)}, f32[8,128]{1,0:T(8,128)S(1)}, u32[]{:S(2)}, u32[]{:S(2)}) %collective-permute-start.25) | collective-permute-done | bytes 4128 | tf_op jit(solution)/shard_map/ppermute | solution.py:536
  111.4 1.2 %shard_map.112 = (bf16[128,3584]{1,0:T(8,128)(2,1)}, bf16[128,512]{1,0:T(8,128)(2,1)}, bf16[128,512]{1,0:T(8,128)(2,1)}, f32[1,28]{1,0:T(1,128)}) custom-call(s32[1]{0:T(128)} %bitcast.x_ref, bf16[1792,128]{1,0:T(8,128)(2,1)S(1)} %get-tuple-element.73.keep_ref, bf16[1792,128]{1,0:T(8,128)(2,1)S(1)} %collective-permute-done.9.got_ref, ...), custom_call_target="tpu_custom_call" | custom-call | flops 1024 | bytes 2097152 | tf_op jit(solution)/shard_map/pallas_call | solution.py:660
  (28 shorter events, 0.2 us)
Async XLA Ops:
  0.6 0.9 copy-start.2
  1.6 0.9 copy-start.3
  2.5 0.7 copy-start.4
  3.1 12.6 %copy-start.5 = (f32[28]{0:T(128)S(1)}, f32[28]{0:T(128)}, u32[]{:S(2)}) copy-start(f32[28]{0:T(128)} %param.11) | copy-start | bytes 340
  3.5 6.3 %collective-permute-start = (bf16[272,256]{1,0:T(8,128)(2,1)S(1)}, bf16[272,256]{1,0:T(8,128)(2,1)S(1)}, u32[]{:S(2)}, u32[]{:S(2)}) collective-permute-start(bf16[272,256]{1,0:T(8,128)(2,1)S(1)} %get-tuple-element.52.after_ref), channel_id=1, source_target_pairs={{0,8},{1,9},{2,10},{3,11},{4,12},{5,13},{6,14},{7,15},{8,0},{9,1},... | collective-permute-start | bytes 417800 | tf_op jit(solution)/shard_map/ppermute | solution.py:536
  5.6 1.2 %copy-start = (bf16[1,128,3584]{2,1,0:T(8,128)(2,1)S(1)}, bf16[1,128,3584]{2,1,0:T(8,128)(2,1)}, u32[]{:S(2)}) copy-start(bf16[1,128,3584]{2,1,0:T(8,128)(2,1)} %param.6) | copy-start | bytes 2752516
  6.8 1.2 %copy-start.1 = (bf16[1,128,3584]{2,1,0:T(8,128)(2,1)S(1)}, bf16[1,128,3584]{2,1,0:T(8,128)(2,1)}, u32[]{:S(2)}) copy-start(bf16[1,128,3584]{2,1,0:T(8,128)(2,1)} %param.9) | copy-start | bytes 2752516
  9.7 27.4 %collective-permute-start.1 = (bf16[2,1792,128]{2,1,0:T(8,128)(2,1)}, bf16[2,1792,128]{2,1,0:T(8,128)(2,1)S(1)}, u32[]{:S(2)}, u32[]{:S(2)}) collective-permute-start(bf16[2,1792,128]{2,1,0:T(8,128)(2,1)} %get-tuple-element.55), channel_id=1, source_target_pairs={{0,8},{1,9},{2,10},{3,11},{4,12},{5,13},{6,14},{7,15},{8,0},{9,1},... | collective-permute-start | bytes 2752520 | tf_op jit(solution)/shard_map/ppermute | solution.py:536
  9.8 11.6 %collective-permute-start.3 = (bf16[2,272,256]{2,1,0:T(8,128)(2,1)S(1)}, bf16[2,272,256]{2,1,0:T(8,128)(2,1)S(1)}, u32[]{:S(2)}, u32[]{:S(2)}) collective-permute-start(bf16[2,272,256]{2,1,0:T(8,128)(2,1)S(1)} %shard_map.95.refs_1_.refs_4_.refs_7_), channel_id=1, source_target_pairs={{0,7},{1,2},{2,1},{3,4},{4,3},{5,6},{6,5},{7,0},{8,15},{9,10},{10,... | collective-permute-start | bytes 835592 | tf_op jit(solution)/shard_map/ppermute | solution.py:536
  15.7 6.6 %collective-permute-start.2 = (bf16[2,272,256]{2,1,0:T(8,128)(2,1)S(1)}, bf16[2,272,256]{2,1,0:T(8,128)(2,1)S(1)}, u32[]{:S(2)}, u32[]{:S(2)}) collective-permute-start(bf16[2,272,256]{2,1,0:T(8,128)(2,1)S(1)} %shard_map.95.refs_1_.refs_4_.refs_7_), channel_id=1, source_target_pairs={{0,1},{1,0},{2,3},{3,2},{4,5},{5,4},{6,7},{7,6},{8,9},{9,8},{10,11... | collective-permute-start | bytes 835592 | tf_op jit(solution)/shard_map/ppermute | solution.py:536
  22.4 5.8 %collective-permute-start.4 = (bf16[2,272,256]{2,1,0:T(8,128)(2,1)S(1)}, bf16[2,272,256]{2,1,0:T(8,128)(2,1)S(1)}, u32[]{:S(2)}, u32[]{:S(2)}) collective-permute-start(bf16[2,272,256]{2,1,0:T(8,128)(2,1)S(1)} %get-tuple-element.57.refs_5_.refs_6_), channel_id=1, source_target_pairs={{0,1},{1,0},{2,3},{3,2},{4,5},{5,4},{6,7},{7,6},{8,9},{9,8},{10,11... | collective-permute-start | bytes 835592 | tf_op jit(solution)/shard_map/ppermute | solution.py:536
  22.8 6.9 %collective-permute-start.5 = (bf16[2,272,256]{2,1,0:T(8,128)(2,1)S(1)}, bf16[2,272,256]{2,1,0:T(8,128)(2,1)S(1)}, u32[]{:S(2)}, u32[]{:S(2)}) collective-permute-start(bf16[2,272,256]{2,1,0:T(8,128)(2,1)S(1)} %get-tuple-element.58.refs_4_.refs_5_), channel_id=1, source_target_pairs={{0,7},{1,2},{2,1},{3,4},{4,3},{5,6},{6,5},{7,0},{8,15},{9,10},{10,... | collective-permute-start | bytes 835592 | tf_op jit(solution)/shard_map/ppermute | solution.py:536
  29.7 5.5 %collective-permute-start.6 = (bf16[2,272,256]{2,1,0:T(8,128)(2,1)S(1)}, bf16[2,272,256]{2,1,0:T(8,128)(2,1)S(1)}, u32[]{:S(2)}, u32[]{:S(2)}) collective-permute-start(bf16[2,272,256]{2,1,0:T(8,128)(2,1)S(1)} %get-tuple-element.61.refs_5_.refs_8_.refs_6_), channel_id=1, source_target_pairs={{0,1},{1,0},{2,3},{3,2},{4,5},{5,4},{6,7},{7,6},{8,9},{9,8},{10,11... | collective-permute-start | bytes 835592 | tf_op jit(solution)/shard_map/ppermute | solution.py:536
  29.8 6.7 %collective-permute-start.7 = (bf16[2,272,256]{2,1,0:T(8,128)(2,1)S(1)}, bf16[2,272,256]{2,1,0:T(8,128)(2,1)S(1)}, u32[]{:S(2)}, u32[]{:S(2)}) collective-permute-start(bf16[2,272,256]{2,1,0:T(8,128)(2,1)S(1)} %get-tuple-element.62.refs_4_.refs_7_.refs_5_), channel_id=1, source_target_pairs={{0,7},{1,2},{2,1},{3,4},{4,3},{5,6},{6,5},{7,0},{8,15},{9,10},{10,... | collective-permute-start | bytes 835592 | tf_op jit(solution)/shard_map/ppermute | solution.py:536
  36.6 6.6 %collective-permute-start.8 = (bf16[2,272,256]{2,1,0:T(8,128)(2,1)S(1)}, bf16[2,272,256]{2,1,0:T(8,128)(2,1)S(1)}, u32[]{:S(2)}, u32[]{:S(2)}) collective-permute-start(bf16[2,272,256]{2,1,0:T(8,128)(2,1)S(1)} %get-tuple-element.65.refs_10_.refs_6_), channel_id=1, source_target_pairs={{0,1},{1,0},{2,3},{3,2},{4,5},{5,4},{6,7},{7,6},{8,9},{9,8},{10,11... | collective-permute-start | bytes 835592 | tf_op jit(solution)/shard_map/ppermute | solution.py:536
  46.1 16.7 %collective-permute-start.10 = (bf16[2,256,256]{2,1,0:T(8,128)(2,1)S(1)}, bf16[2,256,256]{2,1,0:T(8,128)(2,1)S(1)}, u32[]{:S(2)}, u32[]{:S(2)}) collective-permute-start(bf16[2,256,256]{2,1,0:T(8,128)(2,1)S(1)} %convert_element_type.3), channel_id=1, source_target_pairs={{0,1},{1,0},{2,3},{3,2},{4,5},{5,4},{6,7},{7,6},{8,9},{9,8},{10,11... | collective-permute-start | bytes 786440 | tf_op jit(solution)/shard_map/ppermute | solution.py:536
  47.9 11.1 %collective-permute-start.13 = (f32[8,128]{1,0:T(8,128)S(1)}, f32[8,128]{1,0:T(8,128)S(1)}, u32[]{:S(2)}, u32[]{:S(2)}) collective-permute-start(f32[8,128]{1,0:T(8,128)S(1)} %get-tuple-element.83.refs_3_), channel_id=1, source_target_pairs={{0,12},{1,13},{2,14},{3,15},{4,8},{5,9},{6,10},{7,11},{8,4},{9,5},... | collective-permute-start | bytes 12296 | tf_op jit(solution)/shard_map/ppermute | solution.py:536
  53.9 5.2 %collective-permute-start.12 = (f32[8,128]{1,0:T(8,128)S(1)}, f32[8,128]{1,0:T(8,128)S(1)}, u32[]{:S(2)}, u32[]{:S(2)}) collective-permute-start(f32[8,128]{1,0:T(8,128)S(1)} %get-tuple-element.83.refs_3_), channel_id=1, source_target_pairs={{0,8},{1,9},{2,10},{3,11},{4,12},{5,13},{6,14},{7,15},{8,0},{9,1},... | collective-permute-start | bytes 12296 | tf_op jit(solution)/shard_map/ppermute | solution.py:536
  56.3 6.5 %collective-permute-start.11 = (f32[8,128]{1,0:T(8,128)S(1)}, f32[8,128]{1,0:T(8,128)S(1)}, u32[]{:S(2)}, u32[]{:S(2)}) collective-permute-start(f32[8,128]{1,0:T(8,128)S(1)} %get-tuple-element.83.refs_3_), channel_id=1, source_target_pairs={{0,4},{1,5},{2,6},{3,7},{4,0},{5,1},{6,2},{7,3},{8,12},{9,13},{10,... | collective-permute-start | bytes 12296 | tf_op jit(solution)/shard_map/ppermute | solution.py:536
  62.9 9.7 %collective-permute-start.14 = (bf16[2,288,256]{2,1,0:T(8,128)(2,1)S(1)}, bf16[2,288,256]{2,1,0:T(8,128)(2,1)S(1)}, u32[]{:S(2)}, u32[]{:S(2)}) collective-permute-start(bf16[2,288,256]{2,1,0:T(8,128)(2,1)S(1)} %get-tuple-element.84), channel_id=1, source_target_pairs={{0,1},{1,0},{2,3},{3,2},{4,5},{5,4},{6,7},{7,6},{8,9},{9,8},{10,11... | collective-permute-start | bytes 884744 | tf_op jit(solution)/shard_map/ppermute | solution.py:536
  63.6 9.0 %collective-permute-start.15 = (bf16[2,288,256]{2,1,0:T(8,128)(2,1)S(1)}, bf16[2,288,256]{2,1,0:T(8,128)(2,1)S(1)}, u32[]{:S(2)}, u32[]{:S(2)}) collective-permute-start(bf16[2,288,256]{2,1,0:T(8,128)(2,1)S(1)} %get-tuple-element.85), channel_id=1, source_target_pairs={{0,7},{1,2},{2,1},{3,4},{4,3},{5,6},{6,5},{7,0},{8,15},{9,10},{10,... | collective-permute-start | bytes 884744 | tf_op jit(solution)/shard_map/ppermute | solution.py:536
  72.8 6.2 %collective-permute-start.16 = (bf16[2,288,256]{2,1,0:T(8,128)(2,1)S(1)}, bf16[2,288,256]{2,1,0:T(8,128)(2,1)S(1)}, u32[]{:S(2)}, u32[]{:S(2)}) collective-permute-start(bf16[2,288,256]{2,1,0:T(8,128)(2,1)S(1)} %get-tuple-element.86), channel_id=1, source_target_pairs={{0,1},{1,0},{2,3},{3,2},{4,5},{5,4},{6,7},{7,6},{8,9},{9,8},{10,11... | collective-permute-start | bytes 884744 | tf_op jit(solution)/shard_map/ppermute | solution.py:536
  72.9 7.8 %collective-permute-start.17 = (bf16[2,288,256]{2,1,0:T(8,128)(2,1)S(1)}, bf16[2,288,256]{2,1,0:T(8,128)(2,1)S(1)}, u32[]{:S(2)}, u32[]{:S(2)}) collective-permute-start(bf16[2,288,256]{2,1,0:T(8,128)(2,1)S(1)} %get-tuple-element.87), channel_id=1, source_target_pairs={{0,7},{1,2},{2,1},{3,4},{4,3},{5,6},{6,5},{7,0},{8,15},{9,10},{10,... | collective-permute-start | bytes 884744 | tf_op jit(solution)/shard_map/ppermute | solution.py:536
  78.9 29.0 %collective-permute-start.9 = (bf16[1792,128]{1,0:T(8,128)(2,1)S(1)}, bf16[1792,128]{1,0:T(8,128)(2,1)S(1)}, u32[]{:S(2)}, u32[]{:S(2)}) collective-permute-start(bf16[1792,128]{1,0:T(8,128)(2,1)S(1)} %get-tuple-element.74), channel_id=1, source_target_pairs={{0,8},{1,9},{2,10},{3,11},{4,12},{5,13},{6,14},{7,15},{8,0},{9,1},... | collective-permute-start | bytes 1376264 | tf_op jit(solution)/shard_map/ppermute | solution.py:536
  80.8 10.9 %collective-permute-start.18 = (bf16[2,256,256]{2,1,0:T(8,128)(2,1)S(1)}, bf16[2,256,256]{2,1,0:T(8,128)(2,1)S(1)}, u32[]{:S(2)}, u32[]{:S(2)}) collective-permute-start(bf16[2,256,256]{2,1,0:T(8,128)(2,1)S(1)} %get-tuple-element.90), channel_id=1, source_target_pairs={{0,1},{1,0},{2,3},{3,2},{4,5},{5,4},{6,7},{7,6},{8,9},{9,8},{10,11... | collective-permute-start | bytes 786440 | tf_op jit(solution)/shard_map/ppermute | solution.py:536
  80.9 10.8 %collective-permute-start.19 = (bf16[2,256,256]{2,1,0:T(8,128)(2,1)S(1)}, bf16[2,256,256]{2,1,0:T(8,128)(2,1)S(1)}, u32[]{:S(2)}, u32[]{:S(2)}) collective-permute-start(bf16[2,256,256]{2,1,0:T(8,128)(2,1)S(1)} %get-tuple-element.91), channel_id=1, source_target_pairs={{0,7},{1,2},{2,1},{3,4},{4,3},{5,6},{6,5},{7,0},{8,15},{9,10},{10,... | collective-permute-start | bytes 786440 | tf_op jit(solution)/shard_map/ppermute | solution.py:536
  84.3 4.6 %collective-permute-start.22 = (f32[8,128]{1,0:T(8,128)S(1)}, f32[8,128]{1,0:T(8,128)S(1)}, u32[]{:S(2)}, u32[]{:S(2)}) collective-permute-start(f32[8,128]{1,0:T(8,128)S(1)} %get-tuple-element.92.refs_0_), channel_id=1, source_target_pairs={{0,192},{1,193},{2,194},{3,195},{4,196},{5,197},{6,198},{7,199},{8... | collective-permute-start | bytes 12296 | tf_op jit(solution)/shard_map/ppermute | solution.py:536
  87.7 4.0 %collective-permute-start.21 = (f32[8,128]{1,0:T(8,128)S(1)}, f32[8,128]{1,0:T(8,128)S(1)}, u32[]{:S(2)}, u32[]{:S(2)}) collective-permute-start(f32[8,128]{1,0:T(8,128)S(1)} %get-tuple-element.92.refs_0_), channel_id=1, source_target_pairs={{0,128},{1,129},{2,130},{3,131},{4,132},{5,133},{6,134},{7,135},{8... | collective-permute-start | bytes 12296 | tf_op jit(solution)/shard_map/ppermute | solution.py:536
  89.0 2.8 %collective-permute-start.20 = (f32[8,128]{1,0:T(8,128)S(1)}, f32[8,128]{1,0:T(8,128)S(1)}, u32[]{:S(2)}, u32[]{:S(2)}) collective-permute-start(f32[8,128]{1,0:T(8,128)S(1)} %get-tuple-element.92.refs_0_), channel_id=1, source_target_pairs={{0,64},{1,65},{2,66},{3,67},{4,68},{5,69},{6,70},{7,71},{8,72},{9,... | collective-permute-start | bytes 12296 | tf_op jit(solution)/shard_map/ppermute | solution.py:536
  91.8 19.6 %collective-permute-start.23 = (bf16[256,256]{1,0:T(8,128)(2,1)S(1)}, bf16[256,256]{1,0:T(8,128)(2,1)S(1)}, u32[]{:S(2)}, u32[]{:S(2)}) collective-permute-start(bf16[256,256]{1,0:T(8,128)(2,1)S(1)} %get-tuple-element.94), channel_id=1, source_target_pairs={{0,8},{1,9},{2,10},{3,11},{4,12},{5,13},{6,14},{7,15},{8,0},{9,1},... | collective-permute-start | bytes 393224 | tf_op jit(solution)/shard_map/ppermute | solution.py:536
  93.0 17.1 %collective-permute-start.26 = (f32[8,128]{1,0:T(8,128)S(1)}, f32[8,128]{1,0:T(8,128)S(1)}, u32[]{:S(2)}, u32[]{:S(2)}) collective-permute-start(f32[8,128]{1,0:T(8,128)S(1)} %get-tuple-element.95.refs_0_), channel_id=1, source_target_pairs={{0,48},{1,49},{2,50},{3,51},{4,52},{5,53},{6,54},{7,55},{8,56},{9,... | collective-permute-start | bytes 12296 | tf_op jit(solution)/shard_map/ppermute | solution.py:536
  107.4 4.0 %collective-permute-start.25 = (f32[8,128]{1,0:T(8,128)S(1)}, f32[8,128]{1,0:T(8,128)S(1)}, u32[]{:S(2)}, u32[]{:S(2)}) collective-permute-start(f32[8,128]{1,0:T(8,128)S(1)} %get-tuple-element.95.refs_0_), channel_id=1, source_target_pairs={{0,32},{1,33},{2,34},{3,35},{4,36},{5,37},{6,38},{7,39},{8,40},{9,... | collective-permute-start | bytes 12296 | tf_op jit(solution)/shard_map/ppermute | solution.py:536
  107.4 4.0 %collective-permute-start.24 = (f32[8,128]{1,0:T(8,128)S(1)}, f32[8,128]{1,0:T(8,128)S(1)}, u32[]{:S(2)}, u32[]{:S(2)}) collective-permute-start(f32[8,128]{1,0:T(8,128)S(1)} %get-tuple-element.95.refs_0_), channel_id=1, source_target_pairs={{0,16},{1,17},{2,18},{3,19},{4,20},{5,21},{6,22},{7,23},{8,24},{9,... | collective-permute-start | bytes 12296 | tf_op jit(solution)/shard_map/ppermute | solution.py:536

commit v4 on v3

--- a/solution.py
+++ b/solution.py
@@ -31,16 +31,17 @@
     return lax.dot_general(a, b, dims, preferred_element_type=F32)
 
 
-def call(body, outs, scratch, flops, moved, operands):
+def call(body, outs, scratch, flops, moved, operands, limit=10, aliases=None):
     return pl.pallas_call(
         body,
         out_shape=outs,
         in_specs=operands,
         scratch_shapes=scratch,
+        input_output_aliases=aliases or {},
         cost_estimate=pl.CostEstimate(
             flops=flops, bytes_accessed=moved, transcendentals=flops // 1024
         ),
-        compiler_params=pltpu.CompilerParams(vmem_limit_bytes=20 * 1024 * 1024),
+        compiler_params=pltpu.CompilerParams(vmem_limit_bytes=limit * 1024 * 1024),
     )
 
 
@@ -165,7 +166,7 @@
         to_b[slot, plain, :] = second.astype(BF16)
     parts = [ref[...] for ref in scale_refs]
     if step == 3:
-        scale = four(parts)
+        scale = parts[0] + parts[1]
         put_scale(to_a.at[0], scale)
         put_scale(to_b.at[0], scale)
     elif step == 2:
@@ -190,7 +191,7 @@
     scale_out[...] = four([ref[...] for ref in scale_refs])
 
 
-def place(blocks, first, top, key_c, value_c, pos_c):
+def place(blocks, first, top, key_c, value_c, pos_c, span=TILE):
     start = jnp.int32(0)
     entries = []
     for phase in range(2):
@@ -199,7 +200,7 @@
         begins = [jnp.min(row) for row in rows]
         counts = [jnp.sum(jnp.where(row < FAR, 1.0, 0.0)).astype(jnp.int32) for row in rows]
         counts = [jnp.where(begin <= top, n, 0) for begin, n in zip(begins, counts)]
-        spans = [(n + 15) >> 4 for n in counts]
+        chunks = [(n + 15) >> 4 for n in counts]
         def put(number, at, slot=slot, rows=rows):
             ref = blocks[number]
             target = pl.ds(pl.multiple_of(at, 16), ROWS)
@@ -212,8 +213,8 @@
         if len(blocks) == 2:
             ahead = begins[0] < begins[1]
             starts = [
-                start + jnp.where(ahead, 0, spans[1] * 16),
-                start + jnp.where(ahead, spans[0] * 16, 0),
+                start + jnp.where(ahead, 0, chunks[1] * 16),
+                start + jnp.where(ahead, chunks[0] * 16, 0),
             ]
 
             @pl.when(ahead)
@@ -229,34 +230,38 @@
         else:
             starts = []
             total = start
-            for number, span in enumerate(spans):
+            for number, chunk in enumerate(chunks):
                 starts.append(total)
                 put(number, total)
-                total = total + span * 16
+                total = total + chunk * 16
         entries.append((slot, starts, counts))
-        start = start + sum(spans) * 16
-    rest = pl.ds(pl.multiple_of(start, 16), TILE)
-    pos_c[rest, :] = jnp.full((TILE, ROWS), 1e9, F32)
+        start = start + sum(chunks) * 16
+    rest = pl.ds(pl.multiple_of(start, 16), span)
+    pos_c[rest, :] = jnp.full((span, ROWS), 1e9, F32)
     for g in range(KV_HEADS):
-        key_c[g, rest, :] = jnp.zeros((TILE, HEAD), BF16)
-        value_c[g, rest, :] = jnp.zeros((TILE, HEAD), BF16)
+        key_c[g, rest, :] = jnp.zeros((span, HEAD), BF16)
+        value_c[g, rest, :] = jnp.zeros((span, HEAD), BF16)
     return start, entries
 
 
-def stats_tile(rate_ref, work_ref, state, key_c, value_c, mask, at, slot, g):
+def tile_of(blocks):
+    return 2 * TILE if len(blocks) > 2 else TILE
+
+
+def stats_tile(rate_ref, work_ref, state, key_c, value_c, mask, rows, slot, g):
     some = slice(g * WIDE, (g + 1) * WIDE)
-    raw = product(key_c[g, pl.ds(at, TILE), :], work_ref[0, some, :], NT)
-    dots = product(value_c[g, pl.ds(at, TILE), :], work_ref[1, some, :], NT)
+    raw = product(key_c[g, rows, :], work_ref[0, some, :], NT)
+    dots = product(value_c[g, rows, :], work_ref[1, some, :], NT)
     for head in range(GROUP):
         lanes = slice(head * ROWS, (head + 1) * ROWS)
         scores = jnp.where(mask, raw[:, lanes] * rate_ref[g, 0:1, lanes], LOW)
         held = [state[slot * KV_HEADS + g, n, :, lanes] for n in range(5)]
         top, total, weighted, shifted, both = held
-        scores = scores.reshape(TILE // 8, 8, ROWS)
+        scores = scores.reshape(mask.shape[0] // 8, 8, ROWS)
         new_top = jnp.maximum(top, jnp.max(scores, axis=0))
         above = scores - new_top[None]
         weights = jnp.exp2(above)
-        weighted_dots = weights * dots[:, lanes].reshape(TILE // 8, 8, ROWS)
+        weighted_dots = weights * dots[:, lanes].reshape(mask.shape[0] // 8, 8, ROWS)
         step_down = top - new_top
         factor = jnp.exp2(step_down)
         held = [
@@ -291,12 +296,13 @@
     else:
         state[...] = prior_ref[...]
     for blocks, slots in work:
+        span = tile_of(blocks)
         top = jnp.maximum(tops[0], tops[1]) if len(slots) == 2 else tops[slots[0]]
-        length, _ = place(blocks, first, top, key_c, value_c, pos_c)
-
-        def tile(step, _, slots=slots):
-            at = pl.multiple_of(step * TILE, TILE)
-            key_pos = pos_c[pl.ds(at, TILE), :]
+        length, _ = place(blocks, first, top, key_c, value_c, pos_c, span)
+
+        def tile(step, _, slots=slots, span=span):
+            at = pl.multiple_of(step * span, span)
+            key_pos = pos_c[pl.ds(at, span), :]
             lowest = jnp.min(key_pos)
             for slot in slots:
 
@@ -305,12 +311,20 @@
                     mask = key_pos <= query_rows[slot]
                     for g in range(KV_HEADS):
                         stats_tile(
-                            rate_ref, (kept_ref, got_ref)[slot], state, key_c, value_c, mask, at, slot, g
+                            rate_ref,
+                            (kept_ref, got_ref)[slot],
+                            state,
+                            key_c,
+                            value_c,
+                            mask,
+                            pl.ds(at, span),
+                            slot,
+                            g,
                         )
 
             return 0
 
-        lax.fori_loop(0, (length + TILE - 1) // TILE, tile, 0)
+        lax.fori_loop(0, (length + span - 1) // span, tile, 0)
     if not is_last:
         return
     lane = lax.broadcasted_iota(jnp.int32, (8, ROWS), 1)
@@ -402,7 +416,7 @@
     )
     if is_first:
         query_sum[...] = jnp.zeros_like(query_sum)
-    else:
+    elif is_last:
         query_sum[...] = prior_ref[...]
 
     def tile(step, _):
@@ -458,7 +472,7 @@
 
 
 def compact_scratch(count):
-    size = 2 * count * ROWS + TILE
+    size = 2 * count * ROWS + 2 * TILE
     return [
         pltpu.VMEM((KV_HEADS, size, HEAD), BF16),
         pltpu.VMEM((KV_HEADS, size, HEAD), BF16),
@@ -501,6 +515,7 @@
         scratch = [pltpu.VMEM(sums.shape, F32)]
     else:
         outs, scratch = outs + [sums], []
+    aliases = {} if prior is None or is_last else {len(operands) - 1: len(outs) - 1}
     size = 2 * count * ROWS + TILE
     scratch = (
         scratch
@@ -514,6 +529,7 @@
         count * 2 * ROWS * 2 * HEADS * ROWS * 2 * HEAD * 5,
         6 << 20,
         [pl.BlockSpec(memory_space=pltpu.VMEM)] * len(operands),
+        aliases=aliases,
     )(*operands)
 
 
@@ -553,6 +569,7 @@
         1024,
         1 << 20,
         [smem, in_hbm, in_hbm, in_hbm],
+        60,
     )(x_ref, keys[0], values[0], routes)
     keys_got = swap(keys_sent, across)
     work = jax.ShapeDtypeStruct((2, HEADS * ROWS, HEAD), BF16)
@@ -567,6 +584,7 @@
         1024,
         4 << 20,
         [smem, anywhere, in_hbm, in_hbm],
+        60,
     )(x_ref, keys_sent, queries[0], out_grad[0])
     got = swap(sent, across)
     own = call(
@@ -576,7 +594,7 @@
         1024,
         1 << 20,
         [anywhere, vmem, vmem],
-    )(kept, keys_kept, keys_got)
+    )(sent, keys_kept, keys_got)
 
     half_scale = lax.dynamic_slice_in_dim(per_head_scale, x * HEADS, HEADS)
     rate = jnp.repeat(half_scale * (LOG2E / math.sqrt(HEAD)), ROWS).reshape(KV_HEADS, 1, WIDE)
@@ -631,7 +649,7 @@
             [vmem] * (2 + len(arrived) + len(scales)),
         )(*parts, *arrived, *scales)
 
-    scales = exchange(scale, (4, 8, 12))
+    scales = exchange(scale, (4,))
     far, sums = grads(rate, own, kept, got, final, [a[4]])
     from_even = swap(far.astype(BF16), even)
     part_a, part_b, sums = grads(rate, own, kept, got, final, [a[3], b[3]], sums)
@@ -646,7 +664,8 @@
     query_got = swap(query_sent, across)
     to_a, to_b, scale = hop(1, (part_a, part_b), (sent_a, sent_b), [scale, beside])
     sent_a, sent_b = swap(to_a, even), swap(to_b, odd)
-    scales = exchange(scale, (64, 128, 192))
+    scales = exchange(scale, (8,))
+    scales = exchange(scales[0] + scales[1], (64, 128, 192))
     ours, theirs, scale = call(
         last_hop_body,
         [jax.ShapeDtypeStruct((2 * ROWS, width), BF16)] * 2 + [SMALL],

time: 113 us -> 110 us (0.973)
  the two profiles are of different devices: /device:TPU:1 before, /device:TPU:38 now
where the time goes in v4:
time: 110 us; the launch traced here: 109 us
  starting transfers between devices  50.5 us (46%)
  Pallas kernels  30 us (27%)
  waiting for transfers between devices  26.3 us (24%)
  local copies, waits for them, and re-layouts  1.37 us (1%)
    ppermute x26, starting transfers between devices, swap(): return lax.ppermute(array, axis, pairs)  50.5 us
    ppermute x26, waiting for transfers between devices, swap(): return lax.ppermute(array, axis, pairs)  26.3 us
    pallas_call x4, Pallas kernels, grads(): call(functools.partial(grads_body, count, prior is None, is_last), outs,...  12.5 us
    pallas_call x5, Pallas kernels, stats(): call(functools.partial(stats_body, sizes, prior is None, is_last), outs,...  11 us
    pallas_call x1, Pallas kernels, local(): call(pack_queries_body, [work, work], [pltpu.VMEM((ROWS, 2 * HEADS * HEAD...  3.04 us
  transfers between devices with their start and end apart: 26, of which 16 were waited for; matrix products, arithmetic and copies ran while one was open for 0% of the time, Pallas kernels for 22%

profile of v4, /device:TPU:38, one launch (start us, length us, event | category | flops | bytes accessed | tf_op | source)
XLA Modules:
  0.0 109.1 jit_solution(110705164892685727)
XLA Ops:
  0.7 1.7 %shard_map.93 = (bf16[272,256]{1,0:T(8,128)(2,1)}, bf16[272,256]{1,0:T(8,128)(2,1)}) custom-call(s32[1]{0:T(128)} %bitcast.x_ref, bf16[128,512]{1,0:T(8,128)(2,1)} %bitcast.16, bf16[128,512]{1,0:T(8,128)(2,1)} %bitcast.17, s32[1,128]{1,0:T(1,128)} %pos_in.1), custom_call_target="tpu_custom_call" | custom-call | flops 1024 | bytes 1048576 | tf_op jit(solution)/shard_map/pallas_call | solution.py:560
  2.4 0.9 collective-permute-start
  3.3 3.0 %shard_map.94 = (bf16[2,1792,128]{2,1,0:T(8,128)(2,1)}, bf16[2,1792,128]{2,1,0:T(8,128)(2,1)}) custom-call(s32[1]{0:T(128)} %bitcast.x_ref, bf16[272,256]{1,0:T(8,128)(2,1)} %get-tuple-element.52.after_ref, bf16[128,3584]{1,0:T(8,128)(2,1)} %bitcast.14, bf16[128,3584]{1,0:T(8,128)(2,1)} %bitcast.15), custom_call_target="tpu_custom_call" | custom-call | flops 1024 | bytes 4194304 | tf_op jit(solution)/shard_map/pallas_call | solution.py:576
  6.4 0.0 copy-start
  6.4 1.3 %collective-permute-start.1 = (bf16[2,1792,128]{2,1,0:T(8,128)(2,1)}, bf16[2,1792,128]{2,1,0:T(8,128)(2,1)S(1)}, u32[]{:S(2)}, u32[]{:S(2)}) collective-permute-start(bf16[2,1792,128]{2,1,0:T(8,128)(2,1)} %get-tuple-element.53.after_ref), channel_id=1, source_target_pairs={{0,8},{1,9},{2,10},{3,11},{4,12},{5,13},{6,14},{7,15},{8,0},{9,1},... | collective-permute-start | bytes 2752520 | tf_op jit(solution)/shard_map/ppermute | solution.py:552
  7.7 0.4 collective-permute-done.got_ref
  8.1 1.2 %copy-done.1 = bf16[2,1792,128]{2,1,0:T(8,128)(2,1)S(1)} copy-done((bf16[2,1792,128]{2,1,0:T(8,128)(2,1)S(1)}, bf16[2,1792,128]{2,1,0:T(8,128)(2,1)}, u32[]{:S(2)}) %copy-start.1) | copy-done | bytes 917528
  9.3 2.0 %collective-permute-start.3 = (bf16[2,272,256]{2,1,0:T(8,128)(2,1)S(1)}, bf16[2,272,256]{2,1,0:T(8,128)(2,1)S(1)}, u32[]{:S(2)}, u32[]{:S(2)}) collective-permute-start(bf16[2,272,256]{2,1,0:T(8,128)(2,1)S(1)} %shard_map.95.refs_1_.refs_4_.refs_7_), channel_id=1, source_target_pairs={{0,7},{1,2},{2,1},{3,4},{4,3},{5,6},{6,5},{7,0},{8,15},{9,10},{10,... | collective-permute-start | bytes 835592 | tf_op jit(solution)/shard_map/ppermute | solution.py:552
  11.3 4.0 %collective-permute-start.2 = (bf16[2,272,256]{2,1,0:T(8,128)(2,1)S(1)}, bf16[2,272,256]{2,1,0:T(8,128)(2,1)S(1)}, u32[]{:S(2)}, u32[]{:S(2)}) collective-permute-start(bf16[2,272,256]{2,1,0:T(8,128)(2,1)S(1)} %shard_map.95.refs_1_.refs_4_.refs_7_), channel_id=1, source_target_pairs={{0,1},{1,0},{2,3},{3,2},{4,5},{5,4},{6,7},{7,6},{8,9},{9,8},{10,11... | collective-permute-start | bytes 835592 | tf_op jit(solution)/shard_map/ppermute | solution.py:552
  15.4 0.1 dynamic-slice_multiply_fusion
  15.5 0.1 broadcast_in_dim.21
  15.5 0.1 broadcast_bitcast_fusion
  15.6 1.0 shard_map.96
  16.7 0.4 collective-permute-done.3.refs_1_
  17.1 3.8 %collective-permute-done.2.refs_0_ = bf16[2,272,256]{2,1,0:T(8,128)(2,1)S(1)} collective-permute-done((bf16[2,272,256]{2,1,0:T(8,128)(2,1)S(1)}, bf16[2,272,256]{2,1,0:T(8,128)(2,1)S(1)}, u32[]{:S(2)}, u32[]{:S(2)}) %collective-permute-start.2) | collective-permute-done | bytes 278560 | tf_op jit(solution)/shard_map/ppermute | solution.py:552
  20.9 1.8 %collective-permute-start.4 = (bf16[2,272,256]{2,1,0:T(8,128)(2,1)S(1)}, bf16[2,272,256]{2,1,0:T(8,128)(2,1)S(1)}, u32[]{:S(2)}, u32[]{:S(2)}) collective-permute-start(bf16[2,272,256]{2,1,0:T(8,128)(2,1)S(1)} %get-tuple-element.57.refs_5_.refs_6_), channel_id=1, source_target_pairs={{0,1},{1,0},{2,3},{3,2},{4,5},{5,4},{6,7},{7,6},{8,9},{9,8},{10,11... | collective-permute-start | bytes 835592 | tf_op jit(solution)/shard_map/ppermute | solution.py:552
  22.7 1.0 collective-permute-start.5
  23.7 2.1 %shard_map.98 = (f32[4,5,8,896]{3,2,1,0:T(8,128)S(1)}, f32[8,128]{1,0:T(8,128)S(1)}) custom-call(f32[2,8,896]{2,1,0:T(8,128)S(1)} %broadcast_in_dim.24.refs_0_, bf16[2,272,256]{2,1,0:T(8,128)(2,1)S(1)} %shard_map.95.refs_1_.refs_4_.refs_7_, bf16[2,1792,128]{2,1,0:T(8,128)(2,1)S(1)} %copy-done, bf16[2,1792,128]{2,1,0:T(8,128)(2,1)S(1)} %copy-done, ...), custom_call_target="tpu_custom_call" | custom-call | flops 469762048 | bytes 4194304 | tf_op jit(solution)/shard_map/pallas_call | solution.py:497
  25.8 1.8 %collective-permute-done.4.refs_0_ = bf16[2,272,256]{2,1,0:T(8,128)(2,1)S(1)} collective-permute-done((bf16[2,272,256]{2,1,0:T(8,128)(2,1)S(1)}, bf16[2,272,256]{2,1,0:T(8,128)(2,1)S(1)}, u32[]{:S(2)}, u32[]{:S(2)}) %collective-permute-start.4) | collective-permute-done | bytes 278560 | tf_op jit(solution)/shard_map/ppermute | solution.py:552
  27.6 1.7 %collective-permute-done.5.refs_1_ = bf16[2,272,256]{2,1,0:T(8,128)(2,1)S(1)} collective-permute-done((bf16[2,272,256]{2,1,0:T(8,128)(2,1)S(1)}, bf16[2,272,256]{2,1,0:T(8,128)(2,1)S(1)}, u32[]{:S(2)}, u32[]{:S(2)}) %collective-permute-start.5) | collective-permute-done | bytes 278560 | tf_op jit(solution)/shard_map/ppermute | solution.py:552
  29.3 1.6 %collective-permute-start.6 = (bf16[2,272,256]{2,1,0:T(8,128)(2,1)S(1)}, bf16[2,272,256]{2,1,0:T(8,128)(2,1)S(1)}, u32[]{:S(2)}, u32[]{:S(2)}) collective-permute-start(bf16[2,272,256]{2,1,0:T(8,128)(2,1)S(1)} %get-tuple-element.61.refs_5_.refs_8_.refs_6_), channel_id=1, source_target_pairs={{0,1},{1,0},{2,3},{3,2},{4,5},{5,4},{6,7},{7,6},{8,9},{9,8},{10,11... | collective-permute-start | bytes 835592 | tf_op jit(solution)/shard_map/ppermute | solution.py:552
  30.9 1.0 collective-permute-start.7
  31.9 2.1 %shard_map.100 = (f32[4,5,8,896]{3,2,1,0:T(8,128)S(1)}, f32[8,128]{1,0:T(8,128)S(1)}) custom-call(f32[2,8,896]{2,1,0:T(8,128)S(1)} %broadcast_in_dim.24.refs_0_, bf16[2,272,256]{2,1,0:T(8,128)(2,1)S(1)} %shard_map.95.refs_1_.refs_4_.refs_7_, bf16[2,1792,128]{2,1,0:T(8,128)(2,1)S(1)} %copy-done, bf16[2,1792,128]{2,1,0:T(8,128)(2,1)S(1)} %copy-done, ...), custom_call_target="tpu_custom_call" | custom-call | flops 469762048 | bytes 4194304 | tf_op jit(solution)/shard_map/pallas_call | solution.py:497
  34.0 2.5 %collective-permute-done.6.refs_0_ = bf16[2,272,256]{2,1,0:T(8,128)(2,1)S(1)} collective-permute-done((bf16[2,272,256]{2,1,0:T(8,128)(2,1)S(1)}, bf16[2,272,256]{2,1,0:T(8,128)(2,1)S(1)}, u32[]{:S(2)}, u32[]{:S(2)}) %collective-permute-start.6) | collective-permute-done | bytes 278560 | tf_op jit(solution)/shard_map/ppermute | solution.py:552
  36.5 1.0 collective-permute-done.7.refs_1_
  37.5 1.8 %collective-permute-start.8 = (bf16[2,272,256]{2,1,0:T(8,128)(2,1)S(1)}, bf16[2,272,256]{2,1,0:T(8,128)(2,1)S(1)}, u32[]{:S(2)}, u32[]{:S(2)}) collective-permute-start(bf16[2,272,256]{2,1,0:T(8,128)(2,1)S(1)} %get-tuple-element.65.refs_10_.refs_6_), channel_id=1, source_target_pairs={{0,1},{1,0},{2,3},{3,2},{4,5},{5,4},{6,7},{7,6},{8,9},{9,8},{10,11... | collective-permute-start | bytes 835592 | tf_op jit(solution)/shard_map/ppermute | solution.py:552
  39.3 4.3 %shard_map.102 = (f32[4,5,8,896]{3,2,1,0:T(8,128)S(1)}, f32[8,128]{1,0:T(8,128)}) custom-call(f32[2,8,896]{2,1,0:T(8,128)S(1)} %broadcast_in_dim.24.refs_0_, bf16[2,272,256]{2,1,0:T(8,128)(2,1)S(1)} %shard_map.95.refs_1_.refs_4_.refs_7_, bf16[2,1792,128]{2,1,0:T(8,128)(2,1)S(1)} %copy-done, bf16[2,1792,128]{2,1,0:T(8,128)(2,1)S(1)} %collective-permute-done.1.refs_3_, ...), custom_call_target="tpu_custom_call" | custom-call | flops 2113929216 | bytes 4194304 | tf_op jit(solution)/shard_map/pallas_call | solution.py:497
  43.6 0.5 collective-permute-done.8.refs_4_.refs_5_
  44.1 1.5 %shard_map.103 = (f32[4,8,896]{2,1,0:T(8,128)S(1)}, f32[8,128]{1,0:T(8,128)S(1)}) custom-call(f32[2,8,896]{2,1,0:T(8,128)S(1)} %broadcast_in_dim.24.refs_0_, bf16[2,272,256]{2,1,0:T(8,128)(2,1)S(1)} %shard_map.95.refs_1_.refs_4_.refs_7_, bf16[2,1792,128]{2,1,0:T(8,128)(2,1)S(1)} %copy-done, bf16[2,1792,128]{2,1,0:T(8,128)(2,1)S(1)} %collective-permute-done.1.refs_3_, ...), custom_call_target="tpu_custom_call" | custom-call | flops 469762048 | bytes 4194304 | tf_op jit(solution)/shard_map/pallas_call | solution.py:497
  45.7 1.4 %shard_map.104 = (f32[2,256,256]{2,1,0:T(8,128)S(1)}, f32[4,128,896]{2,1,0:T(8,128)S(1)}) custom-call(f32[2,8,896]{2,1,0:T(8,128)S(1)} %broadcast_in_dim.24.refs_0_, bf16[2,272,256]{2,1,0:T(8,128)(2,1)S(1)} %shard_map.95.refs_1_.refs_4_.refs_7_, bf16[2,1792,128]{2,1,0:T(8,128)(2,1)S(1)} %copy-done, bf16[2,1792,128]{2,1,0:T(8,128)(2,1)S(1)} %collective-permute-done.1.refs_3_, ...), custom_call_target="tpu_custom_call" | custom-call | flops 1174405120 | bytes 6291456 | tf_op jit(solution)/shard_map/pallas_call | solution.py:525
  47.1 1.8 %collective-permute-start.10 = (bf16[2,256,256]{2,1,0:T(8,128)(2,1)S(1)}, bf16[2,256,256]{2,1,0:T(8,128)(2,1)S(1)}, u32[]{:S(2)}, u32[]{:S(2)}) collective-permute-start(bf16[2,256,256]{2,1,0:T(8,128)(2,1)S(1)} %convert_element_type.3), channel_id=1, source_target_pairs={{0,1},{1,0},{2,3},{3,2},{4,5},{5,4},{6,7},{7,6},{8,9},{9,8},{10,11... | collective-permute-start | bytes 786440 | tf_op jit(solution)/shard_map/ppermute | solution.py:552
  48.9 5.2 %collective-permute-start.11 = (f32[8,128]{1,0:T(8,128)S(1)}, f32[8,128]{1,0:T(8,128)S(1)}, u32[]{:S(2)}, u32[]{:S(2)}) collective-permute-start(f32[8,128]{1,0:T(8,128)S(1)} %get-tuple-element.83.refs_3_), channel_id=1, source_target_pairs={{0,4},{1,5},{2,6},{3,7},{4,0},{5,1},{6,2},{7,3},{8,12},{9,13},{10,... | collective-permute-start | bytes 12296 | tf_op jit(solution)/shard_map/ppermute | solution.py:552
  54.1 2.6 %shard_map.105 = (f32[2,256,256]{2,1,0:T(8,128)S(1)}, f32[2,256,256]{2,1,0:T(8,128)S(1)}, f32[4,128,896]{2,1,0:T(8,128)S(1)}) custom-call(f32[2,8,896]{2,1,0:T(8,128)S(1)} %broadcast_in_dim.24.refs_0_, bf16[2,272,256]{2,1,0:T(8,128)(2,1)S(1)} %shard_map.95.refs_1_.refs_4_.refs_7_, ...), custom_call_target="tpu_custom_call", output_to_operand_aliasing={{2}: (7, {})} | custom-call | flops 2348810240 | bytes 6291456 | tf_op jit(solution)/shard_map/pallas_call | solution.py:525
  56.7 1.8 %collective-permute-done.11.refs_4_ = f32[8,128]{1,0:T(8,128)S(1)} collective-permute-done((f32[8,128]{1,0:T(8,128)S(1)}, f32[8,128]{1,0:T(8,128)S(1)}, u32[]{:S(2)}, u32[]{:S(2)}) %collective-permute-start.11) | collective-permute-done | bytes 4128 | tf_op jit(solution)/shard_map/ppermute | solution.py:552
  58.5 0.0 collective-permute-done.10.refs_2_
  58.5 0.1 shard_map.108
  58.6 3.2 %collective-permute-start.12 = (bf16[2,288,256]{2,1,0:T(8,128)(2,1)S(1)}, bf16[2,288,256]{2,1,0:T(8,128)(2,1)S(1)}, u32[]{:S(2)}, u32[]{:S(2)}) collective-permute-start(bf16[2,288,256]{2,1,0:T(8,128)(2,1)S(1)} %get-tuple-element.84), channel_id=1, source_target_pairs={{0,1},{1,0},{2,3},{3,2},{4,5},{5,4},{6,7},{7,6},{8,9},{9,8},{10,11... | collective-permute-start | bytes 884744 | tf_op jit(solution)/shard_map/ppermute | solution.py:552
  61.8 3.4 %collective-permute-start.13 = (bf16[2,288,256]{2,1,0:T(8,128)(2,1)S(1)}, bf16[2,288,256]{2,1,0:T(8,128)(2,1)S(1)}, u32[]{:S(2)}, u32[]{:S(2)}) collective-permute-start(bf16[2,288,256]{2,1,0:T(8,128)(2,1)S(1)} %get-tuple-element.85), channel_id=1, source_target_pairs={{0,7},{1,2},{2,1},{3,4},{4,3},{5,6},{6,5},{7,0},{8,15},{9,10},{10,... | collective-permute-start | bytes 884744 | tf_op jit(solution)/shard_map/ppermute | solution.py:552
  65.3 4.4 %shard_map.106 = (f32[2,256,256]{2,1,0:T(8,128)S(1)}, f32[2,256,256]{2,1,0:T(8,128)S(1)}, f32[2,256,256]{2,1,0:T(8,128)S(1)}, f32[4,128,896]{2,1,0:T(8,128)S(1)}) custom-call(f32[2,8,896]{2,1,0:T(8,128)S(1)} %broadcast_in_dim.24.refs_0_, bf16[2,272,256]{2,1,0:T(8,128)(2,1)S(1)} %shard_map.95.refs_1_.refs_4_.refs_7_, ...), custom_call_target="tpu_custom_call", output_to_operand_aliasing={{3}: (8, {})} | custom-call | flops 3523215360 | bytes 6291456 | tf_op jit(solution)/shard_map/pallas_call | solution.py:525
  69.6 0.0 collective-permute-done.12.refs_2_
  69.7 2.7 %collective-permute-done.13.refs_3_ = bf16[2,288,256]{2,1,0:T(8,128)(2,1)S(1)} collective-permute-done((bf16[2,288,256]{2,1,0:T(8,128)(2,1)S(1)}, bf16[2,288,256]{2,1,0:T(8,128)(2,1)S(1)}, u32[]{:S(2)}, u32[]{:S(2)}) %collective-permute-start.13) | collective-permute-done | bytes 294944 | tf_op jit(solution)/shard_map/ppermute | solution.py:552
  72.3 0.1 shard_map.109
  72.5 0.3 collective-permute-start.14
  72.7 3.5 %collective-permute-start.15 = (bf16[2,288,256]{2,1,0:T(8,128)(2,1)S(1)}, bf16[2,288,256]{2,1,0:T(8,128)(2,1)S(1)}, u32[]{:S(2)}, u32[]{:S(2)}) collective-permute-start(bf16[2,288,256]{2,1,0:T(8,128)(2,1)S(1)} %get-tuple-element.87), channel_id=1, source_target_pairs={{0,7},{1,2},{2,1},{3,4},{4,3},{5,6},{6,5},{7,0},{8,15},{9,10},{10,... | collective-permute-start | bytes 884744 | tf_op jit(solution)/shard_map/ppermute | solution.py:552
  76.2 4.1 %shard_map.107 = (f32[2,256,256]{2,1,0:T(8,128)S(1)}, f32[2,256,256]{2,1,0:T(8,128)S(1)}, bf16[1792,128]{1,0:T(8,128)(2,1)S(1)}, bf16[1792,128]{1,0:T(8,128)(2,1)S(1)}) custom-call(f32[2,8,896]{2,1,0:T(8,128)S(1)} %broadcast_in_dim.24.refs_0_, bf16[2,272,256]{2,1,0:T(8,128)(2,1)S(1)} %shard_map.95.refs_1_.refs_4_.refs_7_, bf16[2,1792,128]{2,1,0:T(8,128)(2,1)S(1)} %copy-done, ...), custom_call_target="tpu_custom_call" | custom-call | flops 2348810240 | bytes 6291456 | tf_op jit(solution)/shard_map/pallas_call | solution.py:525
  80.3 2.1 %collective-permute-start.9 = (bf16[1792,128]{1,0:T(8,128)(2,1)S(1)}, bf16[1792,128]{1,0:T(8,128)(2,1)S(1)}, u32[]{:S(2)}, u32[]{:S(2)}) collective-permute-start(bf16[1792,128]{1,0:T(8,128)(2,1)S(1)} %get-tuple-element.74), channel_id=1, source_target_pairs={{0,8},{1,9},{2,10},{3,11},{4,12},{5,13},{6,14},{7,15},{8,0},{9,1},... | collective-permute-start | bytes 1376264 | tf_op jit(solution)/shard_map/ppermute | solution.py:552
  82.4 0.0 collective-permute-done.14.refs_2_
  82.4 0.0 collective-permute-done.15.refs_3_
  82.4 0.1 shard_map.110
  82.5 1.2 %collective-permute-start.16 = (bf16[2,256,256]{2,1,0:T(8,128)(2,1)S(1)}, bf16[2,256,256]{2,1,0:T(8,128)(2,1)S(1)}, u32[]{:S(2)}, u32[]{:S(2)}) collective-permute-start(bf16[2,256,256]{2,1,0:T(8,128)(2,1)S(1)} %get-tuple-element.90), channel_id=1, source_target_pairs={{0,1},{1,0},{2,3},{3,2},{4,5},{5,4},{6,7},{7,6},{8,9},{9,8},{10,11... | collective-permute-start | bytes 786440 | tf_op jit(solution)/shard_map/ppermute | solution.py:552
  83.7 1.5 %collective-permute-start.17 = (bf16[2,256,256]{2,1,0:T(8,128)(2,1)S(1)}, bf16[2,256,256]{2,1,0:T(8,128)(2,1)S(1)}, u32[]{:S(2)}, u32[]{:S(2)}) collective-permute-start(bf16[2,256,256]{2,1,0:T(8,128)(2,1)S(1)} %get-tuple-element.91), channel_id=1, source_target_pairs={{0,7},{1,2},{2,1},{3,4},{4,3},{5,6},{6,5},{7,0},{8,15},{9,10},{10,... | collective-permute-start | bytes 786440 | tf_op jit(solution)/shard_map/ppermute | solution.py:552
  85.2 2.1 %collective-permute-start.18 = (f32[8,128]{1,0:T(8,128)S(1)}, f32[8,128]{1,0:T(8,128)S(1)}, u32[]{:S(2)}, u32[]{:S(2)}) collective-permute-start(f32[8,128]{1,0:T(8,128)S(1)} %get-tuple-element.92), channel_id=1, source_target_pairs={{0,8},{1,9},{2,10},{3,11},{4,12},{5,13},{6,14},{7,15},{8,0},{9,1},... | collective-permute-start | bytes 12296 | tf_op jit(solution)/shard_map/ppermute | solution.py:552
  87.2 1.7 %collective-permute-done.18 = f32[8,128]{1,0:T(8,128)S(1)} collective-permute-done((f32[8,128]{1,0:T(8,128)S(1)}, f32[8,128]{1,0:T(8,128)S(1)}, u32[]{:S(2)}, u32[]{:S(2)}) %collective-permute-start.18) | collective-permute-done | bytes 4128 | tf_op jit(solution)/shard_map/ppermute | solution.py:552
  88.9 5.2 %collective-permute-start.21 = (f32[8,128]{1,0:T(8,128)S(1)}, f32[8,128]{1,0:T(8,128)S(1)}, u32[]{:S(2)}, u32[]{:S(2)}) collective-permute-start(f32[8,128]{1,0:T(8,128)S(1)} %add.8.refs_0_), channel_id=1, source_target_pairs={{0,192},{1,193},{2,194},{3,195},{4,196},{5,197},{6,198},{7,199},{8... | collective-permute-start | bytes 12296 | tf_op jit(solution)/shard_map/ppermute | solution.py:552
  94.1 1.6 %collective-permute-done.21.refs_3_ = f32[8,128]{1,0:T(8,128)S(1)} collective-permute-done((f32[8,128]{1,0:T(8,128)S(1)}, f32[8,128]{1,0:T(8,128)S(1)}, u32[]{:S(2)}, u32[]{:S(2)}) %collective-permute-start.21) | collective-permute-done | bytes 4128 | tf_op jit(solution)/shard_map/ppermute | solution.py:552
  95.7 3.5 %collective-permute-done.20.refs_2_ = f32[8,128]{1,0:T(8,128)S(1)} collective-permute-done((f32[8,128]{1,0:T(8,128)S(1)}, f32[8,128]{1,0:T(8,128)S(1)}, u32[]{:S(2)}, u32[]{:S(2)}) %collective-permute-start.20) | collective-permute-done | bytes 4128 | tf_op jit(solution)/shard_map/ppermute | solution.py:552
  99.2 0.1 collective-permute-done.19.refs_1_
  99.3 0.1 shard_map.111
  99.4 2.0 %collective-permute-start.22 = (bf16[256,256]{1,0:T(8,128)(2,1)S(1)}, bf16[256,256]{1,0:T(8,128)(2,1)S(1)}, u32[]{:S(2)}, u32[]{:S(2)}) collective-permute-start(bf16[256,256]{1,0:T(8,128)(2,1)S(1)} %get-tuple-element.94), channel_id=1, source_target_pairs={{0,8},{1,9},{2,10},{3,11},{4,12},{5,13},{6,14},{7,15},{8,0},{9,1},... | collective-permute-start | bytes 393224 | tf_op jit(solution)/shard_map/ppermute | solution.py:552
  101.3 3.6 %collective-permute-start.24 = (f32[8,128]{1,0:T(8,128)S(1)}, f32[8,128]{1,0:T(8,128)S(1)}, u32[]{:S(2)}, u32[]{:S(2)}) collective-permute-start(f32[8,128]{1,0:T(8,128)S(1)} %get-tuple-element.95.refs_0_), channel_id=1, source_target_pairs={{0,32},{1,33},{2,34},{3,35},{4,36},{5,37},{6,38},{7,39},{8,40},{9,... | collective-permute-start | bytes 12296 | tf_op jit(solution)/shard_map/ppermute | solution.py:552
  104.9 0.1 collective-permute-start.23
  105.0 0.9 collective-permute-done.25.refs_3_
  105.9 2.1 %collective-permute-done.24.refs_2_ = f32[8,128]{1,0:T(8,128)S(1)} collective-permute-done((f32[8,128]{1,0:T(8,128)S(1)}, f32[8,128]{1,0:T(8,128)S(1)}, u32[]{:S(2)}, u32[]{:S(2)}) %collective-permute-start.24) | collective-permute-done | bytes 4128 | tf_op jit(solution)/shard_map/ppermute | solution.py:552
  107.9 1.2 %shard_map.112 = (bf16[128,3584]{1,0:T(8,128)(2,1)}, bf16[128,512]{1,0:T(8,128)(2,1)}, bf16[128,512]{1,0:T(8,128)(2,1)}, f32[1,28]{1,0:T(1,128)}) custom-call(s32[1]{0:T(128)} %bitcast.x_ref, bf16[1792,128]{1,0:T(8,128)(2,1)S(1)} %get-tuple-element.73.keep_ref, bf16[1792,128]{1,0:T(8,128)(2,1)S(1)} %collective-permute-done.9.got_ref, ...), custom_call_target="tpu_custom_call" | custom-call | flops 1024 | bytes 2097152 | tf_op jit(solution)/shard_map/pallas_call | solution.py:679
  (23 shorter events, 0.2 us)
Async XLA Ops:
  0.6 14.7 %copy-start.3 = (f32[28]{0:T(128)S(1)}, f32[28]{0:T(128)}, u32[]{:S(2)}) copy-start(f32[28]{0:T(128)} %param.11) | copy-start | bytes 340
  2.4 5.7 %copy-start.2 = (bf16[272,256]{1,0:T(8,128)(2,1)S(1)}, bf16[272,256]{1,0:T(8,128)(2,1)}, u32[]{:S(2)}) copy-start(bf16[272,256]{1,0:T(8,128)(2,1)} %get-tuple-element.54.keep_ref) | copy-start | bytes 417796
  2.4 5.7 %collective-permute-start = (bf16[272,256]{1,0:T(8,128)(2,1)}, bf16[272,256]{1,0:T(8,128)(2,1)S(1)}, u32[]{:S(2)}, u32[]{:S(2)}) collective-permute-start(bf16[272,256]{1,0:T(8,128)(2,1)} %get-tuple-element.52.after_ref), channel_id=1, source_target_pairs={{0,8},{1,9},{2,10},{3,11},{4,12},{5,13},{6,14},{7,15},{8,0},{9,1},... | collective-permute-start | bytes 417800 | tf_op jit(solution)/shard_map/ppermute | solution.py:552
  6.4 9.3 %copy-start = (bf16[2,1792,128]{2,1,0:T(8,128)(2,1)S(1)}, bf16[2,1792,128]{2,1,0:T(8,128)(2,1)}, u32[]{:S(2)}) copy-start(bf16[2,1792,128]{2,1,0:T(8,128)(2,1)} %get-tuple-element.55.refs_2_.refs_3_) | copy-start | bytes 2752516
  6.4 33.0 %collective-permute-start.1 = (bf16[2,1792,128]{2,1,0:T(8,128)(2,1)}, bf16[2,1792,128]{2,1,0:T(8,128)(2,1)S(1)}, u32[]{:S(2)}, u32[]{:S(2)}) collective-permute-start(bf16[2,1792,128]{2,1,0:T(8,128)(2,1)} %get-tuple-element.53.after_ref), channel_id=1, source_target_pairs={{0,8},{1,9},{2,10},{3,11},{4,12},{5,13},{6,14},{7,15},{8,0},{9,1},... | collective-permute-start | bytes 2752520 | tf_op jit(solution)/shard_map/ppermute | solution.py:552
  8.1 1.2 %copy-start.1 = (bf16[2,1792,128]{2,1,0:T(8,128)(2,1)S(1)}, bf16[2,1792,128]{2,1,0:T(8,128)(2,1)}, u32[]{:S(2)}) copy-start(bf16[2,1792,128]{2,1,0:T(8,128)(2,1)} %get-tuple-element.53.after_ref) | copy-start | bytes 2752516
  9.3 7.8 %collective-permute-start.3 = (bf16[2,272,256]{2,1,0:T(8,128)(2,1)S(1)}, bf16[2,272,256]{2,1,0:T(8,128)(2,1)S(1)}, u32[]{:S(2)}, u32[]{:S(2)}) collective-permute-start(bf16[2,272,256]{2,1,0:T(8,128)(2,1)S(1)} %shard_map.95.refs_1_.refs_4_.refs_7_), channel_id=1, source_target_pairs={{0,7},{1,2},{2,1},{3,4},{4,3},{5,6},{6,5},{7,0},{8,15},{9,10},{10,... | collective-permute-start | bytes 835592 | tf_op jit(solution)/shard_map/ppermute | solution.py:552
  11.3 9.5 %collective-permute-start.2 = (bf16[2,272,256]{2,1,0:T(8,128)(2,1)S(1)}, bf16[2,272,256]{2,1,0:T(8,128)(2,1)S(1)}, u32[]{:S(2)}, u32[]{:S(2)}) collective-permute-start(bf16[2,272,256]{2,1,0:T(8,128)(2,1)S(1)} %shard_map.95.refs_1_.refs_4_.refs_7_), channel_id=1, source_target_pairs={{0,1},{1,0},{2,3},{3,2},{4,5},{5,4},{6,7},{7,6},{8,9},{9,8},{10,11... | collective-permute-start | bytes 835592 | tf_op jit(solution)/shard_map/ppermute | solution.py:552
  20.9 6.7 %collective-permute-start.4 = (bf16[2,272,256]{2,1,0:T(8,128)(2,1)S(1)}, bf16[2,272,256]{2,1,0:T(8,128)(2,1)S(1)}, u32[]{:S(2)}, u32[]{:S(2)}) collective-permute-start(bf16[2,272,256]{2,1,0:T(8,128)(2,1)S(1)} %get-tuple-element.57.refs_5_.refs_6_), channel_id=1, source_target_pairs={{0,1},{1,0},{2,3},{3,2},{4,5},{5,4},{6,7},{7,6},{8,9},{9,8},{10,11... | collective-permute-start | bytes 835592 | tf_op jit(solution)/shard_map/ppermute | solution.py:552
  22.7 6.5 %collective-permute-start.5 = (bf16[2,272,256]{2,1,0:T(8,128)(2,1)S(1)}, bf16[2,272,256]{2,1,0:T(8,128)(2,1)S(1)}, u32[]{:S(2)}, u32[]{:S(2)}) collective-permute-start(bf16[2,272,256]{2,1,0:T(8,128)(2,1)S(1)} %get-tuple-element.58.refs_4_.refs_5_), channel_id=1, source_target_pairs={{0,7},{1,2},{2,1},{3,4},{4,3},{5,6},{6,5},{7,0},{8,15},{9,10},{10,... | collective-permute-start | bytes 835592 | tf_op jit(solution)/shard_map/ppermute | solution.py:552
  29.3 7.2 %collective-permute-start.6 = (bf16[2,272,256]{2,1,0:T(8,128)(2,1)S(1)}, bf16[2,272,256]{2,1,0:T(8,128)(2,1)S(1)}, u32[]{:S(2)}, u32[]{:S(2)}) collective-permute-start(bf16[2,272,256]{2,1,0:T(8,128)(2,1)S(1)} %get-tuple-element.61.refs_5_.refs_8_.refs_6_), channel_id=1, source_target_pairs={{0,1},{1,0},{2,3},{3,2},{4,5},{5,4},{6,7},{7,6},{8,9},{9,8},{10,11... | collective-permute-start | bytes 835592 | tf_op jit(solution)/shard_map/ppermute | solution.py:552
  30.9 6.5 %collective-permute-start.7 = (bf16[2,272,256]{2,1,0:T(8,128)(2,1)S(1)}, bf16[2,272,256]{2,1,0:T(8,128)(2,1)S(1)}, u32[]{:S(2)}, u32[]{:S(2)}) collective-permute-start(bf16[2,272,256]{2,1,0:T(8,128)(2,1)S(1)} %get-tuple-element.62.refs_4_.refs_7_.refs_5_), channel_id=1, source_target_pairs={{0,7},{1,2},{2,1},{3,4},{4,3},{5,6},{6,5},{7,0},{8,15},{9,10},{10,... | collective-permute-start | bytes 835592 | tf_op jit(solution)/shard_map/ppermute | solution.py:552
  37.5 6.6 %collective-permute-start.8 = (bf16[2,272,256]{2,1,0:T(8,128)(2,1)S(1)}, bf16[2,272,256]{2,1,0:T(8,128)(2,1)S(1)}, u32[]{:S(2)}, u32[]{:S(2)}) collective-permute-start(bf16[2,272,256]{2,1,0:T(8,128)(2,1)S(1)} %get-tuple-element.65.refs_10_.refs_6_), channel_id=1, source_target_pairs={{0,1},{1,0},{2,3},{3,2},{4,5},{5,4},{6,7},{7,6},{8,9},{9,8},{10,11... | collective-permute-start | bytes 835592 | tf_op jit(solution)/shard_map/ppermute | solution.py:552
  47.1 11.4 %collective-permute-start.10 = (bf16[2,256,256]{2,1,0:T(8,128)(2,1)S(1)}, bf16[2,256,256]{2,1,0:T(8,128)(2,1)S(1)}, u32[]{:S(2)}, u32[]{:S(2)}) collective-permute-start(bf16[2,256,256]{2,1,0:T(8,128)(2,1)S(1)} %convert_element_type.3), channel_id=1, source_target_pairs={{0,1},{1,0},{2,3},{3,2},{4,5},{5,4},{6,7},{7,6},{8,9},{9,8},{10,11... | collective-permute-start | bytes 786440 | tf_op jit(solution)/shard_map/ppermute | solution.py:552
  48.9 9.6 %collective-permute-start.11 = (f32[8,128]{1,0:T(8,128)S(1)}, f32[8,128]{1,0:T(8,128)S(1)}, u32[]{:S(2)}, u32[]{:S(2)}) collective-permute-start(f32[8,128]{1,0:T(8,128)S(1)} %get-tuple-element.83.refs_3_), channel_id=1, source_target_pairs={{0,4},{1,5},{2,6},{3,7},{4,0},{5,1},{6,2},{7,3},{8,12},{9,13},{10,... | collective-permute-start | bytes 12296 | tf_op jit(solution)/shard_map/ppermute | solution.py:552
  58.6 11.0 %collective-permute-start.12 = (bf16[2,288,256]{2,1,0:T(8,128)(2,1)S(1)}, bf16[2,288,256]{2,1,0:T(8,128)(2,1)S(1)}, u32[]{:S(2)}, u32[]{:S(2)}) collective-permute-start(bf16[2,288,256]{2,1,0:T(8,128)(2,1)S(1)} %get-tuple-element.84), channel_id=1, source_target_pairs={{0,1},{1,0},{2,3},{3,2},{4,5},{5,4},{6,7},{7,6},{8,9},{9,8},{10,11... | collective-permute-start | bytes 884744 | tf_op jit(solution)/shard_map/ppermute | solution.py:552
  61.8 10.5 %collective-permute-start.13 = (bf16[2,288,256]{2,1,0:T(8,128)(2,1)S(1)}, bf16[2,288,256]{2,1,0:T(8,128)(2,1)S(1)}, u32[]{:S(2)}, u32[]{:S(2)}) collective-permute-start(bf16[2,288,256]{2,1,0:T(8,128)(2,1)S(1)} %get-tuple-element.85), channel_id=1, source_target_pairs={{0,7},{1,2},{2,1},{3,4},{4,3},{5,6},{6,5},{7,0},{8,15},{9,10},{10,... | collective-permute-start | bytes 884744 | tf_op jit(solution)/shard_map/ppermute | solution.py:552
  72.5 9.9 %collective-permute-start.14 = (bf16[2,288,256]{2,1,0:T(8,128)(2,1)S(1)}, bf16[2,288,256]{2,1,0:T(8,128)(2,1)S(1)}, u32[]{:S(2)}, u32[]{:S(2)}) collective-permute-start(bf16[2,288,256]{2,1,0:T(8,128)(2,1)S(1)} %get-tuple-element.86), channel_id=1, source_target_pairs={{0,1},{1,0},{2,3},{3,2},{4,5},{5,4},{6,7},{7,6},{8,9},{9,8},{10,11... | collective-permute-start | bytes 884744 | tf_op jit(solution)/shard_map/ppermute | solution.py:552
  72.7 9.7 %collective-permute-start.15 = (bf16[2,288,256]{2,1,0:T(8,128)(2,1)S(1)}, bf16[2,288,256]{2,1,0:T(8,128)(2,1)S(1)}, u32[]{:S(2)}, u32[]{:S(2)}) collective-permute-start(bf16[2,288,256]{2,1,0:T(8,128)(2,1)S(1)} %get-tuple-element.87), channel_id=1, source_target_pairs={{0,7},{1,2},{2,1},{3,4},{4,3},{5,6},{6,5},{7,0},{8,15},{9,10},{10,... | collective-permute-start | bytes 884744 | tf_op jit(solution)/shard_map/ppermute | solution.py:552
  80.3 24.7 %collective-permute-start.9 = (bf16[1792,128]{1,0:T(8,128)(2,1)S(1)}, bf16[1792,128]{1,0:T(8,128)(2,1)S(1)}, u32[]{:S(2)}, u32[]{:S(2)}) collective-permute-start(bf16[1792,128]{1,0:T(8,128)(2,1)S(1)} %get-tuple-element.74), channel_id=1, source_target_pairs={{0,8},{1,9},{2,10},{3,11},{4,12},{5,13},{6,14},{7,15},{8,0},{9,1},... | collective-permute-start | bytes 1376264 | tf_op jit(solution)/shard_map/ppermute | solution.py:552
  82.5 16.7 %collective-permute-start.16 = (bf16[2,256,256]{2,1,0:T(8,128)(2,1)S(1)}, bf16[2,256,256]{2,1,0:T(8,128)(2,1)S(1)}, u32[]{:S(2)}, u32[]{:S(2)}) collective-permute-start(bf16[2,256,256]{2,1,0:T(8,128)(2,1)S(1)} %get-tuple-element.90), channel_id=1, source_target_pairs={{0,1},{1,0},{2,3},{3,2},{4,5},{5,4},{6,7},{7,6},{8,9},{9,8},{10,11... | collective-permute-start | bytes 786440 | tf_op jit(solution)/shard_map/ppermute | solution.py:552
  83.7 15.6 %collective-permute-start.17 = (bf16[2,256,256]{2,1,0:T(8,128)(2,1)S(1)}, bf16[2,256,256]{2,1,0:T(8,128)(2,1)S(1)}, u32[]{:S(2)}, u32[]{:S(2)}) collective-permute-start(bf16[2,256,256]{2,1,0:T(8,128)(2,1)S(1)} %get-tuple-element.91), channel_id=1, source_target_pairs={{0,7},{1,2},{2,1},{3,4},{4,3},{5,6},{6,5},{7,0},{8,15},{9,10},{10,... | collective-permute-start | bytes 786440 | tf_op jit(solution)/shard_map/ppermute | solution.py:552
  85.2 3.7 %collective-permute-start.18 = (f32[8,128]{1,0:T(8,128)S(1)}, f32[8,128]{1,0:T(8,128)S(1)}, u32[]{:S(2)}, u32[]{:S(2)}) collective-permute-start(f32[8,128]{1,0:T(8,128)S(1)} %get-tuple-element.92), channel_id=1, source_target_pairs={{0,8},{1,9},{2,10},{3,11},{4,12},{5,13},{6,14},{7,15},{8,0},{9,1},... | collective-permute-start | bytes 12296 | tf_op jit(solution)/shard_map/ppermute | solution.py:552
  88.9 6.7 %collective-permute-start.21 = (f32[8,128]{1,0:T(8,128)S(1)}, f32[8,128]{1,0:T(8,128)S(1)}, u32[]{:S(2)}, u32[]{:S(2)}) collective-permute-start(f32[8,128]{1,0:T(8,128)S(1)} %add.8.refs_0_), channel_id=1, source_target_pairs={{0,192},{1,193},{2,194},{3,195},{4,196},{5,197},{6,198},{7,199},{8... | collective-permute-start | bytes 12296 | tf_op jit(solution)/shard_map/ppermute | solution.py:552
  94.1 5.1 %collective-permute-start.20 = (f32[8,128]{1,0:T(8,128)S(1)}, f32[8,128]{1,0:T(8,128)S(1)}, u32[]{:S(2)}, u32[]{:S(2)}) collective-permute-start(f32[8,128]{1,0:T(8,128)S(1)} %add.8.refs_0_), channel_id=1, source_target_pairs={{0,128},{1,129},{2,130},{3,131},{4,132},{5,133},{6,134},{7,135},{8... | collective-permute-start | bytes 12296 | tf_op jit(solution)/shard_map/ppermute | solution.py:552
  95.6 3.6 %collective-permute-start.19 = (f32[8,128]{1,0:T(8,128)S(1)}, f32[8,128]{1,0:T(8,128)S(1)}, u32[]{:S(2)}, u32[]{:S(2)}) collective-permute-start(f32[8,128]{1,0:T(8,128)S(1)} %add.8.refs_0_), channel_id=1, source_target_pairs={{0,64},{1,65},{2,66},{3,67},{4,68},{5,69},{6,70},{7,71},{8,72},{9,... | collective-permute-start | bytes 12296 | tf_op jit(solution)/shard_map/ppermute | solution.py:552
  99.4 8.6 %collective-permute-start.22 = (bf16[256,256]{1,0:T(8,128)(2,1)S(1)}, bf16[256,256]{1,0:T(8,128)(2,1)S(1)}, u32[]{:S(2)}, u32[]{:S(2)}) collective-permute-start(bf16[256,256]{1,0:T(8,128)(2,1)S(1)} %get-tuple-element.94), channel_id=1, source_target_pairs={{0,8},{1,9},{2,10},{3,11},{4,12},{5,13},{6,14},{7,15},{8,0},{9,1},... | collective-permute-start | bytes 393224 | tf_op jit(solution)/shard_map/ppermute | solution.py:552
  101.3 4.5 %collective-permute-start.25 = (f32[8,128]{1,0:T(8,128)S(1)}, f32[8,128]{1,0:T(8,128)S(1)}, u32[]{:S(2)}, u32[]{:S(2)}) collective-permute-start(f32[8,128]{1,0:T(8,128)S(1)} %get-tuple-element.95.refs_0_), channel_id=1, source_target_pairs={{0,48},{1,49},{2,50},{3,51},{4,52},{5,53},{6,54},{7,55},{8,56},{9,... | collective-permute-start | bytes 12296 | tf_op jit(solution)/shard_map/ppermute | solution.py:552
  101.3 6.6 %collective-permute-start.24 = (f32[8,128]{1,0:T(8,128)S(1)}, f32[8,128]{1,0:T(8,128)S(1)}, u32[]{:S(2)}, u32[]{:S(2)}) collective-permute-start(f32[8,128]{1,0:T(8,128)S(1)} %get-tuple-element.95.refs_0_), channel_id=1, source_target_pairs={{0,32},{1,33},{2,34},{3,35},{4,36},{5,37},{6,38},{7,39},{8,40},{9,... | collective-permute-start | bytes 12296 | tf_op jit(solution)/shard_map/ppermute | solution.py:552
  104.9 3.0 %collective-permute-start.23 = (f32[8,128]{1,0:T(8,128)S(1)}, f32[8,128]{1,0:T(8,128)S(1)}, u32[]{:S(2)}, u32[]{:S(2)}) collective-permute-start(f32[8,128]{1,0:T(8,128)S(1)} %get-tuple-element.95.refs_0_), channel_id=1, source_target_pairs={{0,16},{1,17},{2,18},{3,19},{4,20},{5,21},{6,22},{7,23},{8,24},{9,... | collective-permute-start | bytes 12296 | tf_op jit(solution)/shard_map/ppermute | solution.py:552

commit v5 on v4

--- a/solution.py
+++ b/solution.py
@@ -285,7 +285,8 @@
     if not is_first:
         prior_ref, refs = refs[0], refs[1:]
     if is_last:
-        final_ref, scale_ref, state, key_c, value_c, pos_c = refs
+        final_ref, scale_ref, far_ref, query_sum, state, key_c, value_c, pos_c = refs[:8]
+        key_sum, value_sum = refs[8:]
     else:
         state, token_ref, key_c, value_c, pos_c = refs
         token_ref[...] = jnp.zeros_like(token_ref)
@@ -298,7 +299,7 @@
     for blocks, slots in work:
         span = tile_of(blocks)
         top = jnp.maximum(tops[0], tops[1]) if len(slots) == 2 else tops[slots[0]]
-        length, _ = place(blocks, first, top, key_c, value_c, pos_c, span)
+        length, entries = place(blocks, first, top, key_c, value_c, pos_c, span)
 
         def tile(step, _, slots=slots, span=span):
             at = pl.multiple_of(step * span, span)
@@ -360,6 +361,23 @@
                     lane == place_at, jnp.sum(spread, axis=1, keepdims=True), 0.0
                 )
     scale_ref[...] = scale_row
+    query_sum[...] = jnp.zeros_like(query_sum)
+    grads_work(
+        rate_ref,
+        (kept_ref, got_ref),
+        final_ref,
+        key_c,
+        value_c,
+        pos_c,
+        key_sum,
+        value_sum,
+        query_sum,
+        query_rows,
+        tops,
+        length,
+        entries,
+        [far_ref],
+    )
 
 
 def grads_tile(
@@ -400,6 +418,65 @@
     query_sum[slot * KV_HEADS + g] += product(keys, score_low, TN)
 
 
+def grads_work(
+    rate_ref,
+    work_refs,
+    final_ref,
+    key_c,
+    value_c,
+    pos_c,
+    key_sum,
+    value_sum,
+    query_sum,
+    query_rows,
+    tops,
+    length,
+    entries,
+    outs,
+):
+    def tile(step, _):
+        at = pl.multiple_of(step * TILE, TILE)
+        key_pos = pos_c[pl.ds(at, TILE), :]
+        lowest = jnp.min(key_pos)
+        for g in range(KV_HEADS):
+            key_sum[g, pl.ds(at, TILE), :] = jnp.zeros((TILE, HEAD), F32)
+            value_sum[g, pl.ds(at, TILE), :] = jnp.zeros((TILE, HEAD), F32)
+        for slot in range(2):
+
+            @pl.when(lowest <= tops[slot])
+            def _(slot=slot):
+                mask = key_pos <= query_rows[slot]
+                for g in range(KV_HEADS):
+                    grads_tile(
+                        rate_ref,
+                        work_refs[slot],
+                        final_ref,
+                        key_c,
+                        value_c,
+                        key_sum,
+                        value_sum,
+                        query_sum,
+                        mask,
+                        at,
+                        slot,
+                        g,
+                    )
+
+        return 0
+
+    lax.fori_loop(0, (length + TILE - 1) // TILE, tile, 0)
+    row = lax.broadcasted_iota(jnp.int32, (ROWS, HEAD), 0)
+    for slot, starts, counts in entries:
+        for out, at, n in zip(outs, starts, counts):
+            at = pl.multiple_of(at, 16)
+            for g in range(KV_HEADS):
+                lanes = slice(g * HEAD, (g + 1) * HEAD)
+                for number, total in enumerate((key_sum, value_sum)):
+                    out[slot, number * ROWS : (number + 1) * ROWS, lanes] = jnp.where(
+                        row < n, total[g, pl.ds(at, ROWS), :], 0.0
+                    )
+
+
 def grads_body(count, is_first, is_last, *refs):
     rate_ref, own_ref, kept_ref, got_ref, final_ref = refs[:5]
     blocks = refs[5 : 5 + count]
@@ -419,47 +496,22 @@
     elif is_last:
         query_sum[...] = prior_ref[...]
 
-    def tile(step, _):
-        at = pl.multiple_of(step * TILE, TILE)
-        key_pos = pos_c[pl.ds(at, TILE), :]
-        lowest = jnp.min(key_pos)
-        for g in range(KV_HEADS):
-            key_sum[g, pl.ds(at, TILE), :] = jnp.zeros((TILE, HEAD), F32)
-            value_sum[g, pl.ds(at, TILE), :] = jnp.zeros((TILE, HEAD), F32)
-        for slot in range(2):
-
-            @pl.when(lowest <= tops[slot])
-            def _(slot=slot):
-                mask = key_pos <= query_rows[slot]
-                for g in range(KV_HEADS):
-                    grads_tile(
-                        rate_ref,
-                        (kept_ref, got_ref)[slot],
-                        final_ref,
-                        key_c,
-                        value_c,
-                        key_sum,
-                        value_sum,
-                        query_sum,
-                        mask,
-                        at,
-                        slot,
-                        g,
-                    )
-
-        return 0
-
-    lax.fori_loop(0, (length + TILE - 1) // TILE, tile, 0)
-    row = lax.broadcasted_iota(jnp.int32, (ROWS, HEAD), 0)
-    for slot, starts, counts in entries:
-        for out, at, n in zip(outs, starts, counts):
-            at = pl.multiple_of(at, 16)
-            for g in range(KV_HEADS):
-                lanes = slice(g * HEAD, (g + 1) * HEAD)
-                for number, total in enumerate((key_sum, value_sum)):
-                    out[slot, number * ROWS : (number + 1) * ROWS, lanes] = jnp.where(
-                        row < n, total[g, pl.ds(at, ROWS), :], 0.0
-                    )
+    grads_work(
+        rate_ref,
+        (kept_ref, got_ref),
+        final_ref,
+        key_c,
+        value_c,
+        pos_c,
+        key_sum,
+        value_sum,
+        query_sum,
+        query_rows,
+        tops,
+        length,
+        entries,
+        outs,
+    )
     if is_last:
         for slot in range(2):
             for g in range(KV_HEADS):
@@ -481,23 +533,29 @@
 
 
 STATE = jax.ShapeDtypeStruct((2 * KV_HEADS, 5, 8, WIDE), F32)
+PART = jax.ShapeDtypeStruct((2, 2 * ROWS, KV_HEADS * HEAD), F32)
+SUMS = jax.ShapeDtypeStruct((2 * KV_HEADS, HEAD, WIDE), F32)
 SMALL = jax.ShapeDtypeStruct((8, ROWS), F32)
 FINAL = jax.ShapeDtypeStruct((2 * KV_HEADS, 8, WIDE), F32)
 
 
 def stats(rate, own, kept, got, jobs, prior=None, is_last=False):
     if is_last:
-        outs = [FINAL, jax.ShapeDtypeStruct((8, ROWS), F32)]
+        outs = [FINAL, SMALL, PART, SUMS]
         scratch = [pltpu.VMEM(STATE.shape, F32)]
     else:
         outs, scratch = [STATE, SMALL], []
     blocks = [block for some, _ in jobs for block in some]
     operands = [rate, own, kept, got, *blocks] + ([] if prior is None else [prior])
     sizes = [(len(some), slots) for some, slots in jobs]
+    rest = []
+    if is_last:
+        size = 2 * ROWS + TILE
+        rest = [pltpu.VMEM((KV_HEADS, size, HEAD), F32), pltpu.VMEM((KV_HEADS, size, HEAD), F32)]
     return call(
         functools.partial(stats_body, sizes, prior is None, is_last),
         outs,
-        scratch + compact_scratch(max(count for count, _ in sizes)),
+        scratch + compact_scratch(max(count for count, _ in sizes)) + rest,
         sum(count * len(slots) for count, slots in sizes) * ROWS * 2 * HEADS * ROWS * HEAD * 4,
         4 << 20,
         [pl.BlockSpec(memory_space=pltpu.VMEM)] * len(operands),
@@ -630,7 +688,7 @@
     a.append(swap(b[3], even))
     jobs = [([own, a[1], b[1], a[2], b[2]], (1,)), ([a[3], b[3]], (0, 1))]
     state, token = stats(rate, own, kept, got, jobs, state)
-    final, scale = stats(rate, own, kept, got, [([a[4]], (0, 1))], state, is_last=True)
+    final, scale, far, sums = stats(rate, own, kept, got, [([a[4]], (0, 1))], state, is_last=True)
 
     total_devices = lax.axis_size("dp") * size
 
@@ -650,7 +708,6 @@
         )(*parts, *arrived, *scales)
 
     scales = exchange(scale, (4,))
-    far, sums = grads(rate, own, kept, got, final, [a[4]])
     from_even = swap(far.astype(BF16), even)
     part_a, part_b, sums = grads(rate, own, kept, got, final, [a[3], b[3]], sums)
     to_a, to_b, scale = hop(3, (part_a, part_b), (from_even,), scales)

time: 110 us -> 111 us (level); the launches traced: 109 us -> 109 us
  Pallas kernels: 30 us -> 34.1 us
  starting transfers between devices: 50.5 us -> 48 us
  waiting for transfers between devices: 26.3 us -> 24.2 us
    pallas_call x5, Pallas kernels: 11 us -> 13.6 us  [stats(): call(functools.partial(stats_body, sizes, prior is None, is_last), outs,...]
    ppermute x26, starting transfers between devices: 50.5 us -> 48 us  [swap(): return lax.ppermute(array, axis, pairs)]
    ppermute x26, waiting for transfers between devices: 26.3 us -> 24.2 us  [swap(): return lax.ppermute(array, axis, pairs)]
    pallas_call x4 -> x3, Pallas kernels: 12.5 us -> 13.9 us  [grads(): call(functools.partial(grads_body, count, prior is None, is_last), outs,...]
  transfers between devices with their start and end apart: 26 -> 26, of which waited for: 16 -> 14; matrix products, arithmetic and copies ran while one was open for 0% -> 0% of each run, Pallas kernels for 22% -> 26%
where the time goes in v5:
time: 111 us; the launch traced here: 109 us
  starting transfers between devices  48 us (43%)
  Pallas kernels  34.1 us (31%)
  waiting for transfers between devices  24.2 us (22%)
  local copies, waits for them, and re-layouts  1.37 us (1%)
    ppermute x26, starting transfers between devices, swap(): return lax.ppermute(array, axis, pairs)  48 us
    ppermute x26, waiting for transfers between devices, swap(): return lax.ppermute(array, axis, pairs)  24.2 us
    pallas_call x3, Pallas kernels, grads(): call(functools.partial(grads_body, count, prior is None, is_last), outs,...  13.9 us
    pallas_call x5, Pallas kernels, stats(): call(functools.partial(stats_body, sizes, prior is None, is_last), outs,...  13.6 us
    pallas_call x1, Pallas kernels, local(): call(pack_queries_body, [work, work], [pltpu.VMEM((ROWS, 2 * HEADS * HEAD...  3.05 us
  transfers between devices with their start and end apart: 26, of which 14 were waited for; matrix products, arithmetic and copies ran while one was open for 0% of the time, Pallas kernels for 26%

profile of v5, /device:TPU:38, one launch (start us, length us, event | category | flops | bytes accessed | tf_op | source)
XLA Modules:
  0.0 108.6 jit_solution(3705021556510073366)
XLA Ops:
  0.7 1.7 %shard_map.93 = (bf16[272,256]{1,0:T(8,128)(2,1)}, bf16[272,256]{1,0:T(8,128)(2,1)}) custom-call(s32[1]{0:T(128)} %bitcast.x_ref, bf16[128,512]{1,0:T(8,128)(2,1)} %bitcast.16, bf16[128,512]{1,0:T(8,128)(2,1)} %bitcast.17, s32[1,128]{1,0:T(1,128)} %pos_in.1), custom_call_target="tpu_custom_call" | custom-call | flops 1024 | bytes 1048576 | tf_op jit(solution)/shard_map/pallas_call | solution.py:618
  2.4 0.9 collective-permute-start
  3.3 3.0 %shard_map.94 = (bf16[2,1792,128]{2,1,0:T(8,128)(2,1)}, bf16[2,1792,128]{2,1,0:T(8,128)(2,1)}) custom-call(s32[1]{0:T(128)} %bitcast.x_ref, bf16[272,256]{1,0:T(8,128)(2,1)} %get-tuple-element.52.after_ref, bf16[128,3584]{1,0:T(8,128)(2,1)} %bitcast.14, bf16[128,3584]{1,0:T(8,128)(2,1)} %bitcast.15), custom_call_target="tpu_custom_call" | custom-call | flops 1024 | bytes 4194304 | tf_op jit(solution)/shard_map/pallas_call | solution.py:634
  6.4 0.0 copy-start
  6.4 1.3 %collective-permute-start.1 = (bf16[2,1792,128]{2,1,0:T(8,128)(2,1)}, bf16[2,1792,128]{2,1,0:T(8,128)(2,1)S(1)}, u32[]{:S(2)}, u32[]{:S(2)}) collective-permute-start(bf16[2,1792,128]{2,1,0:T(8,128)(2,1)} %get-tuple-element.53.after_ref), channel_id=1, source_target_pairs={{0,8},{1,9},{2,10},{3,11},{4,12},{5,13},{6,14},{7,15},{8,0},{9,1},... | collective-permute-start | bytes 2752520 | tf_op jit(solution)/shard_map/ppermute | solution.py:610
  7.6 0.4 collective-permute-done.got_ref
  8.1 1.2 %copy-done.1 = bf16[2,1792,128]{2,1,0:T(8,128)(2,1)S(1)} copy-done((bf16[2,1792,128]{2,1,0:T(8,128)(2,1)S(1)}, bf16[2,1792,128]{2,1,0:T(8,128)(2,1)}, u32[]{:S(2)}) %copy-start.1) | copy-done | bytes 917528
  9.3 2.0 %collective-permute-start.3 = (bf16[2,272,256]{2,1,0:T(8,128)(2,1)S(1)}, bf16[2,272,256]{2,1,0:T(8,128)(2,1)S(1)}, u32[]{:S(2)}, u32[]{:S(2)}) collective-permute-start(bf16[2,272,256]{2,1,0:T(8,128)(2,1)S(1)} %shard_map.95.refs_1_.refs_4_.refs_7_), channel_id=1, source_target_pairs={{0,7},{1,2},{2,1},{3,4},{4,3},{5,6},{6,5},{7,0},{8,15},{9,10},{10,... | collective-permute-start | bytes 835592 | tf_op jit(solution)/shard_map/ppermute | solution.py:610
  11.3 4.0 %collective-permute-start.2 = (bf16[2,272,256]{2,1,0:T(8,128)(2,1)S(1)}, bf16[2,272,256]{2,1,0:T(8,128)(2,1)S(1)}, u32[]{:S(2)}, u32[]{:S(2)}) collective-permute-start(bf16[2,272,256]{2,1,0:T(8,128)(2,1)S(1)} %shard_map.95.refs_1_.refs_4_.refs_7_), channel_id=1, source_target_pairs={{0,1},{1,0},{2,3},{3,2},{4,5},{5,4},{6,7},{7,6},{8,9},{9,8},{10,11... | collective-permute-start | bytes 835592 | tf_op jit(solution)/shard_map/ppermute | solution.py:610
  15.4 0.1 dynamic-slice_multiply_fusion
  15.4 0.1 broadcast_in_dim.21
  15.5 0.1 broadcast_bitcast_fusion
  15.6 1.8 %shard_map.96 = (f32[4,5,8,896]{3,2,1,0:T(8,128)S(1)}, f32[8,128]{1,0:T(8,128)S(1)}) custom-call(f32[2,8,896]{2,1,0:T(8,128)S(1)} %broadcast_in_dim.24.refs_0_, bf16[2,272,256]{2,1,0:T(8,128)(2,1)S(1)} %shard_map.95.refs_1_.refs_4_.refs_7_, bf16[2,1792,128]{2,1,0:T(8,128)(2,1)S(1)} %copy-done, bf16[2,1792,128]{2,1,0:T(8,128)(2,1)S(1)} %copy-done, ...), custom_call_target="tpu_custom_call" | custom-call | flops 234881024 | bytes 4194304 | tf_op jit(solution)/shard_map/pallas_call | solution.py:555
  17.4 0.0 collective-permute-done.3.refs_1_
  17.4 3.5 %collective-permute-done.2.refs_0_ = bf16[2,272,256]{2,1,0:T(8,128)(2,1)S(1)} collective-permute-done((bf16[2,272,256]{2,1,0:T(8,128)(2,1)S(1)}, bf16[2,272,256]{2,1,0:T(8,128)(2,1)S(1)}, u32[]{:S(2)}, u32[]{:S(2)}) %collective-permute-start.2) | collective-permute-done | bytes 278560 | tf_op jit(solution)/shard_map/ppermute | solution.py:610
  20.9 1.8 %collective-permute-start.4 = (bf16[2,272,256]{2,1,0:T(8,128)(2,1)S(1)}, bf16[2,272,256]{2,1,0:T(8,128)(2,1)S(1)}, u32[]{:S(2)}, u32[]{:S(2)}) collective-permute-start(bf16[2,272,256]{2,1,0:T(8,128)(2,1)S(1)} %get-tuple-element.57.refs_5_.refs_6_), channel_id=1, source_target_pairs={{0,1},{1,0},{2,3},{3,2},{4,5},{5,4},{6,7},{7,6},{8,9},{9,8},{10,11... | collective-permute-start | bytes 835592 | tf_op jit(solution)/shard_map/ppermute | solution.py:610
  22.7 1.0 collective-permute-start.5
  23.7 2.8 %shard_map.98 = (f32[4,5,8,896]{3,2,1,0:T(8,128)S(1)}, f32[8,128]{1,0:T(8,128)S(1)}) custom-call(f32[2,8,896]{2,1,0:T(8,128)S(1)} %broadcast_in_dim.24.refs_0_, bf16[2,272,256]{2,1,0:T(8,128)(2,1)S(1)} %shard_map.95.refs_1_.refs_4_.refs_7_, bf16[2,1792,128]{2,1,0:T(8,128)(2,1)S(1)} %copy-done, bf16[2,1792,128]{2,1,0:T(8,128)(2,1)S(1)} %copy-done, ...), custom_call_target="tpu_custom_call" | custom-call | flops 469762048 | bytes 4194304 | tf_op jit(solution)/shard_map/pallas_call | solution.py:555
  26.5 1.0 collective-permute-done.4.refs_0_
  27.6 1.7 %collective-permute-done.5.refs_1_ = bf16[2,272,256]{2,1,0:T(8,128)(2,1)S(1)} collective-permute-done((bf16[2,272,256]{2,1,0:T(8,128)(2,1)S(1)}, bf16[2,272,256]{2,1,0:T(8,128)(2,1)S(1)}, u32[]{:S(2)}, u32[]{:S(2)}) %collective-permute-start.5) | collective-permute-done | bytes 278560 | tf_op jit(solution)/shard_map/ppermute | solution.py:610
  29.3 1.6 %collective-permute-start.6 = (bf16[2,272,256]{2,1,0:T(8,128)(2,1)S(1)}, bf16[2,272,256]{2,1,0:T(8,128)(2,1)S(1)}, u32[]{:S(2)}, u32[]{:S(2)}) collective-permute-start(bf16[2,272,256]{2,1,0:T(8,128)(2,1)S(1)} %get-tuple-element.61.refs_5_.refs_8_.refs_6_), channel_id=1, source_target_pairs={{0,1},{1,0},{2,3},{3,2},{4,5},{5,4},{6,7},{7,6},{8,9},{9,8},{10,11... | collective-permute-start | bytes 835592 | tf_op jit(solution)/shard_map/ppermute | solution.py:610
  30.9 1.0 collective-permute-start.7
  31.9 2.1 %shard_map.100 = (f32[4,5,8,896]{3,2,1,0:T(8,128)S(1)}, f32[8,128]{1,0:T(8,128)S(1)}) custom-call(f32[2,8,896]{2,1,0:T(8,128)S(1)} %broadcast_in_dim.24.refs_0_, bf16[2,272,256]{2,1,0:T(8,128)(2,1)S(1)} %shard_map.95.refs_1_.refs_4_.refs_7_, bf16[2,1792,128]{2,1,0:T(8,128)(2,1)S(1)} %copy-done, bf16[2,1792,128]{2,1,0:T(8,128)(2,1)S(1)} %copy-done, ...), custom_call_target="tpu_custom_call" | custom-call | flops 469762048 | bytes 4194304 | tf_op jit(solution)/shard_map/pallas_call | solution.py:555
  34.0 2.5 %collective-permute-done.6.refs_0_ = bf16[2,272,256]{2,1,0:T(8,128)(2,1)S(1)} collective-permute-done((bf16[2,272,256]{2,1,0:T(8,128)(2,1)S(1)}, bf16[2,272,256]{2,1,0:T(8,128)(2,1)S(1)}, u32[]{:S(2)}, u32[]{:S(2)}) %collective-permute-start.6) | collective-permute-done | bytes 278560 | tf_op jit(solution)/shard_map/ppermute | solution.py:610
  36.5 1.0 collective-permute-done.7.refs_1_
  37.5 1.8 %collective-permute-start.8 = (bf16[2,272,256]{2,1,0:T(8,128)(2,1)S(1)}, bf16[2,272,256]{2,1,0:T(8,128)(2,1)S(1)}, u32[]{:S(2)}, u32[]{:S(2)}) collective-permute-start(bf16[2,272,256]{2,1,0:T(8,128)(2,1)S(1)} %get-tuple-element.65.refs_10_.refs_6_), channel_id=1, source_target_pairs={{0,1},{1,0},{2,3},{3,2},{4,5},{5,4},{6,7},{7,6},{8,9},{9,8},{10,11... | collective-permute-start | bytes 835592 | tf_op jit(solution)/shard_map/ppermute | solution.py:610
  39.3 4.3 %shard_map.102 = (f32[4,5,8,896]{3,2,1,0:T(8,128)S(1)}, f32[8,128]{1,0:T(8,128)}) custom-call(f32[2,8,896]{2,1,0:T(8,128)S(1)} %broadcast_in_dim.24.refs_0_, bf16[2,272,256]{2,1,0:T(8,128)(2,1)S(1)} %shard_map.95.refs_1_.refs_4_.refs_7_, bf16[2,1792,128]{2,1,0:T(8,128)(2,1)S(1)} %copy-done, bf16[2,1792,128]{2,1,0:T(8,128)(2,1)S(1)} %collective-permute-done.1.refs_3_, ...), custom_call_target="tpu_custom_call" | custom-call | flops 2113929216 | bytes 4194304 | tf_op jit(solution)/shard_map/pallas_call | solution.py:555
  43.6 0.5 collective-permute-done.8.refs_4_
  44.1 2.6 %shard_map.103 = (f32[4,8,896]{2,1,0:T(8,128)S(1)}, f32[8,128]{1,0:T(8,128)S(1)}, f32[2,256,256]{2,1,0:T(8,128)S(1)}, f32[4,128,896]{2,1,0:T(8,128)S(1)}) custom-call(f32[2,8,896]{2,1,0:T(8,128)S(1)} %broadcast_in_dim.24.refs_0_, bf16[2,272,256]{2,1,0:T(8,128)(2,1)S(1)} %shard_map.95.refs_1_.refs_4_.refs_7_, bf16[2,1792,128]{2,1,0:T(8,128)(2,1)S(1)} %copy-done, ...), custom_call_target="tpu_custom_call" | custom-call | flops 469762048 | bytes 4194304 | tf_op jit(solution)/shard_map/pallas_call | solution.py:555
  46.8 2.0 %collective-permute-start.10 = (bf16[2,256,256]{2,1,0:T(8,128)(2,1)S(1)}, bf16[2,256,256]{2,1,0:T(8,128)(2,1)S(1)}, u32[]{:S(2)}, u32[]{:S(2)}) collective-permute-start(bf16[2,256,256]{2,1,0:T(8,128)(2,1)S(1)} %convert_element_type.3), channel_id=1, source_target_pairs={{0,1},{1,0},{2,3},{3,2},{4,5},{5,4},{6,7},{7,6},{8,9},{9,8},{10,11... | collective-permute-start | bytes 786440 | tf_op jit(solution)/shard_map/ppermute | solution.py:610
  48.8 6.7 %collective-permute-start.11 = (f32[8,128]{1,0:T(8,128)S(1)}, f32[8,128]{1,0:T(8,128)S(1)}, u32[]{:S(2)}, u32[]{:S(2)}) collective-permute-start(f32[8,128]{1,0:T(8,128)S(1)} %get-tuple-element.83.refs_3_), channel_id=1, source_target_pairs={{0,4},{1,5},{2,6},{3,7},{4,0},{5,1},{6,2},{7,3},{8,12},{9,13},{10,... | collective-permute-start | bytes 12296 | tf_op jit(solution)/shard_map/ppermute | solution.py:610
  55.6 2.7 %shard_map.104 = (f32[2,256,256]{2,1,0:T(8,128)S(1)}, f32[2,256,256]{2,1,0:T(8,128)S(1)}, f32[4,128,896]{2,1,0:T(8,128)S(1)}) custom-call(f32[2,8,896]{2,1,0:T(8,128)S(1)} %broadcast_in_dim.24.refs_0_, bf16[2,272,256]{2,1,0:T(8,128)(2,1)S(1)} %shard_map.95.refs_1_.refs_4_.refs_7_, ...), custom_call_target="tpu_custom_call", output_to_operand_aliasing={{2}: (7, {})} | custom-call | flops 2348810240 | bytes 6291456 | tf_op jit(solution)/shard_map/pallas_call | solution.py:583
  58.2 1.8 %collective-permute-done.11.refs_4_ = f32[8,128]{1,0:T(8,128)S(1)} collective-permute-done((f32[8,128]{1,0:T(8,128)S(1)}, f32[8,128]{1,0:T(8,128)S(1)}, u32[]{:S(2)}, u32[]{:S(2)}) %collective-permute-start.11) | collective-permute-done | bytes 4128 | tf_op jit(solution)/shard_map/ppermute | solution.py:610
  60.0 0.1 shard_map.107
  60.1 3.9 %collective-permute-start.12 = (bf16[2,288,256]{2,1,0:T(8,128)(2,1)S(1)}, bf16[2,288,256]{2,1,0:T(8,128)(2,1)S(1)}, u32[]{:S(2)}, u32[]{:S(2)}) collective-permute-start(bf16[2,288,256]{2,1,0:T(8,128)(2,1)S(1)} %get-tuple-element.84), channel_id=1, source_target_pairs={{0,1},{1,0},{2,3},{3,2},{4,5},{5,4},{6,7},{7,6},{8,9},{9,8},{10,11... | collective-permute-start | bytes 884744 | tf_op jit(solution)/shard_map/ppermute | solution.py:610
  64.1 2.6 %collective-permute-start.13 = (bf16[2,288,256]{2,1,0:T(8,128)(2,1)S(1)}, bf16[2,288,256]{2,1,0:T(8,128)(2,1)S(1)}, u32[]{:S(2)}, u32[]{:S(2)}) collective-permute-start(bf16[2,288,256]{2,1,0:T(8,128)(2,1)S(1)} %get-tuple-element.85), channel_id=1, source_target_pairs={{0,7},{1,2},{2,1},{3,4},{4,3},{5,6},{6,5},{7,0},{8,15},{9,10},{10,... | collective-permute-start | bytes 884744 | tf_op jit(solution)/shard_map/ppermute | solution.py:610
  66.6 6.2 %shard_map.105 = (f32[2,256,256]{2,1,0:T(8,128)S(1)}, f32[2,256,256]{2,1,0:T(8,128)S(1)}, f32[2,256,256]{2,1,0:T(8,128)S(1)}, f32[4,128,896]{2,1,0:T(8,128)S(1)}) custom-call(f32[2,8,896]{2,1,0:T(8,128)S(1)} %broadcast_in_dim.24.refs_0_, bf16[2,272,256]{2,1,0:T(8,128)(2,1)S(1)} %shard_map.95.refs_1_.refs_4_.refs_7_, ...), custom_call_target="tpu_custom_call", output_to_operand_aliasing={{3}: (8, {})} | custom-call | flops 3523215360 | bytes 6291456 | tf_op jit(solution)/shard_map/pallas_call | solution.py:583
  72.8 0.0 collective-permute-done.13.refs_3_
  72.9 0.2 shard_map.108
  73.0 1.0 collective-permute-start.14
  74.1 2.1 %collective-permute-start.15 = (bf16[2,288,256]{2,1,0:T(8,128)(2,1)S(1)}, bf16[2,288,256]{2,1,0:T(8,128)(2,1)S(1)}, u32[]{:S(2)}, u32[]{:S(2)}) collective-permute-start(bf16[2,288,256]{2,1,0:T(8,128)(2,1)S(1)} %get-tuple-element.87), channel_id=1, source_target_pairs={{0,7},{1,2},{2,1},{3,4},{4,3},{5,6},{6,5},{7,0},{8,15},{9,10},{10,... | collective-permute-start | bytes 884744 | tf_op jit(solution)/shard_map/ppermute | solution.py:610
  76.2 5.1 %shard_map.106 = (f32[2,256,256]{2,1,0:T(8,128)S(1)}, f32[2,256,256]{2,1,0:T(8,128)S(1)}, bf16[1792,128]{1,0:T(8,128)(2,1)S(1)}, bf16[1792,128]{1,0:T(8,128)(2,1)S(1)}) custom-call(f32[2,8,896]{2,1,0:T(8,128)S(1)} %broadcast_in_dim.24.refs_0_, bf16[2,272,256]{2,1,0:T(8,128)(2,1)S(1)} %shard_map.95.refs_1_.refs_4_.refs_7_, bf16[2,1792,128]{2,1,0:T(8,128)(2,1)S(1)} %copy-done, ...), custom_call_target="tpu_custom_call" | custom-call | flops 2348810240 | bytes 6291456 | tf_op jit(solution)/shard_map/pallas_call | solution.py:583
  81.3 2.1 %collective-permute-start.9 = (bf16[1792,128]{1,0:T(8,128)(2,1)S(1)}, bf16[1792,128]{1,0:T(8,128)(2,1)S(1)}, u32[]{:S(2)}, u32[]{:S(2)}) collective-permute-start(bf16[1792,128]{1,0:T(8,128)(2,1)S(1)} %get-tuple-element.74), channel_id=1, source_target_pairs={{0,8},{1,9},{2,10},{3,11},{4,12},{5,13},{6,14},{7,15},{8,0},{9,1},... | collective-permute-start | bytes 1376264 | tf_op jit(solution)/shard_map/ppermute | solution.py:610
  83.3 0.1 shard_map.109
  83.5 0.1 collective-permute-start.16
  83.6 0.9 collective-permute-start.17
  84.4 2.0 %collective-permute-start.18 = (f32[8,128]{1,0:T(8,128)S(1)}, f32[8,128]{1,0:T(8,128)S(1)}, u32[]{:S(2)}, u32[]{:S(2)}) collective-permute-start(f32[8,128]{1,0:T(8,128)S(1)} %get-tuple-element.92), channel_id=1, source_target_pairs={{0,8},{1,9},{2,10},{3,11},{4,12},{5,13},{6,14},{7,15},{8,0},{9,1},... | collective-permute-start | bytes 12296 | tf_op jit(solution)/shard_map/ppermute | solution.py:610
  86.4 4.9 %collective-permute-done.18 = f32[8,128]{1,0:T(8,128)S(1)} collective-permute-done((f32[8,128]{1,0:T(8,128)S(1)}, f32[8,128]{1,0:T(8,128)S(1)}, u32[]{:S(2)}, u32[]{:S(2)}) %collective-permute-start.18) | collective-permute-done | bytes 4128 | tf_op jit(solution)/shard_map/ppermute | solution.py:610
  91.3 3.6 %collective-permute-start.21 = (f32[8,128]{1,0:T(8,128)S(1)}, f32[8,128]{1,0:T(8,128)S(1)}, u32[]{:S(2)}, u32[]{:S(2)}) collective-permute-start(f32[8,128]{1,0:T(8,128)S(1)} %add.8.refs_0_), channel_id=1, source_target_pairs={{0,192},{1,193},{2,194},{3,195},{4,196},{5,197},{6,198},{7,199},{8... | collective-permute-start | bytes 12296 | tf_op jit(solution)/shard_map/ppermute | solution.py:610
  94.9 1.6 %collective-permute-done.21.refs_3_ = f32[8,128]{1,0:T(8,128)S(1)} collective-permute-done((f32[8,128]{1,0:T(8,128)S(1)}, f32[8,128]{1,0:T(8,128)S(1)}, u32[]{:S(2)}, u32[]{:S(2)}) %collective-permute-start.21) | collective-permute-done | bytes 4128 | tf_op jit(solution)/shard_map/ppermute | solution.py:610
  96.5 3.5 %collective-permute-done.20.refs_2_ = f32[8,128]{1,0:T(8,128)S(1)} collective-permute-done((f32[8,128]{1,0:T(8,128)S(1)}, f32[8,128]{1,0:T(8,128)S(1)}, u32[]{:S(2)}, u32[]{:S(2)}) %collective-permute-start.20) | collective-permute-done | bytes 4128 | tf_op jit(solution)/shard_map/ppermute | solution.py:610
  100.0 0.1 collective-permute-done.19.refs_1_
  100.1 0.0 collective-permute-done.16.sent_a
  100.1 0.0 collective-permute-done.17.sent_b
  100.1 0.1 shard_map.110
  100.2 2.1 %collective-permute-start.22 = (bf16[256,256]{1,0:T(8,128)(2,1)S(1)}, bf16[256,256]{1,0:T(8,128)(2,1)S(1)}, u32[]{:S(2)}, u32[]{:S(2)}) collective-permute-start(bf16[256,256]{1,0:T(8,128)(2,1)S(1)} %get-tuple-element.94), channel_id=1, source_target_pairs={{0,8},{1,9},{2,10},{3,11},{4,12},{5,13},{6,14},{7,15},{8,0},{9,1},... | collective-permute-start | bytes 393224 | tf_op jit(solution)/shard_map/ppermute | solution.py:610
  102.3 1.1 %collective-permute-start.24 = (f32[8,128]{1,0:T(8,128)S(1)}, f32[8,128]{1,0:T(8,128)S(1)}, u32[]{:S(2)}, u32[]{:S(2)}) collective-permute-start(f32[8,128]{1,0:T(8,128)S(1)} %get-tuple-element.95.refs_0_), channel_id=1, source_target_pairs={{0,32},{1,33},{2,34},{3,35},{4,36},{5,37},{6,38},{7,39},{8,40},{9,... | collective-permute-start | bytes 12296 | tf_op jit(solution)/shard_map/ppermute | solution.py:610
  103.4 2.2 %collective-permute-start.23 = (f32[8,128]{1,0:T(8,128)S(1)}, f32[8,128]{1,0:T(8,128)S(1)}, u32[]{:S(2)}, u32[]{:S(2)}) collective-permute-start(f32[8,128]{1,0:T(8,128)S(1)} %get-tuple-element.95.refs_0_), channel_id=1, source_target_pairs={{0,16},{1,17},{2,18},{3,19},{4,20},{5,21},{6,22},{7,23},{8,24},{9,... | collective-permute-start | bytes 12296 | tf_op jit(solution)/shard_map/ppermute | solution.py:610
  105.7 0.0 collective-permute-done.9.got_ref
  105.7 1.2 %collective-permute-done.25.refs_3_ = f32[8,128]{1,0:T(8,128)S(1)} collective-permute-done((f32[8,128]{1,0:T(8,128)S(1)}, f32[8,128]{1,0:T(8,128)S(1)}, u32[]{:S(2)}, u32[]{:S(2)}) %collective-permute-start.25) | collective-permute-done | bytes 4128 | tf_op jit(solution)/shard_map/ppermute | solution.py:610
  106.8 0.6 collective-permute-done.24.refs_2_
  107.4 0.0 collective-permute-done.23.refs_1_
  107.4 0.0 collective-permute-done.22.other_ref
  107.4 1.2 %shard_map.111 = (bf16[128,3584]{1,0:T(8,128)(2,1)}, bf16[128,512]{1,0:T(8,128)(2,1)}, bf16[128,512]{1,0:T(8,128)(2,1)}, f32[1,28]{1,0:T(1,128)}) custom-call(s32[1]{0:T(128)} %bitcast.x_ref, bf16[1792,128]{1,0:T(8,128)(2,1)S(1)} %get-tuple-element.73.keep_ref, bf16[1792,128]{1,0:T(8,128)(2,1)S(1)} %collective-permute-done.9.got_ref, ...), custom_call_target="tpu_custom_call" | custom-call | flops 1024 | bytes 2097152 | tf_op jit(solution)/shard_map/pallas_call | solution.py:736
  (22 shorter events, 0.2 us)
Async XLA Ops:
  0.6 14.7 %copy-start.3 = (f32[28]{0:T(128)S(1)}, f32[28]{0:T(128)}, u32[]{:S(2)}) copy-start(f32[28]{0:T(128)} %param.11) | copy-start | bytes 340
  2.4 5.7 %copy-start.2 = (bf16[272,256]{1,0:T(8,128)(2,1)S(1)}, bf16[272,256]{1,0:T(8,128)(2,1)}, u32[]{:S(2)}) copy-start(bf16[272,256]{1,0:T(8,128)(2,1)} %get-tuple-element.54.keep_ref) | copy-start | bytes 417796
  2.4 5.7 %collective-permute-start = (bf16[272,256]{1,0:T(8,128)(2,1)}, bf16[272,256]{1,0:T(8,128)(2,1)S(1)}, u32[]{:S(2)}, u32[]{:S(2)}) collective-permute-start(bf16[272,256]{1,0:T(8,128)(2,1)} %get-tuple-element.52.after_ref), channel_id=1, source_target_pairs={{0,8},{1,9},{2,10},{3,11},{4,12},{5,13},{6,14},{7,15},{8,0},{9,1},... | collective-permute-start | bytes 417800 | tf_op jit(solution)/shard_map/ppermute | solution.py:610
  6.4 9.3 %copy-start = (bf16[2,1792,128]{2,1,0:T(8,128)(2,1)S(1)}, bf16[2,1792,128]{2,1,0:T(8,128)(2,1)}, u32[]{:S(2)}) copy-start(bf16[2,1792,128]{2,1,0:T(8,128)(2,1)} %get-tuple-element.55.refs_2_.refs_3_) | copy-start | bytes 2752516
  6.4 33.0 %collective-permute-start.1 = (bf16[2,1792,128]{2,1,0:T(8,128)(2,1)}, bf16[2,1792,128]{2,1,0:T(8,128)(2,1)S(1)}, u32[]{:S(2)}, u32[]{:S(2)}) collective-permute-start(bf16[2,1792,128]{2,1,0:T(8,128)(2,1)} %get-tuple-element.53.after_ref), channel_id=1, source_target_pairs={{0,8},{1,9},{2,10},{3,11},{4,12},{5,13},{6,14},{7,15},{8,0},{9,1},... | collective-permute-start | bytes 2752520 | tf_op jit(solution)/shard_map/ppermute | solution.py:610
  8.1 1.2 %copy-start.1 = (bf16[2,1792,128]{2,1,0:T(8,128)(2,1)S(1)}, bf16[2,1792,128]{2,1,0:T(8,128)(2,1)}, u32[]{:S(2)}) copy-start(bf16[2,1792,128]{2,1,0:T(8,128)(2,1)} %get-tuple-element.53.after_ref) | copy-start | bytes 2752516
  9.3 8.1 %collective-permute-start.3 = (bf16[2,272,256]{2,1,0:T(8,128)(2,1)S(1)}, bf16[2,272,256]{2,1,0:T(8,128)(2,1)S(1)}, u32[]{:S(2)}, u32[]{:S(2)}) collective-permute-start(bf16[2,272,256]{2,1,0:T(8,128)(2,1)S(1)} %shard_map.95.refs_1_.refs_4_.refs_7_), channel_id=1, source_target_pairs={{0,7},{1,2},{2,1},{3,4},{4,3},{5,6},{6,5},{7,0},{8,15},{9,10},{10,... | collective-permute-start | bytes 835592 | tf_op jit(solution)/shard_map/ppermute | solution.py:610
  11.3 9.5 %collective-permute-start.2 = (bf16[2,272,256]{2,1,0:T(8,128)(2,1)S(1)}, bf16[2,272,256]{2,1,0:T(8,128)(2,1)S(1)}, u32[]{:S(2)}, u32[]{:S(2)}) collective-permute-start(bf16[2,272,256]{2,1,0:T(8,128)(2,1)S(1)} %shard_map.95.refs_1_.refs_4_.refs_7_), channel_id=1, source_target_pairs={{0,1},{1,0},{2,3},{3,2},{4,5},{5,4},{6,7},{7,6},{8,9},{9,8},{10,11... | collective-permute-start | bytes 835592 | tf_op jit(solution)/shard_map/ppermute | solution.py:610
  20.9 6.7 %collective-permute-start.4 = (bf16[2,272,256]{2,1,0:T(8,128)(2,1)S(1)}, bf16[2,272,256]{2,1,0:T(8,128)(2,1)S(1)}, u32[]{:S(2)}, u32[]{:S(2)}) collective-permute-start(bf16[2,272,256]{2,1,0:T(8,128)(2,1)S(1)} %get-tuple-element.57.refs_5_.refs_6_), channel_id=1, source_target_pairs={{0,1},{1,0},{2,3},{3,2},{4,5},{5,4},{6,7},{7,6},{8,9},{9,8},{10,11... | collective-permute-start | bytes 835592 | tf_op jit(solution)/shard_map/ppermute | solution.py:610
  22.7 6.5 %collective-permute-start.5 = (bf16[2,272,256]{2,1,0:T(8,128)(2,1)S(1)}, bf16[2,272,256]{2,1,0:T(8,128)(2,1)S(1)}, u32[]{:S(2)}, u32[]{:S(2)}) collective-permute-start(bf16[2,272,256]{2,1,0:T(8,128)(2,1)S(1)} %get-tuple-element.58.refs_4_.refs_5_), channel_id=1, source_target_pairs={{0,7},{1,2},{2,1},{3,4},{4,3},{5,6},{6,5},{7,0},{8,15},{9,10},{10,... | collective-permute-start | bytes 835592 | tf_op jit(solution)/shard_map/ppermute | solution.py:610
  29.3 7.2 %collective-permute-start.6 = (bf16[2,272,256]{2,1,0:T(8,128)(2,1)S(1)}, bf16[2,272,256]{2,1,0:T(8,128)(2,1)S(1)}, u32[]{:S(2)}, u32[]{:S(2)}) collective-permute-start(bf16[2,272,256]{2,1,0:T(8,128)(2,1)S(1)} %get-tuple-element.61.refs_5_.refs_8_.refs_6_), channel_id=1, source_target_pairs={{0,1},{1,0},{2,3},{3,2},{4,5},{5,4},{6,7},{7,6},{8,9},{9,8},{10,11... | collective-permute-start | bytes 835592 | tf_op jit(solution)/shard_map/ppermute | solution.py:610
  30.9 6.5 %collective-permute-start.7 = (bf16[2,272,256]{2,1,0:T(8,128)(2,1)S(1)}, bf16[2,272,256]{2,1,0:T(8,128)(2,1)S(1)}, u32[]{:S(2)}, u32[]{:S(2)}) collective-permute-start(bf16[2,272,256]{2,1,0:T(8,128)(2,1)S(1)} %get-tuple-element.62.refs_4_.refs_7_.refs_5_), channel_id=1, source_target_pairs={{0,7},{1,2},{2,1},{3,4},{4,3},{5,6},{6,5},{7,0},{8,15},{9,10},{10,... | collective-permute-start | bytes 835592 | tf_op jit(solution)/shard_map/ppermute | solution.py:610
  37.5 6.6 %collective-permute-start.8 = (bf16[2,272,256]{2,1,0:T(8,128)(2,1)S(1)}, bf16[2,272,256]{2,1,0:T(8,128)(2,1)S(1)}, u32[]{:S(2)}, u32[]{:S(2)}) collective-permute-start(bf16[2,272,256]{2,1,0:T(8,128)(2,1)S(1)} %get-tuple-element.65.refs_10_.refs_6_), channel_id=1, source_target_pairs={{0,1},{1,0},{2,3},{3,2},{4,5},{5,4},{6,7},{7,6},{8,9},{9,8},{10,11... | collective-permute-start | bytes 835592 | tf_op jit(solution)/shard_map/ppermute | solution.py:610
  46.8 13.2 %collective-permute-start.10 = (bf16[2,256,256]{2,1,0:T(8,128)(2,1)S(1)}, bf16[2,256,256]{2,1,0:T(8,128)(2,1)S(1)}, u32[]{:S(2)}, u32[]{:S(2)}) collective-permute-start(bf16[2,256,256]{2,1,0:T(8,128)(2,1)S(1)} %convert_element_type.3), channel_id=1, source_target_pairs={{0,1},{1,0},{2,3},{3,2},{4,5},{5,4},{6,7},{7,6},{8,9},{9,8},{10,11... | collective-permute-start | bytes 786440 | tf_op jit(solution)/shard_map/ppermute | solution.py:610
  48.8 11.2 %collective-permute-start.11 = (f32[8,128]{1,0:T(8,128)S(1)}, f32[8,128]{1,0:T(8,128)S(1)}, u32[]{:S(2)}, u32[]{:S(2)}) collective-permute-start(f32[8,128]{1,0:T(8,128)S(1)} %get-tuple-element.83.refs_3_), channel_id=1, source_target_pairs={{0,4},{1,5},{2,6},{3,7},{4,0},{5,1},{6,2},{7,3},{8,12},{9,13},{10,... | collective-permute-start | bytes 12296 | tf_op jit(solution)/shard_map/ppermute | solution.py:610
  60.1 12.7 %collective-permute-start.12 = (bf16[2,288,256]{2,1,0:T(8,128)(2,1)S(1)}, bf16[2,288,256]{2,1,0:T(8,128)(2,1)S(1)}, u32[]{:S(2)}, u32[]{:S(2)}) collective-permute-start(bf16[2,288,256]{2,1,0:T(8,128)(2,1)S(1)} %get-tuple-element.84), channel_id=1, source_target_pairs={{0,1},{1,0},{2,3},{3,2},{4,5},{5,4},{6,7},{7,6},{8,9},{9,8},{10,11... | collective-permute-start | bytes 884744 | tf_op jit(solution)/shard_map/ppermute | solution.py:610
  64.1 8.8 %collective-permute-start.13 = (bf16[2,288,256]{2,1,0:T(8,128)(2,1)S(1)}, bf16[2,288,256]{2,1,0:T(8,128)(2,1)S(1)}, u32[]{:S(2)}, u32[]{:S(2)}) collective-permute-start(bf16[2,288,256]{2,1,0:T(8,128)(2,1)S(1)} %get-tuple-element.85), channel_id=1, source_target_pairs={{0,7},{1,2},{2,1},{3,4},{4,3},{5,6},{6,5},{7,0},{8,15},{9,10},{10,... | collective-permute-start | bytes 884744 | tf_op jit(solution)/shard_map/ppermute | solution.py:610
  73.0 10.3 %collective-permute-start.14 = (bf16[2,288,256]{2,1,0:T(8,128)(2,1)S(1)}, bf16[2,288,256]{2,1,0:T(8,128)(2,1)S(1)}, u32[]{:S(2)}, u32[]{:S(2)}) collective-permute-start(bf16[2,288,256]{2,1,0:T(8,128)(2,1)S(1)} %get-tuple-element.86), channel_id=1, source_target_pairs={{0,1},{1,0},{2,3},{3,2},{4,5},{5,4},{6,7},{7,6},{8,9},{9,8},{10,11... | collective-permute-start | bytes 884744 | tf_op jit(solution)/shard_map/ppermute | solution.py:610
  74.1 9.3 %collective-permute-start.15 = (bf16[2,288,256]{2,1,0:T(8,128)(2,1)S(1)}, bf16[2,288,256]{2,1,0:T(8,128)(2,1)S(1)}, u32[]{:S(2)}, u32[]{:S(2)}) collective-permute-start(bf16[2,288,256]{2,1,0:T(8,128)(2,1)S(1)} %get-tuple-element.87), channel_id=1, source_target_pairs={{0,7},{1,2},{2,1},{3,4},{4,3},{5,6},{6,5},{7,0},{8,15},{9,10},{10,... | collective-permute-start | bytes 884744 | tf_op jit(solution)/shard_map/ppermute | solution.py:610
  81.3 24.4 %collective-permute-start.9 = (bf16[1792,128]{1,0:T(8,128)(2,1)S(1)}, bf16[1792,128]{1,0:T(8,128)(2,1)S(1)}, u32[]{:S(2)}, u32[]{:S(2)}) collective-permute-start(bf16[1792,128]{1,0:T(8,128)(2,1)S(1)} %get-tuple-element.74), channel_id=1, source_target_pairs={{0,8},{1,9},{2,10},{3,11},{4,12},{5,13},{6,14},{7,15},{8,0},{9,1},... | collective-permute-start | bytes 1376264 | tf_op jit(solution)/shard_map/ppermute | solution.py:610
  83.5 16.6 %collective-permute-start.16 = (bf16[2,256,256]{2,1,0:T(8,128)(2,1)S(1)}, bf16[2,256,256]{2,1,0:T(8,128)(2,1)S(1)}, u32[]{:S(2)}, u32[]{:S(2)}) collective-permute-start(bf16[2,256,256]{2,1,0:T(8,128)(2,1)S(1)} %get-tuple-element.90), channel_id=1, source_target_pairs={{0,1},{1,0},{2,3},{3,2},{4,5},{5,4},{6,7},{7,6},{8,9},{9,8},{10,11... | collective-permute-start | bytes 786440 | tf_op jit(solution)/shard_map/ppermute | solution.py:610
  83.6 16.5 %collective-permute-start.17 = (bf16[2,256,256]{2,1,0:T(8,128)(2,1)S(1)}, bf16[2,256,256]{2,1,0:T(8,128)(2,1)S(1)}, u32[]{:S(2)}, u32[]{:S(2)}) collective-permute-start(bf16[2,256,256]{2,1,0:T(8,128)(2,1)S(1)} %get-tuple-element.91), channel_id=1, source_target_pairs={{0,7},{1,2},{2,1},{3,4},{4,3},{5,6},{6,5},{7,0},{8,15},{9,10},{10,... | collective-permute-start | bytes 786440 | tf_op jit(solution)/shard_map/ppermute | solution.py:610
  84.4 6.8 %collective-permute-start.18 = (f32[8,128]{1,0:T(8,128)S(1)}, f32[8,128]{1,0:T(8,128)S(1)}, u32[]{:S(2)}, u32[]{:S(2)}) collective-permute-start(f32[8,128]{1,0:T(8,128)S(1)} %get-tuple-element.92), channel_id=1, source_target_pairs={{0,8},{1,9},{2,10},{3,11},{4,12},{5,13},{6,14},{7,15},{8,0},{9,1},... | collective-permute-start | bytes 12296 | tf_op jit(solution)/shard_map/ppermute | solution.py:610
  91.3 5.2 %collective-permute-start.21 = (f32[8,128]{1,0:T(8,128)S(1)}, f32[8,128]{1,0:T(8,128)S(1)}, u32[]{:S(2)}, u32[]{:S(2)}) collective-permute-start(f32[8,128]{1,0:T(8,128)S(1)} %add.8.refs_0_), channel_id=1, source_target_pairs={{0,192},{1,193},{2,194},{3,195},{4,196},{5,197},{6,198},{7,199},{8... | collective-permute-start | bytes 12296 | tf_op jit(solution)/shard_map/ppermute | solution.py:610
  94.9 5.1 %collective-permute-start.20 = (f32[8,128]{1,0:T(8,128)S(1)}, f32[8,128]{1,0:T(8,128)S(1)}, u32[]{:S(2)}, u32[]{:S(2)}) collective-permute-start(f32[8,128]{1,0:T(8,128)S(1)} %add.8.refs_0_), channel_id=1, source_target_pairs={{0,128},{1,129},{2,130},{3,131},{4,132},{5,133},{6,134},{7,135},{8... | collective-permute-start | bytes 12296 | tf_op jit(solution)/shard_map/ppermute | solution.py:610
  96.5 3.6 %collective-permute-start.19 = (f32[8,128]{1,0:T(8,128)S(1)}, f32[8,128]{1,0:T(8,128)S(1)}, u32[]{:S(2)}, u32[]{:S(2)}) collective-permute-start(f32[8,128]{1,0:T(8,128)S(1)} %add.8.refs_0_), channel_id=1, source_target_pairs={{0,64},{1,65},{2,66},{3,67},{4,68},{5,69},{6,70},{7,71},{8,72},{9,... | collective-permute-start | bytes 12296 | tf_op jit(solution)/shard_map/ppermute | solution.py:610
  100.2 7.3 %collective-permute-start.22 = (bf16[256,256]{1,0:T(8,128)(2,1)S(1)}, bf16[256,256]{1,0:T(8,128)(2,1)S(1)}, u32[]{:S(2)}, u32[]{:S(2)}) collective-permute-start(bf16[256,256]{1,0:T(8,128)(2,1)S(1)} %get-tuple-element.94), channel_id=1, source_target_pairs={{0,8},{1,9},{2,10},{3,11},{4,12},{5,13},{6,14},{7,15},{8,0},{9,1},... | collective-permute-start | bytes 393224 | tf_op jit(solution)/shard_map/ppermute | solution.py:610
  102.3 4.5 %collective-permute-start.25 = (f32[8,128]{1,0:T(8,128)S(1)}, f32[8,128]{1,0:T(8,128)S(1)}, u32[]{:S(2)}, u32[]{:S(2)}) collective-permute-start(f32[8,128]{1,0:T(8,128)S(1)} %get-tuple-element.95.refs_0_), channel_id=1, source_target_pairs={{0,48},{1,49},{2,50},{3,51},{4,52},{5,53},{6,54},{7,55},{8,56},{9,... | collective-permute-start | bytes 12296 | tf_op jit(solution)/shard_map/ppermute | solution.py:610
  102.3 5.1 %collective-permute-start.24 = (f32[8,128]{1,0:T(8,128)S(1)}, f32[8,128]{1,0:T(8,128)S(1)}, u32[]{:S(2)}, u32[]{:S(2)}) collective-permute-start(f32[8,128]{1,0:T(8,128)S(1)} %get-tuple-element.95.refs_0_), channel_id=1, source_target_pairs={{0,32},{1,33},{2,34},{3,35},{4,36},{5,37},{6,38},{7,39},{8,40},{9,... | collective-permute-start | bytes 12296 | tf_op jit(solution)/shard_map/ppermute | solution.py:610
  103.4 4.0 %collective-permute-start.23 = (f32[8,128]{1,0:T(8,128)S(1)}, f32[8,128]{1,0:T(8,128)S(1)}, u32[]{:S(2)}, u32[]{:S(2)}) collective-permute-start(f32[8,128]{1,0:T(8,128)S(1)} %get-tuple-element.95.refs_0_), channel_id=1, source_target_pairs={{0,16},{1,17},{2,18},{3,19},{4,20},{5,21},{6,22},{7,23},{8,24},{9,... | collective-permute-start | bytes 12296 | tf_op jit(solution)/shard_map/ppermute | solution.py:610

commit v6 on v5

--- a/solution.py
+++ b/solution.py
@@ -722,7 +722,7 @@
     to_a, to_b, scale = hop(1, (part_a, part_b), (sent_a, sent_b), [scale, beside])
     sent_a, sent_b = swap(to_a, even), swap(to_b, odd)
     scales = exchange(scale, (8,))
-    scales = exchange(scales[0] + scales[1], (64, 128, 192))
+    scales = exchange(scales[0] + scales[1], (16, 32, 48))
     ours, theirs, scale = call(
         last_hop_body,
         [jax.ShapeDtypeStruct((2 * ROWS, width), BF16)] * 2 + [SMALL],
@@ -732,7 +732,7 @@
         [vmem] * 7,
     )(near, sent_a, sent_b, *scales)
     other = swap(theirs, across)
-    scales = exchange(scale, (16, 32, 48))
+    scales = exchange(scale, (64, 128, 192))
     query_out, key_out, value_out, scale_out = call(
         finish_body,
         [

time: 111 us -> 109 us (0.982); the launches traced: 109 us -> 109 us
  waiting for transfers between devices: 24.2 us -> 30 us
  starting transfers between devices: 48 us -> 44.1 us
  Pallas kernels: 34.1 us -> 32.3 us
    ppermute x26, waiting for transfers between devices: 24.2 us -> 30 us  [swap(): return lax.ppermute(array, axis, pairs)]
    ppermute x26, starting transfers between devices: 48 us -> 44.1 us  [swap(): return lax.ppermute(array, axis, pairs)]
    pallas_call x3, Pallas kernels: 13.9 us -> 12.1 us  [grads(): call(functools.partial(grads_body, count, prior is None, is_last), outs,...]
  transfers between devices with their start and end apart: 26 -> 26, of which waited for: 14 -> 16; matrix products, arithmetic and copies ran while one was open for 0% -> 0% of each run, Pallas kernels for 26% -> 24%
where the time goes in v6:
time: 109 us
  starting transfers between devices  44.1 us (40%)
  Pallas kernels  32.3 us (30%)
  waiting for transfers between devices  30 us (28%)
  local copies, waits for them, and re-layouts  1.37 us (1%)
    ppermute x26, starting transfers between devices, swap(): return lax.ppermute(array, axis, pairs)  44.1 us
    ppermute x26, waiting for transfers between devices, swap(): return lax.ppermute(array, axis, pairs)  30 us
    pallas_call x5, Pallas kernels, stats(): call(functools.partial(stats_body, sizes, prior is None, is_last), outs,...  13.6 us
    pallas_call x3, Pallas kernels, grads(): call(functools.partial(grads_body, count, prior is None, is_last), outs,...  12.1 us
    pallas_call x1, Pallas kernels, local(): call(pack_queries_body, [work, work], [pltpu.VMEM((ROWS, 2 * HEADS * HEAD...  3.05 us
  transfers between devices with their start and end apart: 26, of which 16 were waited for; matrix products, arithmetic and copies ran while one was open for 0% of the time, Pallas kernels for 24%

profile of v6, /device:TPU:38, one launch (start us, length us, event | category | flops | bytes accessed | tf_op | source)
XLA Modules:
  0.0 108.7 jit_solution(10311574128383747027)
XLA Ops:
  0.7 1.7 %shard_map.93 = (bf16[272,256]{1,0:T(8,128)(2,1)}, bf16[272,256]{1,0:T(8,128)(2,1)}) custom-call(s32[1]{0:T(128)} %bitcast.x_ref, bf16[128,512]{1,0:T(8,128)(2,1)} %bitcast.16, bf16[128,512]{1,0:T(8,128)(2,1)} %bitcast.17, s32[1,128]{1,0:T(1,128)} %pos_in.1), custom_call_target="tpu_custom_call" | custom-call | flops 1024 | bytes 1048576 | tf_op jit(solution)/shard_map/pallas_call | solution.py:618
  2.4 0.9 collective-permute-start
  3.3 3.0 %shard_map.94 = (bf16[2,1792,128]{2,1,0:T(8,128)(2,1)}, bf16[2,1792,128]{2,1,0:T(8,128)(2,1)}) custom-call(s32[1]{0:T(128)} %bitcast.x_ref, bf16[272,256]{1,0:T(8,128)(2,1)} %get-tuple-element.52.after_ref, bf16[128,3584]{1,0:T(8,128)(2,1)} %bitcast.14, bf16[128,3584]{1,0:T(8,128)(2,1)} %bitcast.15), custom_call_target="tpu_custom_call" | custom-call | flops 1024 | bytes 4194304 | tf_op jit(solution)/shard_map/pallas_call | solution.py:634
  6.4 0.0 copy-start
  6.4 1.3 %collective-permute-start.1 = (bf16[2,1792,128]{2,1,0:T(8,128)(2,1)}, bf16[2,1792,128]{2,1,0:T(8,128)(2,1)S(1)}, u32[]{:S(2)}, u32[]{:S(2)}) collective-permute-start(bf16[2,1792,128]{2,1,0:T(8,128)(2,1)} %get-tuple-element.53.after_ref), channel_id=1, source_target_pairs={{0,8},{1,9},{2,10},{3,11},{4,12},{5,13},{6,14},{7,15},{8,0},{9,1},... | collective-permute-start | bytes 2752520 | tf_op jit(solution)/shard_map/ppermute | solution.py:610
  7.6 0.4 collective-permute-done.got_ref
  8.1 1.2 %copy-done.1 = bf16[2,1792,128]{2,1,0:T(8,128)(2,1)S(1)} copy-done((bf16[2,1792,128]{2,1,0:T(8,128)(2,1)S(1)}, bf16[2,1792,128]{2,1,0:T(8,128)(2,1)}, u32[]{:S(2)}) %copy-start.1) | copy-done | bytes 917528
  9.3 2.0 %collective-permute-start.3 = (bf16[2,272,256]{2,1,0:T(8,128)(2,1)S(1)}, bf16[2,272,256]{2,1,0:T(8,128)(2,1)S(1)}, u32[]{:S(2)}, u32[]{:S(2)}) collective-permute-start(bf16[2,272,256]{2,1,0:T(8,128)(2,1)S(1)} %shard_map.95.refs_1_.refs_4_.refs_7_), channel_id=1, source_target_pairs={{0,7},{1,2},{2,1},{3,4},{4,3},{5,6},{6,5},{7,0},{8,15},{9,10},{10,... | collective-permute-start | bytes 835592 | tf_op jit(solution)/shard_map/ppermute | solution.py:610
  11.3 4.0 %collective-permute-start.2 = (bf16[2,272,256]{2,1,0:T(8,128)(2,1)S(1)}, bf16[2,272,256]{2,1,0:T(8,128)(2,1)S(1)}, u32[]{:S(2)}, u32[]{:S(2)}) collective-permute-start(bf16[2,272,256]{2,1,0:T(8,128)(2,1)S(1)} %shard_map.95.refs_1_.refs_4_.refs_7_), channel_id=1, source_target_pairs={{0,1},{1,0},{2,3},{3,2},{4,5},{5,4},{6,7},{7,6},{8,9},{9,8},{10,11... | collective-permute-start | bytes 835592 | tf_op jit(solution)/shard_map/ppermute | solution.py:610
  15.4 0.1 dynamic-slice_multiply_fusion
  15.4 0.1 broadcast_in_dim.21
  15.5 0.1 broadcast_bitcast_fusion
  15.6 1.8 %shard_map.96 = (f32[4,5,8,896]{3,2,1,0:T(8,128)S(1)}, f32[8,128]{1,0:T(8,128)S(1)}) custom-call(f32[2,8,896]{2,1,0:T(8,128)S(1)} %broadcast_in_dim.24.refs_0_, bf16[2,272,256]{2,1,0:T(8,128)(2,1)S(1)} %shard_map.95.refs_1_.refs_4_.refs_7_, bf16[2,1792,128]{2,1,0:T(8,128)(2,1)S(1)} %copy-done, bf16[2,1792,128]{2,1,0:T(8,128)(2,1)S(1)} %copy-done, ...), custom_call_target="tpu_custom_call" | custom-call | flops 234881024 | bytes 4194304 | tf_op jit(solution)/shard_map/pallas_call | solution.py:555
  17.4 3.5 %collective-permute-done.2.refs_0_ = bf16[2,272,256]{2,1,0:T(8,128)(2,1)S(1)} collective-permute-done((bf16[2,272,256]{2,1,0:T(8,128)(2,1)S(1)}, bf16[2,272,256]{2,1,0:T(8,128)(2,1)S(1)}, u32[]{:S(2)}, u32[]{:S(2)}) %collective-permute-start.2) | collective-permute-done | bytes 278560 | tf_op jit(solution)/shard_map/ppermute | solution.py:610
  20.9 1.8 %collective-permute-start.4 = (bf16[2,272,256]{2,1,0:T(8,128)(2,1)S(1)}, bf16[2,272,256]{2,1,0:T(8,128)(2,1)S(1)}, u32[]{:S(2)}, u32[]{:S(2)}) collective-permute-start(bf16[2,272,256]{2,1,0:T(8,128)(2,1)S(1)} %get-tuple-element.57.refs_5_.refs_6_), channel_id=1, source_target_pairs={{0,1},{1,0},{2,3},{3,2},{4,5},{5,4},{6,7},{7,6},{8,9},{9,8},{10,11... | collective-permute-start | bytes 835592 | tf_op jit(solution)/shard_map/ppermute | solution.py:610
  22.7 1.0 collective-permute-start.5
  23.7 2.8 %shard_map.98 = (f32[4,5,8,896]{3,2,1,0:T(8,128)S(1)}, f32[8,128]{1,0:T(8,128)S(1)}) custom-call(f32[2,8,896]{2,1,0:T(8,128)S(1)} %broadcast_in_dim.24.refs_0_, bf16[2,272,256]{2,1,0:T(8,128)(2,1)S(1)} %shard_map.95.refs_1_.refs_4_.refs_7_, bf16[2,1792,128]{2,1,0:T(8,128)(2,1)S(1)} %copy-done, bf16[2,1792,128]{2,1,0:T(8,128)(2,1)S(1)} %copy-done, ...), custom_call_target="tpu_custom_call" | custom-call | flops 469762048 | bytes 4194304 | tf_op jit(solution)/shard_map/pallas_call | solution.py:555
  26.5 1.0 collective-permute-done.4.refs_0_
  27.6 1.7 %collective-permute-done.5.refs_1_ = bf16[2,272,256]{2,1,0:T(8,128)(2,1)S(1)} collective-permute-done((bf16[2,272,256]{2,1,0:T(8,128)(2,1)S(1)}, bf16[2,272,256]{2,1,0:T(8,128)(2,1)S(1)}, u32[]{:S(2)}, u32[]{:S(2)}) %collective-permute-start.5) | collective-permute-done | bytes 278560 | tf_op jit(solution)/shard_map/ppermute | solution.py:610
  29.3 1.6 %collective-permute-start.6 = (bf16[2,272,256]{2,1,0:T(8,128)(2,1)S(1)}, bf16[2,272,256]{2,1,0:T(8,128)(2,1)S(1)}, u32[]{:S(2)}, u32[]{:S(2)}) collective-permute-start(bf16[2,272,256]{2,1,0:T(8,128)(2,1)S(1)} %get-tuple-element.61.refs_5_.refs_8_.refs_6_), channel_id=1, source_target_pairs={{0,1},{1,0},{2,3},{3,2},{4,5},{5,4},{6,7},{7,6},{8,9},{9,8},{10,11... | collective-permute-start | bytes 835592 | tf_op jit(solution)/shard_map/ppermute | solution.py:610
  30.9 1.0 collective-permute-start.7
  31.9 2.1 %shard_map.100 = (f32[4,5,8,896]{3,2,1,0:T(8,128)S(1)}, f32[8,128]{1,0:T(8,128)S(1)}) custom-call(f32[2,8,896]{2,1,0:T(8,128)S(1)} %broadcast_in_dim.24.refs_0_, bf16[2,272,256]{2,1,0:T(8,128)(2,1)S(1)} %shard_map.95.refs_1_.refs_4_.refs_7_, bf16[2,1792,128]{2,1,0:T(8,128)(2,1)S(1)} %copy-done, bf16[2,1792,128]{2,1,0:T(8,128)(2,1)S(1)} %copy-done, ...), custom_call_target="tpu_custom_call" | custom-call | flops 469762048 | bytes 4194304 | tf_op jit(solution)/shard_map/pallas_call | solution.py:555
  34.0 2.5 %collective-permute-done.6.refs_0_ = bf16[2,272,256]{2,1,0:T(8,128)(2,1)S(1)} collective-permute-done((bf16[2,272,256]{2,1,0:T(8,128)(2,1)S(1)}, bf16[2,272,256]{2,1,0:T(8,128)(2,1)S(1)}, u32[]{:S(2)}, u32[]{:S(2)}) %collective-permute-start.6) | collective-permute-done | bytes 278560 | tf_op jit(solution)/shard_map/ppermute | solution.py:610
  36.5 1.0 collective-permute-done.7.refs_1_
  37.5 1.8 %collective-permute-start.8 = (bf16[2,272,256]{2,1,0:T(8,128)(2,1)S(1)}, bf16[2,272,256]{2,1,0:T(8,128)(2,1)S(1)}, u32[]{:S(2)}, u32[]{:S(2)}) collective-permute-start(bf16[2,272,256]{2,1,0:T(8,128)(2,1)S(1)} %get-tuple-element.65.refs_10_.refs_6_), channel_id=1, source_target_pairs={{0,1},{1,0},{2,3},{3,2},{4,5},{5,4},{6,7},{7,6},{8,9},{9,8},{10,11... | collective-permute-start | bytes 835592 | tf_op jit(solution)/shard_map/ppermute | solution.py:610
  39.3 0.0 collective-permute-done.1.refs_3_
  39.3 4.3 %shard_map.102 = (f32[4,5,8,896]{3,2,1,0:T(8,128)S(1)}, f32[8,128]{1,0:T(8,128)}) custom-call(f32[2,8,896]{2,1,0:T(8,128)S(1)} %broadcast_in_dim.24.refs_0_, bf16[2,272,256]{2,1,0:T(8,128)(2,1)S(1)} %shard_map.95.refs_1_.refs_4_.refs_7_, bf16[2,1792,128]{2,1,0:T(8,128)(2,1)S(1)} %copy-done, bf16[2,1792,128]{2,1,0:T(8,128)(2,1)S(1)} %collective-permute-done.1.refs_3_, ...), custom_call_target="tpu_custom_call" | custom-call | flops 2113929216 | bytes 4194304 | tf_op jit(solution)/shard_map/pallas_call | solution.py:555
  43.6 0.5 collective-permute-done.8.refs_4_
  44.1 2.6 %shard_map.103 = (f32[4,8,896]{2,1,0:T(8,128)S(1)}, f32[8,128]{1,0:T(8,128)S(1)}, f32[2,256,256]{2,1,0:T(8,128)S(1)}, f32[4,128,896]{2,1,0:T(8,128)S(1)}) custom-call(f32[2,8,896]{2,1,0:T(8,128)S(1)} %broadcast_in_dim.24.refs_0_, bf16[2,272,256]{2,1,0:T(8,128)(2,1)S(1)} %shard_map.95.refs_1_.refs_4_.refs_7_, bf16[2,1792,128]{2,1,0:T(8,128)(2,1)S(1)} %copy-done, ...), custom_call_target="tpu_custom_call" | custom-call | flops 469762048 | bytes 4194304 | tf_op jit(solution)/shard_map/pallas_call | solution.py:555
  46.8 2.0 %collective-permute-start.10 = (bf16[2,256,256]{2,1,0:T(8,128)(2,1)S(1)}, bf16[2,256,256]{2,1,0:T(8,128)(2,1)S(1)}, u32[]{:S(2)}, u32[]{:S(2)}) collective-permute-start(bf16[2,256,256]{2,1,0:T(8,128)(2,1)S(1)} %convert_element_type.3), channel_id=1, source_target_pairs={{0,1},{1,0},{2,3},{3,2},{4,5},{5,4},{6,7},{7,6},{8,9},{9,8},{10,11... | collective-permute-start | bytes 786440 | tf_op jit(solution)/shard_map/ppermute | solution.py:610
  48.8 6.6 %collective-permute-start.11 = (f32[8,128]{1,0:T(8,128)S(1)}, f32[8,128]{1,0:T(8,128)S(1)}, u32[]{:S(2)}, u32[]{:S(2)}) collective-permute-start(f32[8,128]{1,0:T(8,128)S(1)} %get-tuple-element.83.refs_3_), channel_id=1, source_target_pairs={{0,4},{1,5},{2,6},{3,7},{4,0},{5,1},{6,2},{7,3},{8,12},{9,13},{10,... | collective-permute-start | bytes 12296 | tf_op jit(solution)/shard_map/ppermute | solution.py:610
  55.4 2.6 %shard_map.104 = (f32[2,256,256]{2,1,0:T(8,128)S(1)}, f32[2,256,256]{2,1,0:T(8,128)S(1)}, f32[4,128,896]{2,1,0:T(8,128)S(1)}) custom-call(f32[2,8,896]{2,1,0:T(8,128)S(1)} %broadcast_in_dim.24.refs_0_, bf16[2,272,256]{2,1,0:T(8,128)(2,1)S(1)} %shard_map.95.refs_1_.refs_4_.refs_7_, ...), custom_call_target="tpu_custom_call", output_to_operand_aliasing={{2}: (7, {})} | custom-call | flops 2348810240 | bytes 6291456 | tf_op jit(solution)/shard_map/pallas_call | solution.py:583
  58.1 3.0 %collective-permute-done.11.refs_4_ = f32[8,128]{1,0:T(8,128)S(1)} collective-permute-done((f32[8,128]{1,0:T(8,128)S(1)}, f32[8,128]{1,0:T(8,128)S(1)}, u32[]{:S(2)}, u32[]{:S(2)}) %collective-permute-start.11) | collective-permute-done | bytes 4128 | tf_op jit(solution)/shard_map/ppermute | solution.py:610
  61.1 0.0 collective-permute-done.10.refs_2_
  61.1 0.1 shard_map.107
  61.2 1.6 %collective-permute-start.12 = (bf16[2,288,256]{2,1,0:T(8,128)(2,1)S(1)}, bf16[2,288,256]{2,1,0:T(8,128)(2,1)S(1)}, u32[]{:S(2)}, u32[]{:S(2)}) collective-permute-start(bf16[2,288,256]{2,1,0:T(8,128)(2,1)S(1)} %get-tuple-element.84), channel_id=1, source_target_pairs={{0,1},{1,0},{2,3},{3,2},{4,5},{5,4},{6,7},{7,6},{8,9},{9,8},{10,11... | collective-permute-start | bytes 884744 | tf_op jit(solution)/shard_map/ppermute | solution.py:610
  62.8 4.4 %shard_map.105 = (f32[2,256,256]{2,1,0:T(8,128)S(1)}, f32[2,256,256]{2,1,0:T(8,128)S(1)}, f32[2,256,256]{2,1,0:T(8,128)S(1)}, f32[4,128,896]{2,1,0:T(8,128)S(1)}) custom-call(f32[2,8,896]{2,1,0:T(8,128)S(1)} %broadcast_in_dim.24.refs_0_, bf16[2,272,256]{2,1,0:T(8,128)(2,1)S(1)} %shard_map.95.refs_1_.refs_4_.refs_7_, ...), custom_call_target="tpu_custom_call", output_to_operand_aliasing={{3}: (8, {})} | custom-call | flops 3523215360 | bytes 6291456 | tf_op jit(solution)/shard_map/pallas_call | solution.py:583
  67.2 3.7 %collective-permute-done.12.refs_2_ = bf16[2,288,256]{2,1,0:T(8,128)(2,1)S(1)} collective-permute-done((bf16[2,288,256]{2,1,0:T(8,128)(2,1)S(1)}, bf16[2,288,256]{2,1,0:T(8,128)(2,1)S(1)}, u32[]{:S(2)}, u32[]{:S(2)}) %collective-permute-start.12) | collective-permute-done | bytes 294944 | tf_op jit(solution)/shard_map/ppermute | solution.py:610
  70.9 1.0 collective-permute-done.13.refs_3_
  72.0 0.1 shard_map.108
  72.1 2.0 %collective-permute-start.14 = (bf16[2,288,256]{2,1,0:T(8,128)(2,1)S(1)}, bf16[2,288,256]{2,1,0:T(8,128)(2,1)S(1)}, u32[]{:S(2)}, u32[]{:S(2)}) collective-permute-start(bf16[2,288,256]{2,1,0:T(8,128)(2,1)S(1)} %get-tuple-element.86), channel_id=1, source_target_pairs={{0,1},{1,0},{2,3},{3,2},{4,5},{5,4},{6,7},{7,6},{8,9},{9,8},{10,11... | collective-permute-start | bytes 884744 | tf_op jit(solution)/shard_map/ppermute | solution.py:610
  74.1 5.1 %shard_map.106 = (f32[2,256,256]{2,1,0:T(8,128)S(1)}, f32[2,256,256]{2,1,0:T(8,128)S(1)}, bf16[1792,128]{1,0:T(8,128)(2,1)S(1)}, bf16[1792,128]{1,0:T(8,128)(2,1)S(1)}) custom-call(f32[2,8,896]{2,1,0:T(8,128)S(1)} %broadcast_in_dim.24.refs_0_, bf16[2,272,256]{2,1,0:T(8,128)(2,1)S(1)} %shard_map.95.refs_1_.refs_4_.refs_7_, bf16[2,1792,128]{2,1,0:T(8,128)(2,1)S(1)} %copy-done, ...), custom_call_target="tpu_custom_call" | custom-call | flops 2348810240 | bytes 6291456 | tf_op jit(solution)/shard_map/pallas_call | solution.py:583
  79.2 4.2 %collective-permute-start.9 = (bf16[1792,128]{1,0:T(8,128)(2,1)S(1)}, bf16[1792,128]{1,0:T(8,128)(2,1)S(1)}, u32[]{:S(2)}, u32[]{:S(2)}) collective-permute-start(bf16[1792,128]{1,0:T(8,128)(2,1)S(1)} %get-tuple-element.74), channel_id=1, source_target_pairs={{0,8},{1,9},{2,10},{3,11},{4,12},{5,13},{6,14},{7,15},{8,0},{9,1},... | collective-permute-start | bytes 1376264 | tf_op jit(solution)/shard_map/ppermute | solution.py:610
  83.4 0.0 collective-permute-done.14.refs_2_
  83.4 0.0 collective-permute-done.15.refs_3_
  83.4 0.1 shard_map.109
  83.5 0.4 collective-permute-start.16
  83.8 1.3 %collective-permute-start.17 = (bf16[2,256,256]{2,1,0:T(8,128)(2,1)S(1)}, bf16[2,256,256]{2,1,0:T(8,128)(2,1)S(1)}, u32[]{:S(2)}, u32[]{:S(2)}) collective-permute-start(bf16[2,256,256]{2,1,0:T(8,128)(2,1)S(1)} %get-tuple-element.91), channel_id=1, source_target_pairs={{0,7},{1,2},{2,1},{3,4},{4,3},{5,6},{6,5},{7,0},{8,15},{9,10},{10,... | collective-permute-start | bytes 786440 | tf_op jit(solution)/shard_map/ppermute | solution.py:610
  85.1 2.3 %collective-permute-start.18 = (f32[8,128]{1,0:T(8,128)S(1)}, f32[8,128]{1,0:T(8,128)S(1)}, u32[]{:S(2)}, u32[]{:S(2)}) collective-permute-start(f32[8,128]{1,0:T(8,128)S(1)} %get-tuple-element.92), channel_id=1, source_target_pairs={{0,8},{1,9},{2,10},{3,11},{4,12},{5,13},{6,14},{7,15},{8,0},{9,1},... | collective-permute-start | bytes 12296 | tf_op jit(solution)/shard_map/ppermute | solution.py:610
  87.5 2.4 %collective-permute-done.18 = f32[8,128]{1,0:T(8,128)S(1)} collective-permute-done((f32[8,128]{1,0:T(8,128)S(1)}, f32[8,128]{1,0:T(8,128)S(1)}, u32[]{:S(2)}, u32[]{:S(2)}) %collective-permute-start.18) | collective-permute-done | bytes 4128 | tf_op jit(solution)/shard_map/ppermute | solution.py:610
  89.9 0.0 collective-permute-start.21
  89.9 0.0 collective-permute-start.20
  89.9 4.5 %collective-permute-done.21.refs_3_ = f32[8,128]{1,0:T(8,128)S(1)} collective-permute-done((f32[8,128]{1,0:T(8,128)S(1)}, f32[8,128]{1,0:T(8,128)S(1)}, u32[]{:S(2)}, u32[]{:S(2)}) %collective-permute-start.21) | collective-permute-done | bytes 4128 | tf_op jit(solution)/shard_map/ppermute | solution.py:610
  94.4 0.6 collective-permute-done.20.refs_2_
  95.0 0.6 collective-permute-done.19.refs_1_
  95.6 0.1 shard_map.110
  95.7 2.1 %collective-permute-start.22 = (bf16[256,256]{1,0:T(8,128)(2,1)S(1)}, bf16[256,256]{1,0:T(8,128)(2,1)S(1)}, u32[]{:S(2)}, u32[]{:S(2)}) collective-permute-start(bf16[256,256]{1,0:T(8,128)(2,1)S(1)} %get-tuple-element.94), channel_id=1, source_target_pairs={{0,8},{1,9},{2,10},{3,11},{4,12},{5,13},{6,14},{7,15},{8,0},{9,1},... | collective-permute-start | bytes 393224 | tf_op jit(solution)/shard_map/ppermute | solution.py:610
  97.8 3.4 %collective-permute-start.25 = (f32[8,128]{1,0:T(8,128)S(1)}, f32[8,128]{1,0:T(8,128)S(1)}, u32[]{:S(2)}, u32[]{:S(2)}) collective-permute-start(f32[8,128]{1,0:T(8,128)S(1)} %get-tuple-element.95.refs_0_), channel_id=1, source_target_pairs={{0,192},{1,193},{2,194},{3,195},{4,196},{5,197},{6,198},{7,199},{8... | collective-permute-start | bytes 12296 | tf_op jit(solution)/shard_map/ppermute | solution.py:610
  101.2 2.8 %collective-permute-start.24 = (f32[8,128]{1,0:T(8,128)S(1)}, f32[8,128]{1,0:T(8,128)S(1)}, u32[]{:S(2)}, u32[]{:S(2)}) collective-permute-start(f32[8,128]{1,0:T(8,128)S(1)} %get-tuple-element.95.refs_0_), channel_id=1, source_target_pairs={{0,128},{1,129},{2,130},{3,131},{4,132},{5,133},{6,134},{7,135},{8... | collective-permute-start | bytes 12296 | tf_op jit(solution)/shard_map/ppermute | solution.py:610
  103.9 0.0 collective-permute-start.23
  103.9 0.0 collective-permute-done.9.got_ref
  104.0 2.3 %collective-permute-done.24.refs_2_ = f32[8,128]{1,0:T(8,128)S(1)} collective-permute-done((f32[8,128]{1,0:T(8,128)S(1)}, f32[8,128]{1,0:T(8,128)S(1)}, u32[]{:S(2)}, u32[]{:S(2)}) %collective-permute-start.24) | collective-permute-done | bytes 4128 | tf_op jit(solution)/shard_map/ppermute | solution.py:610
  106.3 1.3 %collective-permute-done.23.refs_1_ = f32[8,128]{1,0:T(8,128)S(1)} collective-permute-done((f32[8,128]{1,0:T(8,128)S(1)}, f32[8,128]{1,0:T(8,128)S(1)}, u32[]{:S(2)}, u32[]{:S(2)}) %collective-permute-start.23) | collective-permute-done | bytes 4128 | tf_op jit(solution)/shard_map/ppermute | solution.py:610
  107.6 1.2 %shard_map.111 = (bf16[128,3584]{1,0:T(8,128)(2,1)}, bf16[128,512]{1,0:T(8,128)(2,1)}, bf16[128,512]{1,0:T(8,128)(2,1)}, f32[1,28]{1,0:T(1,128)}) custom-call(s32[1]{0:T(128)} %bitcast.x_ref, bf16[1792,128]{1,0:T(8,128)(2,1)S(1)} %get-tuple-element.73.keep_ref, bf16[1792,128]{1,0:T(8,128)(2,1)S(1)} %collective-permute-done.9.got_ref, ...), custom_call_target="tpu_custom_call" | custom-call | flops 1024 | bytes 2097152 | tf_op jit(solution)/shard_map/pallas_call | solution.py:736
  (22 shorter events, 0.2 us)
Async XLA Ops:
  0.6 14.7 %copy-start.3 = (f32[28]{0:T(128)S(1)}, f32[28]{0:T(128)}, u32[]{:S(2)}) copy-start(f32[28]{0:T(128)} %param.11) | copy-start | bytes 340
  2.4 5.7 %copy-start.2 = (bf16[272,256]{1,0:T(8,128)(2,1)S(1)}, bf16[272,256]{1,0:T(8,128)(2,1)}, u32[]{:S(2)}) copy-start(bf16[272,256]{1,0:T(8,128)(2,1)} %get-tuple-element.54.keep_ref) | copy-start | bytes 417796
  2.4 5.7 %collective-permute-start = (bf16[272,256]{1,0:T(8,128)(2,1)}, bf16[272,256]{1,0:T(8,128)(2,1)S(1)}, u32[]{:S(2)}, u32[]{:S(2)}) collective-permute-start(bf16[272,256]{1,0:T(8,128)(2,1)} %get-tuple-element.52.after_ref), channel_id=1, source_target_pairs={{0,8},{1,9},{2,10},{3,11},{4,12},{5,13},{6,14},{7,15},{8,0},{9,1},... | collective-permute-start | bytes 417800 | tf_op jit(solution)/shard_map/ppermute | solution.py:610
  6.4 9.3 %copy-start = (bf16[2,1792,128]{2,1,0:T(8,128)(2,1)S(1)}, bf16[2,1792,128]{2,1,0:T(8,128)(2,1)}, u32[]{:S(2)}) copy-start(bf16[2,1792,128]{2,1,0:T(8,128)(2,1)} %get-tuple-element.55.refs_2_.refs_3_) | copy-start | bytes 2752516
  6.4 33.0 %collective-permute-start.1 = (bf16[2,1792,128]{2,1,0:T(8,128)(2,1)}, bf16[2,1792,128]{2,1,0:T(8,128)(2,1)S(1)}, u32[]{:S(2)}, u32[]{:S(2)}) collective-permute-start(bf16[2,1792,128]{2,1,0:T(8,128)(2,1)} %get-tuple-element.53.after_ref), channel_id=1, source_target_pairs={{0,8},{1,9},{2,10},{3,11},{4,12},{5,13},{6,14},{7,15},{8,0},{9,1},... | collective-permute-start | bytes 2752520 | tf_op jit(solution)/shard_map/ppermute | solution.py:610
  8.1 1.2 %copy-start.1 = (bf16[2,1792,128]{2,1,0:T(8,128)(2,1)S(1)}, bf16[2,1792,128]{2,1,0:T(8,128)(2,1)}, u32[]{:S(2)}) copy-start(bf16[2,1792,128]{2,1,0:T(8,128)(2,1)} %get-tuple-element.53.after_ref) | copy-start | bytes 2752516
  9.3 8.1 %collective-permute-start.3 = (bf16[2,272,256]{2,1,0:T(8,128)(2,1)S(1)}, bf16[2,272,256]{2,1,0:T(8,128)(2,1)S(1)}, u32[]{:S(2)}, u32[]{:S(2)}) collective-permute-start(bf16[2,272,256]{2,1,0:T(8,128)(2,1)S(1)} %shard_map.95.refs_1_.refs_4_.refs_7_), channel_id=1, source_target_pairs={{0,7},{1,2},{2,1},{3,4},{4,3},{5,6},{6,5},{7,0},{8,15},{9,10},{10,... | collective-permute-start | bytes 835592 | tf_op jit(solution)/shard_map/ppermute | solution.py:610
  11.3 9.5 %collective-permute-start.2 = (bf16[2,272,256]{2,1,0:T(8,128)(2,1)S(1)}, bf16[2,272,256]{2,1,0:T(8,128)(2,1)S(1)}, u32[]{:S(2)}, u32[]{:S(2)}) collective-permute-start(bf16[2,272,256]{2,1,0:T(8,128)(2,1)S(1)} %shard_map.95.refs_1_.refs_4_.refs_7_), channel_id=1, source_target_pairs={{0,1},{1,0},{2,3},{3,2},{4,5},{5,4},{6,7},{7,6},{8,9},{9,8},{10,11... | collective-permute-start | bytes 835592 | tf_op jit(solution)/shard_map/ppermute | solution.py:610
  20.9 6.7 %collective-permute-start.4 = (bf16[2,272,256]{2,1,0:T(8,128)(2,1)S(1)}, bf16[2,272,256]{2,1,0:T(8,128)(2,1)S(1)}, u32[]{:S(2)}, u32[]{:S(2)}) collective-permute-start(bf16[2,272,256]{2,1,0:T(8,128)(2,1)S(1)} %get-tuple-element.57.refs_5_.refs_6_), channel_id=1, source_target_pairs={{0,1},{1,0},{2,3},{3,2},{4,5},{5,4},{6,7},{7,6},{8,9},{9,8},{10,11... | collective-permute-start | bytes 835592 | tf_op jit(solution)/shard_map/ppermute | solution.py:610
  22.7 6.5 %collective-permute-start.5 = (bf16[2,272,256]{2,1,0:T(8,128)(2,1)S(1)}, bf16[2,272,256]{2,1,0:T(8,128)(2,1)S(1)}, u32[]{:S(2)}, u32[]{:S(2)}) collective-permute-start(bf16[2,272,256]{2,1,0:T(8,128)(2,1)S(1)} %get-tuple-element.58.refs_4_.refs_5_), channel_id=1, source_target_pairs={{0,7},{1,2},{2,1},{3,4},{4,3},{5,6},{6,5},{7,0},{8,15},{9,10},{10,... | collective-permute-start | bytes 835592 | tf_op jit(solution)/shard_map/ppermute | solution.py:610
  29.3 7.2 %collective-permute-start.6 = (bf16[2,272,256]{2,1,0:T(8,128)(2,1)S(1)}, bf16[2,272,256]{2,1,0:T(8,128)(2,1)S(1)}, u32[]{:S(2)}, u32[]{:S(2)}) collective-permute-start(bf16[2,272,256]{2,1,0:T(8,128)(2,1)S(1)} %get-tuple-element.61.refs_5_.refs_8_.refs_6_), channel_id=1, source_target_pairs={{0,1},{1,0},{2,3},{3,2},{4,5},{5,4},{6,7},{7,6},{8,9},{9,8},{10,11... | collective-permute-start | bytes 835592 | tf_op jit(solution)/shard_map/ppermute | solution.py:610
  30.9 6.5 %collective-permute-start.7 = (bf16[2,272,256]{2,1,0:T(8,128)(2,1)S(1)}, bf16[2,272,256]{2,1,0:T(8,128)(2,1)S(1)}, u32[]{:S(2)}, u32[]{:S(2)}) collective-permute-start(bf16[2,272,256]{2,1,0:T(8,128)(2,1)S(1)} %get-tuple-element.62.refs_4_.refs_7_.refs_5_), channel_id=1, source_target_pairs={{0,7},{1,2},{2,1},{3,4},{4,3},{5,6},{6,5},{7,0},{8,15},{9,10},{10,... | collective-permute-start | bytes 835592 | tf_op jit(solution)/shard_map/ppermute | solution.py:610
  37.5 6.6 %collective-permute-start.8 = (bf16[2,272,256]{2,1,0:T(8,128)(2,1)S(1)}, bf16[2,272,256]{2,1,0:T(8,128)(2,1)S(1)}, u32[]{:S(2)}, u32[]{:S(2)}) collective-permute-start(bf16[2,272,256]{2,1,0:T(8,128)(2,1)S(1)} %get-tuple-element.65.refs_10_.refs_6_), channel_id=1, source_target_pairs={{0,1},{1,0},{2,3},{3,2},{4,5},{5,4},{6,7},{7,6},{8,9},{9,8},{10,11... | collective-permute-start | bytes 835592 | tf_op jit(solution)/shard_map/ppermute | solution.py:610
  46.8 14.3 %collective-permute-start.10 = (bf16[2,256,256]{2,1,0:T(8,128)(2,1)S(1)}, bf16[2,256,256]{2,1,0:T(8,128)(2,1)S(1)}, u32[]{:S(2)}, u32[]{:S(2)}) collective-permute-start(bf16[2,256,256]{2,1,0:T(8,128)(2,1)S(1)} %convert_element_type.3), channel_id=1, source_target_pairs={{0,1},{1,0},{2,3},{3,2},{4,5},{5,4},{6,7},{7,6},{8,9},{9,8},{10,11... | collective-permute-start | bytes 786440 | tf_op jit(solution)/shard_map/ppermute | solution.py:610
  48.8 12.3 %collective-permute-start.11 = (f32[8,128]{1,0:T(8,128)S(1)}, f32[8,128]{1,0:T(8,128)S(1)}, u32[]{:S(2)}, u32[]{:S(2)}) collective-permute-start(f32[8,128]{1,0:T(8,128)S(1)} %get-tuple-element.83.refs_3_), channel_id=1, source_target_pairs={{0,4},{1,5},{2,6},{3,7},{4,0},{5,1},{6,2},{7,3},{8,12},{9,13},{10,... | collective-permute-start | bytes 12296 | tf_op jit(solution)/shard_map/ppermute | solution.py:610
  61.2 9.7 %collective-permute-start.12 = (bf16[2,288,256]{2,1,0:T(8,128)(2,1)S(1)}, bf16[2,288,256]{2,1,0:T(8,128)(2,1)S(1)}, u32[]{:S(2)}, u32[]{:S(2)}) collective-permute-start(bf16[2,288,256]{2,1,0:T(8,128)(2,1)S(1)} %get-tuple-element.84), channel_id=1, source_target_pairs={{0,1},{1,0},{2,3},{3,2},{4,5},{5,4},{6,7},{7,6},{8,9},{9,8},{10,11... | collective-permute-start | bytes 884744 | tf_op jit(solution)/shard_map/ppermute | solution.py:610
  62.8 9.2 %collective-permute-start.13 = (bf16[2,288,256]{2,1,0:T(8,128)(2,1)S(1)}, bf16[2,288,256]{2,1,0:T(8,128)(2,1)S(1)}, u32[]{:S(2)}, u32[]{:S(2)}) collective-permute-start(bf16[2,288,256]{2,1,0:T(8,128)(2,1)S(1)} %get-tuple-element.85), channel_id=1, source_target_pairs={{0,7},{1,2},{2,1},{3,4},{4,3},{5,6},{6,5},{7,0},{8,15},{9,10},{10,... | collective-permute-start | bytes 884744 | tf_op jit(solution)/shard_map/ppermute | solution.py:610
  72.1 11.2 %collective-permute-start.14 = (bf16[2,288,256]{2,1,0:T(8,128)(2,1)S(1)}, bf16[2,288,256]{2,1,0:T(8,128)(2,1)S(1)}, u32[]{:S(2)}, u32[]{:S(2)}) collective-permute-start(bf16[2,288,256]{2,1,0:T(8,128)(2,1)S(1)} %get-tuple-element.86), channel_id=1, source_target_pairs={{0,1},{1,0},{2,3},{3,2},{4,5},{5,4},{6,7},{7,6},{8,9},{9,8},{10,11... | collective-permute-start | bytes 884744 | tf_op jit(solution)/shard_map/ppermute | solution.py:610
  74.1 9.2 %collective-permute-start.15 = (bf16[2,288,256]{2,1,0:T(8,128)(2,1)S(1)}, bf16[2,288,256]{2,1,0:T(8,128)(2,1)S(1)}, u32[]{:S(2)}, u32[]{:S(2)}) collective-permute-start(bf16[2,288,256]{2,1,0:T(8,128)(2,1)S(1)} %get-tuple-element.87), channel_id=1, source_target_pairs={{0,7},{1,2},{2,1},{3,4},{4,3},{5,6},{6,5},{7,0},{8,15},{9,10},{10,... | collective-permute-start | bytes 884744 | tf_op jit(solution)/shard_map/ppermute | solution.py:610
  79.2 24.8 %collective-permute-start.9 = (bf16[1792,128]{1,0:T(8,128)(2,1)S(1)}, bf16[1792,128]{1,0:T(8,128)(2,1)S(1)}, u32[]{:S(2)}, u32[]{:S(2)}) collective-permute-start(bf16[1792,128]{1,0:T(8,128)(2,1)S(1)} %get-tuple-element.74), channel_id=1, source_target_pairs={{0,8},{1,9},{2,10},{3,11},{4,12},{5,13},{6,14},{7,15},{8,0},{9,1},... | collective-permute-start | bytes 1376264 | tf_op jit(solution)/shard_map/ppermute | solution.py:610
  83.5 12.1 %collective-permute-start.16 = (bf16[2,256,256]{2,1,0:T(8,128)(2,1)S(1)}, bf16[2,256,256]{2,1,0:T(8,128)(2,1)S(1)}, u32[]{:S(2)}, u32[]{:S(2)}) collective-permute-start(bf16[2,256,256]{2,1,0:T(8,128)(2,1)S(1)} %get-tuple-element.90), channel_id=1, source_target_pairs={{0,1},{1,0},{2,3},{3,2},{4,5},{5,4},{6,7},{7,6},{8,9},{9,8},{10,11... | collective-permute-start | bytes 786440 | tf_op jit(solution)/shard_map/ppermute | solution.py:610
  83.8 11.7 %collective-permute-start.17 = (bf16[2,256,256]{2,1,0:T(8,128)(2,1)S(1)}, bf16[2,256,256]{2,1,0:T(8,128)(2,1)S(1)}, u32[]{:S(2)}, u32[]{:S(2)}) collective-permute-start(bf16[2,256,256]{2,1,0:T(8,128)(2,1)S(1)} %get-tuple-element.91), channel_id=1, source_target_pairs={{0,7},{1,2},{2,1},{3,4},{4,3},{5,6},{6,5},{7,0},{8,15},{9,10},{10,... | collective-permute-start | bytes 786440 | tf_op jit(solution)/shard_map/ppermute | solution.py:610
  85.1 4.7 %collective-permute-start.18 = (f32[8,128]{1,0:T(8,128)S(1)}, f32[8,128]{1,0:T(8,128)S(1)}, u32[]{:S(2)}, u32[]{:S(2)}) collective-permute-start(f32[8,128]{1,0:T(8,128)S(1)} %get-tuple-element.92), channel_id=1, source_target_pairs={{0,8},{1,9},{2,10},{3,11},{4,12},{5,13},{6,14},{7,15},{8,0},{9,1},... | collective-permute-start | bytes 12296 | tf_op jit(solution)/shard_map/ppermute | solution.py:610
  89.9 4.5 %collective-permute-start.21 = (f32[8,128]{1,0:T(8,128)S(1)}, f32[8,128]{1,0:T(8,128)S(1)}, u32[]{:S(2)}, u32[]{:S(2)}) collective-permute-start(f32[8,128]{1,0:T(8,128)S(1)} %add.8.refs_0_), channel_id=1, source_target_pairs={{0,48},{1,49},{2,50},{3,51},{4,52},{5,53},{6,54},{7,55},{8,56},{9,... | collective-permute-start | bytes 12296 | tf_op jit(solution)/shard_map/ppermute | solution.py:610
  89.9 5.1 %collective-permute-start.20 = (f32[8,128]{1,0:T(8,128)S(1)}, f32[8,128]{1,0:T(8,128)S(1)}, u32[]{:S(2)}, u32[]{:S(2)}) collective-permute-start(f32[8,128]{1,0:T(8,128)S(1)} %add.8.refs_0_), channel_id=1, source_target_pairs={{0,32},{1,33},{2,34},{3,35},{4,36},{5,37},{6,38},{7,39},{8,40},{9,... | collective-permute-start | bytes 12296 | tf_op jit(solution)/shard_map/ppermute | solution.py:610
  94.4 1.2 %collective-permute-start.19 = (f32[8,128]{1,0:T(8,128)S(1)}, f32[8,128]{1,0:T(8,128)S(1)}, u32[]{:S(2)}, u32[]{:S(2)}) collective-permute-start(f32[8,128]{1,0:T(8,128)S(1)} %add.8.refs_0_), channel_id=1, source_target_pairs={{0,16},{1,17},{2,18},{3,19},{4,20},{5,21},{6,22},{7,23},{8,24},{9,... | collective-permute-start | bytes 12296 | tf_op jit(solution)/shard_map/ppermute | solution.py:610
  95.7 11.9 %collective-permute-start.22 = (bf16[256,256]{1,0:T(8,128)(2,1)S(1)}, bf16[256,256]{1,0:T(8,128)(2,1)S(1)}, u32[]{:S(2)}, u32[]{:S(2)}) collective-permute-start(bf16[256,256]{1,0:T(8,128)(2,1)S(1)} %get-tuple-element.94), channel_id=1, source_target_pairs={{0,8},{1,9},{2,10},{3,11},{4,12},{5,13},{6,14},{7,15},{8,0},{9,1},... | collective-permute-start | bytes 393224 | tf_op jit(solution)/shard_map/ppermute | solution.py:610
  97.8 6.2 %collective-permute-start.25 = (f32[8,128]{1,0:T(8,128)S(1)}, f32[8,128]{1,0:T(8,128)S(1)}, u32[]{:S(2)}, u32[]{:S(2)}) collective-permute-start(f32[8,128]{1,0:T(8,128)S(1)} %get-tuple-element.95.refs_0_), channel_id=1, source_target_pairs={{0,192},{1,193},{2,194},{3,195},{4,196},{5,197},{6,198},{7,199},{8... | collective-permute-start | bytes 12296 | tf_op jit(solution)/shard_map/ppermute | solution.py:610
  101.2 5.1 %collective-permute-start.24 = (f32[8,128]{1,0:T(8,128)S(1)}, f32[8,128]{1,0:T(8,128)S(1)}, u32[]{:S(2)}, u32[]{:S(2)}) collective-permute-start(f32[8,128]{1,0:T(8,128)S(1)} %get-tuple-element.95.refs_0_), channel_id=1, source_target_pairs={{0,128},{1,129},{2,130},{3,131},{4,132},{5,133},{6,134},{7,135},{8... | collective-permute-start | bytes 12296 | tf_op jit(solution)/shard_map/ppermute | solution.py:610
  103.9 3.6 %collective-permute-start.23 = (f32[8,128]{1,0:T(8,128)S(1)}, f32[8,128]{1,0:T(8,128)S(1)}, u32[]{:S(2)}, u32[]{:S(2)}) collective-permute-start(f32[8,128]{1,0:T(8,128)S(1)} %get-tuple-element.95.refs_0_), channel_id=1, source_target_pairs={{0,64},{1,65},{2,66},{3,67},{4,68},{5,69},{6,70},{7,71},{8,72},{9,... | collective-permute-start | bytes 12296 | tf_op jit(solution)/shard_map/ppermute | solution.py:610
